TPU v7x, 32 devices: a whole 2x2x4 slice. The times are simulated.
32 devices in a mesh: dp: 8 (over y, x, core), mp: 4 (over z).
Axes of the slice: x: 2, y: 2, z: 4, core: 2. Of those that a mesh axis runs over, the one named last changes fastest.
Arguments:
- stream_in: float32 [16384, 512], P(('dp', 'mp')), may hold values from -6 to 6
- segments: int32 [8, 2048], P('dp'), may hold values from 0 to 3, as said below
- norm_gain: float32 [2, 2, 512], replicated, may hold values from 0.1 to 1.9
- norm_bias: float32 [2, 2, 512], replicated, may hold values from -1.8 to 1.8
- w_in: bfloat16 [2, 512, 2, 512], P(None, None, None, 'mp'), may hold values from -0.25 to 0.25
- w_out: bfloat16 [2, 512, 512], P(None, 'mp'), may hold values from -0.5 to 0.5
- sub_kernels: float32 [2, 6, 32, 512], P(None, None, None, 'mp'), may hold values from -6 to 6
- w_up: bfloat16 [2, 512, 2048], P(None, None, 'mp'), may hold values from -0.25 to 0.25
- w_down: bfloat16 [2, 2048, 512], P(None, 'mp'), may hold values from -0.1875 to 0.1875
- cotangent: float32 [16384, 512], P(('dp', 'mp')), may hold values from -6 to 6
Outputs:
- out_stream: float32 [16384, 512], P(('dp', 'mp'))
- grad_stream: float32 [16384, 512], P(('dp', 'mp'))
- grad_norm_gain: float32 [2, 2, 512], replicated
- grad_norm_bias: float32 [2, 2, 512], replicated
- grad_w_in: float32 [2, 512, 2, 512], P(None, None, None, 'mp')
- grad_w_out: float32 [2, 512, 512], P(None, 'mp')
- grad_sub_kernels: float32 [2, 6, 32, 512], P(None, None, None, 'mp')
- grad_w_up: float32 [2, 512, 2048], P(None, None, 'mp')
- grad_w_down: float32 [2, 2048, 512], P(None, 'mp')
Inputs may be any that keep to these rules, and one draw needn't show every extreme that they name: `segments`: in each row the document numbers never fall and every number from 0 to 3 occurs, so each row holds 4 whole documents; one of them starts in the row's first quarter and ends in its last quarter.
All inputs are finite; a program needn't handle non-finite values.
Results may differ from a plain program's by a relative error of at most 0.025.
Values may be sent and summed in bfloat16 or wider, within the bound.
A program may use at most 448 MiB of HBM per device.

v0:
```python
import jax
import jax.numpy as jnp
from jax import lax
from jax.sharding import PartitionSpec as P

DOCS = 4
LAYERS = 2


DECAY_RATE = 0.5
EPSILON = 1e-05


def norm_rows(values, gain_row, bias_row):
    centred = values - jnp.mean(values, axis=-1, keepdims=True)
    variance = jnp.mean(centred * centred, axis=-1, keepdims=True)
    return centred * lax.rsqrt(variance + EPSILON) * gain_row + bias_row


def build_kernel(sub_taps):
    pieces = []
    for level_index in range(sub_taps.shape[0]):
        repeats = 2 ** max(level_index, 1)
        pieces.append(jnp.repeat(sub_taps[level_index], repeats, axis=0) * DECAY_RATE**level_index)
    raw_taps = jnp.concatenate(pieces, axis=0)
    return raw_taps * lax.rsqrt(jnp.sum(raw_taps * raw_taps, axis=0, keepdims=True) + EPSILON)


def toeplitz_table(sub_taps):
    kernel = build_kernel(sub_taps).astype(jnp.bfloat16)
    length, channels = kernel.shape
    block_rows = min(64, length // 2)
    padded = jnp.concatenate([jnp.zeros((block_rows, channels), jnp.bfloat16), kernel], axis=0)
    columns = [
        padded[block_rows - column : block_rows - column + length] for column in range(block_rows)
    ]
    table = jnp.stack(columns, axis=1)
    return table.reshape(length // block_rows, block_rows, block_rows, channels)


def doc_onehot(seg_blocks, float_type):
    return (seg_blocks[..., None] == jnp.arange(DOCS, dtype=jnp.int32)).astype(float_type)


def spread_docs(value_blocks, onehot):
    return jnp.moveaxis(onehot, 3, 2)[..., None] * value_blocks[:, :, None]


def conv_blocks(values, toeplitz, segments):
    rows_dev, length, channels = values.shape
    blocks, block_rows = (toeplitz.shape[0], toeplitz.shape[1])
    value_blocks = values.reshape(rows_dev, blocks, block_rows, channels)
    seg_blocks = segments.reshape(rows_dev, blocks, block_rows)
    onehot = doc_onehot(seg_blocks, jnp.bfloat16)
    inner = jnp.einsum(
        "abc,rndbc->rndac",
        toeplitz[0],
        spread_docs(value_blocks, onehot),
        preferred_element_type=jnp.float32,
    )
    total = jnp.einsum("rndac,rnad->rnac", inner, onehot.astype(jnp.float32))
    tail_doc = seg_blocks[:, :, -1:]
    source = (seg_blocks == tail_doc).astype(jnp.bfloat16)[..., None] * value_blocks
    padded_source = jnp.concatenate([jnp.zeros_like(source), source], axis=1)
    padded_tail = jnp.concatenate([jnp.full(tail_doc.shape, -1, jnp.int32), tail_doc], axis=1)

    def lag_step(carry, lag_block):
        shifted = lax.dynamic_slice_in_dim(padded_source, blocks - lag_block, blocks, 1)
        shifted_tail = lax.dynamic_slice_in_dim(padded_tail, blocks - lag_block, blocks, 1)
        tile = lax.dynamic_index_in_dim(toeplitz, lag_block, 0, keepdims=False)
        term = jnp.einsum("abc,rnbc->rnac", tile, shifted, preferred_element_type=jnp.float32)
        return (carry + term * (seg_blocks == shifted_tail).astype(jnp.float32)[..., None], None)

    total, _ = lax.scan(lag_step, total, jnp.arange(1, blocks, dtype=jnp.int32))
    return total.reshape(rows_dev, length, channels)


def conv_rows(values, toeplitz, segments):
    rows_dev, length = segments.shape
    shaped = values.reshape(rows_dev, length, values.shape[1])
    return conv_blocks(shaped, toeplitz, segments).reshape(values.shape)


def conv_back_rows(upstream, toeplitz, segments):
    rows_dev, length = segments.shape
    channels = upstream.shape[1]
    blocks, block_rows = (toeplitz.shape[0], toeplitz.shape[1])
    up_blocks = upstream.reshape(rows_dev, blocks, block_rows, channels)
    seg_blocks = segments.reshape(rows_dev, blocks, block_rows)
    onehot = doc_onehot(seg_blocks, jnp.bfloat16)
    inner = jnp.einsum(
        "abc,rndac->rndbc",
        toeplitz[0],
        spread_docs(up_blocks, onehot),
        preferred_element_type=jnp.float32,
    )
    diagonal = jnp.einsum("rndbc,rnbd->rnbc", inner, onehot.astype(jnp.float32))
    tail_doc = seg_blocks[:, :, -1:]
    padded_up = jnp.concatenate([up_blocks, jnp.zeros_like(up_blocks)], axis=1)
    padded_seg = jnp.concatenate([seg_blocks, jnp.full(seg_blocks.shape, -1, jnp.int32)], axis=1)

    def lag_step(carry, lag_block):
        shifted = lax.dynamic_slice_in_dim(padded_up, lag_block, blocks, 1)
        shifted_seg = lax.dynamic_slice_in_dim(padded_seg, lag_block, blocks, 1)
        masked = shifted * (shifted_seg == tail_doc).astype(jnp.bfloat16)[..., None]
        tile = lax.dynamic_index_in_dim(toeplitz, lag_block, 0, keepdims=False)
        return (
            carry + jnp.einsum("abc,rnac->rnbc", tile, masked, preferred_element_type=jnp.float32),
            None,
        )

    crossing, _ = lax.scan(
        lag_step, jnp.zeros(up_blocks.shape, jnp.float32), jnp.arange(1, blocks, dtype=jnp.int32)
    )
    total = diagonal + crossing * (seg_blocks == tail_doc).astype(jnp.float32)[..., None]
    return total.reshape(upstream.shape)


def diagonal_sums(tile):
    block_rows, channels = (tile.shape[0], tile.shape[2])
    flipped = tile[:, ::-1]
    padded = jnp.concatenate(
        [flipped, jnp.zeros((block_rows, block_rows, channels), jnp.float32)], axis=1
    )
    flat = padded.reshape(block_rows * 2 * block_rows, channels)[
        : block_rows * (2 * block_rows - 1)
    ]
    return jnp.sum(flat.reshape(block_rows, 2 * block_rows - 1, channels), axis=0)


def kernel_grads(upstream, conv_input, segments, block_rows):
    rows_dev, length = segments.shape
    channels = upstream.shape[1]
    blocks = length // block_rows
    up_blocks = upstream.reshape(rows_dev, blocks, block_rows, channels)
    in_blocks = conv_input.reshape(rows_dev, blocks, block_rows, channels)
    seg_blocks = segments.reshape(rows_dev, blocks, block_rows)
    onehot = doc_onehot(seg_blocks, jnp.bfloat16)
    first_tile = jnp.einsum(
        "rndac,rndbc->abc",
        spread_docs(up_blocks, onehot),
        spread_docs(in_blocks, onehot),
        preferred_element_type=jnp.float32,
    )
    tail_doc = seg_blocks[:, :, -1:]
    source = (seg_blocks == tail_doc).astype(jnp.bfloat16)[..., None] * in_blocks
    padded_up = jnp.concatenate([up_blocks, jnp.zeros_like(up_blocks)], axis=1)
    padded_seg = jnp.concatenate([seg_blocks, jnp.full(seg_blocks.shape, -1, jnp.int32)], axis=1)

    def lag_step(carry, lag_block):
        shifted = lax.dynamic_slice_in_dim(padded_up, lag_block, blocks, 1)
        shifted_seg = lax.dynamic_slice_in_dim(padded_seg, lag_block, blocks, 1)
        masked = shifted * (shifted_seg == tail_doc).astype(jnp.bfloat16)[..., None]
        tile = jnp.einsum("rnac,rnbc->abc", masked, source, preferred_element_type=jnp.float32)
        return (carry, diagonal_sums(tile))

    _, later_sums = lax.scan(
        lag_step, jnp.zeros((), jnp.float32), jnp.arange(1, blocks, dtype=jnp.int32)
    )
    all_sums = jnp.concatenate([diagonal_sums(first_tile)[None], later_sums], axis=0)
    upper = all_sums[:, block_rows - 1 :].reshape(length, channels)
    lower = jnp.concatenate(
        [jnp.zeros((blocks - 1, 1, channels), jnp.float32), all_sums[1:, : block_rows - 1]], axis=1
    )
    lower = jnp.concatenate([lower, jnp.zeros((1, block_rows, channels), jnp.float32)], axis=0)
    return upper + lower.reshape(length, channels)


def gather_rows(local_rows):
    return lax.all_gather(local_rows, "mp", axis=0, tiled=True)


def gather_grads(local_rows):
    return lax.all_gather(local_rows, "mp", axis=0, tiled=True)


def reduce_rows(gathered, weight):

    def row_term(first_row, count_rows):
        return jnp.dot(gathered, weight, preferred_element_type=jnp.float32)

    return lax.psum_scatter(
        row_term(
            jnp.int32(0), lax.axis_size("mp") * (gathered.shape[0] // lax.axis_size("mp"))
        ).astype(jnp.bfloat16),
        "mp",
        scatter_dimension=0,
        tiled=True,
    ).astype(jnp.float32)


def reduce_back(gathered, weight):

    def row_term(first_row, count_rows):
        return lax.dot_general(
            gathered, weight, (((1,), (1,)), ((), ())), preferred_element_type=jnp.float32
        )

    return lax.psum_scatter(
        row_term(
            jnp.int32(0), lax.axis_size("mp") * (gathered.shape[0] // lax.axis_size("mp"))
        ).astype(jnp.bfloat16),
        "mp",
        scatter_dimension=0,
        tiled=True,
    ).astype(jnp.float32)


def mixer_forward(stream, segments, gain_row, bias_row, w_in_layer, w_out_layer, sub_layer):
    hidden = norm_rows(stream, gain_row, bias_row).astype(jnp.bfloat16)
    toeplitz = toeplitz_table(sub_layer)
    hidden_full = gather_rows(hidden)
    channels = w_in_layer.shape[2]
    joined = jnp.dot(
        hidden_full,
        w_in_layer.reshape(w_in_layer.shape[0], 2 * channels),
        preferred_element_type=jnp.float32,
    )
    conv_input = joined[:, :channels].astype(jnp.bfloat16)
    gate_pre = joined[:, channels:]
    convolved = conv_rows(conv_input, toeplitz, segments)
    gated_out = (jax.nn.gelu(gate_pre) * convolved).astype(jnp.bfloat16)
    middle = stream + reduce_rows(gated_out, w_out_layer)
    return (
        middle,
        (
            hidden_full,
            conv_input,
            gate_pre,
            convolved,
            gated_out,
            w_in_layer,
            w_out_layer,
            toeplitz,
        ),
    )


def mixer_backward(middle_grad, stream, segments, gain_row, bias_row, sub_layer, stored):
    hidden_rows, conv_input, gate_pre, convolved, gated_rows, in_weight, out_weight, toeplitz = (
        stored
    )
    out_grad = middle_grad.astype(jnp.bfloat16)
    out_grad = gather_grads(out_grad)
    grad_out_w = lax.dot_general(
        gated_rows, out_grad, (((0,), (0,)), ((), ())), preferred_element_type=jnp.float32
    )
    gated_grad = lax.dot_general(
        out_grad, out_weight, (((1,), (1,)), ((), ())), preferred_element_type=jnp.float32
    )
    gate_act, gate_pull = jax.vjp(jax.nn.gelu, gate_pre)
    conv_grad = (gated_grad * gate_act).astype(jnp.bfloat16)
    gate_grad = gate_pull(gated_grad * convolved)[0].astype(jnp.bfloat16)
    input_grad = conv_back_rows(conv_grad, toeplitz, segments).astype(jnp.bfloat16)
    taps_grad = kernel_grads(conv_grad, conv_input, segments, toeplitz.shape[1])
    kernel_pull = jax.vjp(build_kernel, sub_layer)[1]
    grad_sub = kernel_pull(taps_grad)[0]
    joined_grad = jnp.concatenate([input_grad, gate_grad], axis=1)
    grad_in_w = lax.dot_general(
        hidden_rows, joined_grad, (((0,), (0,)), ((), ())), preferred_element_type=jnp.float32
    ).reshape(in_weight.shape)
    hidden_grad = reduce_back(joined_grad, in_weight.reshape(in_weight.shape[0], -1))
    norm_pull = jax.vjp(norm_rows, stream, gain_row, bias_row)[1]
    norm_grad, gain_grad, bias_grad = norm_pull(hidden_grad)
    return (middle_grad + norm_grad, (grad_in_w, grad_out_w, grad_sub), (gain_grad, bias_grad))


def mlp_forward(middle, gain_row, bias_row, w_up_layer, w_down_layer):
    hidden_mid = norm_rows(middle, gain_row, bias_row).astype(jnp.bfloat16)
    mid_full = gather_rows(hidden_mid)
    up_pre = jnp.dot(mid_full, w_up_layer, preferred_element_type=jnp.float32)
    active = jax.nn.gelu(up_pre).astype(jnp.bfloat16)
    branch = reduce_rows(active, w_down_layer)
    stored = (mid_full, up_pre, active, w_up_layer, w_down_layer)
    return (middle + branch, stored)


def mlp_backward(stream_grad, middle, gain_row, bias_row, stored):
    mid_rows, up_pre, active, up_weight, down_weight = stored
    branch_grad = stream_grad.astype(jnp.bfloat16)
    rows_grad = gather_grads(branch_grad)
    grad_down = lax.dot_general(
        active, rows_grad, (((0,), (0,)), ((), ())), preferred_element_type=jnp.float32
    )
    active_grad = lax.dot_general(
        rows_grad, down_weight, (((1,), (1,)), ((), ())), preferred_element_type=jnp.float32
    )
    gelu_pull = jax.vjp(jax.nn.gelu, up_pre)[1]
    up_grad = gelu_pull(active_grad)[0].astype(jnp.bfloat16)
    grad_up = lax.dot_general(
        mid_rows, up_grad, (((0,), (0,)), ((), ())), preferred_element_type=jnp.float32
    )
    hidden_grad = reduce_back(up_grad, up_weight)
    norm_pull = jax.vjp(norm_rows, middle, gain_row, bias_row)[1]
    norm_grad, gain_grad, bias_grad = norm_pull(hidden_grad)
    return (stream_grad + norm_grad, (grad_up, grad_down), (gain_grad, bias_grad))


def per_device(
    stream_in, segments, norm_gain, norm_bias, w_in, w_out, sub_kernels, w_up, w_down, cotangent
):
    stream = stream_in
    kept_layers = []
    for layer_index in range(LAYERS):
        middle, mixer_kept = mixer_forward(
            stream,
            segments,
            norm_gain[layer_index, 0],
            norm_bias[layer_index, 0],
            w_in[layer_index],
            w_out[layer_index],
            sub_kernels[layer_index],
        )
        result, mlp_kept = mlp_forward(
            middle,
            norm_gain[layer_index, 1],
            norm_bias[layer_index, 1],
            w_up[layer_index],
            w_down[layer_index],
        )
        kept_layers.append((stream, middle, mixer_kept, mlp_kept))
        stream = result
    stream_grad = cotangent
    collected = []
    for layer_index in reversed(range(LAYERS)):
        layer_in, middle, mixer_kept, mlp_kept = kept_layers[layer_index]
        middle_grad, mlp_weight_grads, mlp_norm_grads = mlp_backward(
            stream_grad, middle, norm_gain[layer_index, 1], norm_bias[layer_index, 1], mlp_kept
        )
        stream_grad, mixer_weight_grads, mixer_norm_grads = mixer_backward(
            middle_grad,
            layer_in,
            segments,
            norm_gain[layer_index, 0],
            norm_bias[layer_index, 0],
            sub_kernels[layer_index],
            mixer_kept,
        )
        grad_in_w, grad_out_w, grad_sub = mixer_weight_grads
        grad_up, grad_down = mlp_weight_grads
        gains_pair = jnp.stack([mixer_norm_grads[0], mlp_norm_grads[0]])
        biases_pair = jnp.stack([mixer_norm_grads[1], mlp_norm_grads[1]])
        collected.insert(
            0, (gains_pair, biases_pair, grad_in_w, grad_out_w, grad_sub, grad_up, grad_down)
        )
    stacks = [jnp.stack([layer_part[member] for layer_part in collected]) for member in range(7)]
    gain_stack, bias_stack, in_stack, out_stack, sub_stack, up_stack, down_stack = stacks
    in_stack, out_stack, sub_stack, up_stack, down_stack = lax.psum(
        (in_stack, out_stack, sub_stack, up_stack, down_stack), "dp"
    )
    gain_stack, bias_stack = lax.psum((gain_stack, bias_stack), ("dp", "mp"))
    return (
        stream,
        stream_grad,
        gain_stack,
        bias_stack,
        in_stack,
        out_stack,
        sub_stack,
        up_stack,
        down_stack,
    )


def solution(mesh):
    placed = (
        P(("dp", "mp"), None),
        P("dp", None),
        P(),
        P(),
        P(None, None, None, "mp"),
        P(None, "mp", None),
        P(None, None, None, "mp"),
        P(None, None, "mp"),
        P(None, "mp", None),
        P(("dp", "mp"), None),
    )
    return jax.shard_map(
        per_device,
        mesh=mesh,
        in_specs=placed,
        out_specs=(
            P(("dp", "mp"), None),
            P(("dp", "mp"), None),
            P(),
            P(),
            P(None, None, None, "mp"),
            P(None, "mp", None),
            P(None, None, None, "mp"),
            P(None, None, "mp"),
            P(None, "mp", None),
        ),
        check_vma=False,
    )
```

profile of v0, /device:TPU:0, one launch (start us, length us, event | category | flops | bytes accessed | tf_op | source)
XLA Modules:
  0.0 5051.0 jit_solution(15388029641492191558)
XLA Ops:
  130.8 12.6 constant_dynamic-update-slice_fusion.12
  260.9 110.8 %copy.9103 = bf16[32,64,64,128]{2,1,3,0:T(8,128)(2,1)} copy(bf16[32,64,64,128]{3,1,0,2:T(8,128)(2,1)} %constant_dynamic-update-slice_fusion.76) | data formatting | bytes 67108864 | tf_op jit(solution)/shard_map/while | solution.py:74
  398.3 393.0 %while.66 = (s32[]{:T(128)}, f32[1,32,64,128]{2,1,3,0:T(8,128)}, s32[31]{0:T(128)}, bf16[1,64,64,128]{3,2,1,0:T(8,128)(2,1)}, bf16[32,64,64,128]{2,1,3,0:T(8,128...) while((s32[]{:T(128)}, f32[1,32,64,128]{2,1,3,0:T(8,128)}, ...), condition=%wide.region_4.5_spmd, body=%wide.region_3.4_spmd.sunk | while | flops 34082824 | bytes 7889501 | solution.py:74
  818.7 27.2 reduce-scatter.9.cloned.1.call-done
  862.6 31.4 all-gather.11.cloned.1.call-done
  920.0 25.7 reduce-scatter.11.cloned.1.call-done
  985.1 110.6 %copy.9235 = bf16[32,64,64,128]{2,1,3,0:T(8,128)(2,1)} copy(bf16[32,64,64,128]{3,1,0,2:T(8,128)(2,1)} %constant_dynamic-update-slice_fusion.216) | data formatting | bytes 67108864 | tf_op jit(solution)/shard_map/while | solution.py:74
  1107.0 383.1 %while.67 = (s32[]{:T(128)}, f32[1,32,64,128]{2,1,3,0:T(8,128)S(1)}, s32[31]{0:T(128)}, bf16[1,64,64,128]{3,2,1,0:T(8,128)(2,1)}, bf16[32,64,64,128]{2,1,3,0:T(8...) while((s32[]{:T(128)}, ...), condition=%wide.region_13.14_spmd, body=%wide.region_12.13_spmd.sunk | while | flops 34082824 | bytes 6840925 | solution.py:74
  1496.4 43.3 reduce-scatter.13.cloned.1.call-done
  1544.7 43.2 all-gather.15.cloned.1.call-done
  1592.9 42.0 all-gather.17.cloned.1.call-done
  1651.9 37.4 reduce-scatter.17.cloned.1.call-done
  1691.4 43.3 reduce-scatter.15.cloned.1.call-done
  1741.1 44.9 all-gather.19.cloned.1.call-done
  1800.2 269.1 %while.70 = (s32[]{:T(128)}, f32[1,32,64,128]{2,1,3,0:T(8,128)}, s32[31]{0:T(128)}, bf16[1,64,64,128]{2,1,3,0:T(8,128)(2,1)S(1)}, s32[1,64,64]{2,1,0:T(8,128)S(1...) while((s32[]{:T(128)}, f32[1,32,64,128]{2,1,3,0:T(8,128)}, ...), condition=%wide.region_22.23_spmd.clone, body=%wide.region_21.22_spmd.clone.sunk | while | flops 35131400 | bytes 6312274 | solution.py:112
  2079.4 42.7 reduce-scatter.19.cloned.1.call-done
  2145.9 29.2 all-gather.21.cloned.1.call-done
  2188.5 1135.7 %while.69 = (s32[]{:T(128)}, f32[31,127,128]{2,1,0:T(8,128)}, s32[31]{0:T(128)}, bf16[1,64,64,128]{2,1,3,0:T(8,128)(2,1)S(1)}, s32[1,64,64]{2,1,0:T(8,128)S(1)},...) while((s32[]{:T(128)}, f32[31,127,128]{2,1,0:T(8,128)}, ...), condition=%wide.region_60.61_spmd, body=%wide.region_58.60_spmd.sunk | while | flops 35631236 | bytes 35375412 | solution.py:157
  3390.2 18.8 all-gather.23.cloned.1.call-done
  3430.0 1141.2 %while.68 = (s32[]{:T(128)}, f32[31,127,128]{2,1,0:T(8,128)}, s32[31]{0:T(128)}, bf16[1,64,64,128]{2,1,3,0:T(8,128)(2,1)}, s32[1,64,64]{2,1,0:T(8,128)S(1)}, /*i...) while((s32[]{:T(128)}, f32[31,127,128]{2,1,0:T(8,128)}, ...), condition=%wide.region_49.50_spmd, body=%wide.region_47.49_spmd.sunk | while | flops 35631236 | bytes 35371316 | solution.py:157
  4599.5 227.2 %while.71 = (s32[]{:T(128)}, f32[1,32,64,128]{2,1,3,0:T(8,128)S(1)}, s32[31]{0:T(128)}, bf16[1,64,64,128]{2,1,3,0:T(8,128)(2,1)}, s32[1,64,64]{2,1,0:T(8,128)S(1...) while((s32[]{:T(128)}, ...), condition=%wide.region_30.31_spmd.clone, body=%wide.region_29.30_spmd.clone.sunk | while | flops 35131400 | bytes 5259602 | solution.py:112
  4844.7 97.1 %all-reduce.32.cloned.1.call-done = (f32[2,512,2,128]{1,3,2,0:T(8,128)}, f32[2,128,512]{2,1,0:T(8,128)}, f32[2,6,32,128]{3,2,1,0:T(8,128)}, f32[2,512,512]{2,1,0:T(8,128)}, f32[2,512,512]{2,1,0:T(8,128)}) async-done(((f32[2,512,2,128]{1,3,2,0:T(8,128)}, f32[2,128,512]{2,1,0:T(8,128)}, f32[2,6,32,128]{3,2,1,0:T(8,128)}, f32[2,512,512]{2,1,0:T(8,128)}, f32[2,512,512]{2,1,0:T(8,128)}), ...) | async-done | bytes 5963792 | tf_op jit(solution)/shard_map/psum | solution.py:348
  4944.1 44.6 reduce-scatter.23.cloned.1.call-done
  4991.8 39.7 all-reduce.28
  (2011 shorter events, 3665.8 us)
Async XLA Ops:
  7.2 377.7 %all-gather.9.cloned.1.call-start = ((), (), s32[]{:S(2)}) async-start(), calls=%async_computation.8 | async-start | bytes 2621440 | tf_op jit(solution)/shard_map/all_gather | solution.py:170
  15.7 830.1 %reduce-scatter.9.cloned.1.call-start = ((), (), s32[]{:S(2)}) async-start(), calls=%async_computation.9 | async-start | bytes 2621440 | tf_op jit(solution)/shard_map/reduce_scatter | solution.py:182
  384.9 710.8 %copy-start.106 = (bf16[1,512,2,128]{3,2,1,0:T(2,128)(2,1)}, bf16[1,512,2,128]{3,2,1,0:T(2,128)(2,1)S(1)}, u32[]{:S(2)}) copy-start(bf16[1,512,2,128]{3,2,1,0:T(2,128)(2,1)S(1)} %get-tuple-element.2039) | copy-start | bytes 786436
  398.3 447.5 %copy-start.1 = (f32[512,512]{1,0:T(8,128)S(1)}, f32[512,512]{1,0:T(8,128)}, u32[]{:S(2)}) copy-start(f32[512,512]{1,0:T(8,128)} %param.22) | copy-start | bytes 3145732
  398.3 449.1 %copy-start.133 = (f32[1,1,512]{2,1,0:T(1,128)S(1)}, f32[1,1,512]{2,1,0:T(1,128)}, u32[]{:S(2)}) copy-start(f32[1,1,512]{2,1,0:T(1,128)} %get-tuple-element.2119) | copy-start | bytes 6148
  398.3 449.1 %copy-start.150 = (f32[1,1,512]{2,1,0:T(1,128)S(1)}, f32[1,1,512]{2,1,0:T(1,128)}, u32[]{:S(2)}) copy-start(f32[1,1,512]{2,1,0:T(1,128)} %get-tuple-element.2123) | copy-start | bytes 6148
  799.1 94.8 %all-gather.11.cloned.1.call-start = ((), (), s32[]{:S(2)}) async-start(), calls=%async_computation.10 | async-start | bytes 2621440 | tf_op jit(solution)/shard_map/all_gather | solution.py:170
  848.5 97.1 %reduce-scatter.11.cloned.1.call-start = ((), (), s32[]{:S(2)}) async-start(), calls=%async_computation.11 | async-start | bytes 2621440 | tf_op jit(solution)/shard_map/reduce_scatter | solution.py:182
  902.9 192.8 %all-gather.13.cloned.1.call-start = ((), (), s32[]{:S(2)}) async-start(), calls=%async_computation.12 | async-start | bytes 2621440 | tf_op jit(solution)/shard_map/all_gather | solution.py:170
  948.9 590.8 %reduce-scatter.13.cloned.1.call-start = ((), (), s32[]{:S(2)}) async-start(), calls=%async_computation.13 | async-start | bytes 2621440 | tf_op jit(solution)/shard_map/reduce_scatter | solution.py:182
  1102.3 392.0 %copy-start.113 = (bf16[2,128,512]{2,1,0:T(8,128)(2,1)S(1)}, bf16[2,128,512]{2,1,0:T(8,128)(2,1)}, u32[]{:S(2)}) copy-start(bf16[2,128,512]{2,1,0:T(8,128)(2,1)} %param.27) | copy-start | bytes 786436
  1107.0 434.5 %copy-start.128 = (f32[1,1,512]{2,1,0:T(1,128)S(1)}, f32[1,1,512]{2,1,0:T(1,128)}, u32[]{:S(2)}) copy-start(f32[1,1,512]{2,1,0:T(1,128)} %get-tuple-element.2118) | copy-start | bytes 6148
  1107.0 434.5 %copy-start.148 = (f32[1,1,512]{2,1,0:T(1,128)S(1)}, f32[1,1,512]{2,1,0:T(1,128)}, u32[]{:S(2)}) copy-start(f32[1,1,512]{2,1,0:T(1,128)} %get-tuple-element.2122) | copy-start | bytes 6148
  1496.3 91.6 %all-gather.15.cloned.1.call-start = ((), (), s32[]{:S(2)}) async-start(), calls=%async_computation.14 | async-start | bytes 2621440 | tf_op jit(solution)/shard_map/all_gather | solution.py:170
  1542.5 92.3 %all-gather.17.cloned.1.call-start = ((), (), s32[]{:S(2)}) async-start(), calls=%async_computation.16 | async-start | bytes 2621440 | tf_op jit(solution)/shard_map/all_gather | solution.py:174
  1544.7 144.6 %reduce-scatter.17.cloned.1.call-start = ((), (), s32[]{:S(2)}) async-start(), calls=%async_computation.17 | async-start | bytes 2621440 | tf_op jit(solution)/shard_map/reduce_scatter | solution.py:199
  1646.6 88.1 %reduce-scatter.15.cloned.1.call-start = ((), (), s32[]{:S(2)}) async-start(), calls=%async_computation.15 | async-start | bytes 2621440 | tf_op jit(solution)/shard_map/reduce_scatter | solution.py:182
  1651.9 134.1 %all-gather.19.cloned.1.call-start = ((), (), s32[]{:S(2)}) async-start(), calls=%async_computation.18 | async-start | bytes 2621440 | tf_op jit(solution)/shard_map/all_gather | solution.py:174
  1740.6 381.5 %reduce-scatter.19.cloned.1.call-start = ((), (), s32[]{:S(2)}) async-start(), calls=%async_computation.19 | async-start | bytes 2621440 | tf_op jit(solution)/shard_map/reduce_scatter | solution.py:199
  2079.4 95.7 %all-gather.21.cloned.1.call-start = ((), (), s32[]{:S(2)}) async-start(), calls=%async_computation.20 | async-start | bytes 2621440 | tf_op jit(solution)/shard_map/all_gather | solution.py:174
  2129.6 1228.2 %reduce-scatter.21.cloned.1.call-start = ((), (), s32[]{:S(2)}) async-start(), calls=%async_computation.21 | async-start | bytes 2621440 | tf_op jit(solution)/shard_map/reduce_scatter | solution.py:199
  2186.7 1222.3 %all-gather.23.cloned.1.call-start = ((), (), s32[]{:S(2)}) async-start(), calls=%async_computation.22 | async-start | bytes 2621440 | tf_op jit(solution)/shard_map/all_gather | solution.py:174
  3364.2 1577.6 %all-reduce.32.cloned.1.call-start = ((), (), s32[]{:S(2)}) async-start(), calls=%async_computation.24 | async-start | bytes 11927552 | tf_op jit(solution)/shard_map/psum | solution.py:348
  4841.4 147.3 %reduce-scatter.23.cloned.1.call-start = ((), (), s32[]{:S(2)}) async-start(), calls=%async_computation.23 | async-start | bytes 2621440 | tf_op jit(solution)/shard_map/reduce_scatter | solution.py:199
  (150 other events, 11397.0 us)
Sparse Core Ops, SparseCore 0:
  15.8 48.6 all-gather.8
  799.3 46.5 reduce-scatter.8
  848.6 45.2 all-gather.10
  903.0 42.5 reduce-scatter.10
  949.0 45.2 all-gather.12
  1496.4 43.1 reduce-scatter.12
  1542.7 45.2 all-gather.14
  1590.2 44.6 all-gather.16
  1646.7 42.5 reduce-scatter.16
  1691.5 43.1 reduce-scatter.14
  1740.7 45.2 all-gather.18
  2079.5 42.5 reduce-scatter.18
  2129.8 45.2 all-gather.20
  2186.8 42.6 reduce-scatter.20
  3364.4 44.5 all-gather.22
  4841.5 100.2 all-reduce.31
  4944.7 43.9 reduce-scatter.22
where the time goes:
time: 5090 us; the launch traced here: 5050 us
  local copies, waits for them, and re-layouts  2790 us (55%)
  matrix products  822 us (16%)
  waiting for transfers between devices  571 us (11%)
  loops' own time  525 us (10%)
  other arithmetic  285 us (6%)
    reshape x64, local copies, waits for them, and re-layouts, diagonal_sums(): flat.reshape(block_rows, 2 * block_rows - 1, channels)  668 us
    rev x64, local copies, waits for them, and re-layouts, diagonal_sums(): flipped = tile[:, ::-1]  462 us
    while x124, local copies, waits for them, and re-layouts  335 us
    unnamed x592, local copies, waits for them, and re-layouts  311 us
    dot_general x62, matrix products, lag_step(): jnp.einsum('rnac,rnbc->abc', masked, source, preferred_element_type=jnp.f...  253 us
    dot_general x62, matrix products, lag_step(): jnp.einsum('abc,rnbc->rnac', tile, shifted, preferred_element_type=jnp.fl...  234 us
    while x4, local copies, waits for them, and re-layouts, conv_blocks(): total, _ = lax.scan(lag_step, total, jnp.arange(1, blocks, dtype=jnp.int32))  225 us
    dot_general x62, matrix products, lag_step(): jnp.einsum('abc,rnac->rnbc', tile, masked, preferred_element_type=jnp.flo...  218 us
  transfers between devices with their start and end apart: 17, of which 14 were waited for; matrix products, arithmetic and copies ran while one was open for 34% of the time, Pallas kernels for 0%

commit v1 on v0

v1 whole, which is shorter than its diff:
```python
import functools

import jax
import jax.numpy as jnp
import numpy as np
from jax import lax
from jax.sharding import PartitionSpec as P

DECAY_RATE = 0.5
EPSILON = 1e-05
BF = jnp.bfloat16
F32 = jnp.float32


def norm_rows(values, gain_row, bias_row):
    centred = values - jnp.mean(values, axis=-1, keepdims=True)
    variance = jnp.mean(centred * centred, axis=-1, keepdims=True)
    return centred * lax.rsqrt(variance + EPSILON) * gain_row + bias_row


def build_kernel(sub_taps):
    pieces = []
    for level_index in range(sub_taps.shape[0]):
        repeats = 2 ** max(level_index, 1)
        pieces.append(jnp.repeat(sub_taps[level_index], repeats, axis=0) * DECAY_RATE**level_index)
    raw_taps = jnp.concatenate(pieces, axis=0)
    return raw_taps * lax.rsqrt(jnp.sum(raw_taps * raw_taps, axis=0, keepdims=True) + EPSILON)


def transform_matrix(quarter):
    freq = np.arange(quarter)[:, None] + 0.5
    angle = np.pi * freq * np.arange(quarter)[None, :] / quarter
    return np.concatenate([np.cos(angle), -np.sin(angle)], axis=0).astype(np.float32)


def mul(a, b):
    return (a[0] * b[0] - a[1] * b[1], a[0] * b[1] + a[1] * b[0])


def mul_conj(a, b):
    return (a[0] * b[0] + a[1] * b[1], a[0] * b[1] - a[1] * b[0])


def add(a, b):
    return (a[0] + b[0], a[1] + b[1])


def turn(a, sign):
    return (-sign * a[1], sign * a[0])


def turn_back(a, sign):
    return (sign * a[1], -sign * a[0])


def split_docs(blocks, seg):
    long_doc = seg[1, 0]
    kept = [jnp.where((seg[n] == long_doc)[:, None], blocks[n], 0) for n in range(4)]
    for k in range(3):
        doc = k + (k >= long_doc).astype(jnp.int32)
        kept.append(
            jnp.where((seg[0] == doc)[:, None], blocks[0], 0)
            + jnp.where((seg[3] == doc)[:, None], blocks[3], 0)
        )
    return jnp.stack(kept)


def join_docs(parts, seg):
    long_doc = seg[1, 0]
    out = [jnp.where((seg[n] == long_doc)[:, None], parts[n], 0) for n in range(4)]
    for k in range(3):
        doc = k + (k >= long_doc).astype(jnp.int32)
        for n in (0, 3):
            out[n] = out[n] + jnp.where((seg[n] == doc)[:, None], parts[4 + k], 0)
    return jnp.stack(out)


def spectrum(blocks, table):
    both = jnp.einsum("fp,npc->nfc", table, blocks.astype(BF), preferred_element_type=F32)
    quarter = blocks.shape[1]
    return both[:, :quarter], both[:, quarter:]


def unspectrum(pair, table):
    both = jnp.concatenate(pair, axis=1).astype(BF)
    return jnp.einsum("fp,nfc->npc", table, both, preferred_element_type=F32) / table.shape[1]


def at(pair, n):
    return (pair[0][n], pair[1][n])


def windows(kernel, table, sign):
    length, channels = kernel.shape
    quarter = length // 4
    d = spectrum(kernel.reshape(4, quarter, channels), table)
    out = [at(d, 0)]
    for m in range(1, 4):
        out.append(add(at(d, m), turn(at(d, m - 1), sign)))
    return out


def conv(values, kernel, seg, table, sign):
    w = windows(kernel, table, sign)
    x = spectrum(split_docs(values, seg), table)
    ys = []
    for n in range(7):
        if n < 4:
            y = mul(w[0], at(x, n))
            for m in range(1, n + 1):
                y = add(y, mul(w[m], at(x, n - m)))
        else:
            y = mul(w[0], at(x, n))
        ys.append(y)
    parts = unspectrum((jnp.stack([y[0] for y in ys]), jnp.stack([y[1] for y in ys])), table)
    return join_docs(parts, seg), x


def conv_back(upstream, x, kernel, seg, table, sign):
    w = windows(kernel, table, sign)
    c = spectrum(split_docs(upstream, seg), table)
    gs = []
    for n in range(7):
        g = mul_conj(w[0], at(c, n))
        if n < 4:
            for m in range(1, 4 - n):
                g = add(g, mul_conj(w[m], at(c, n + m)))
        gs.append(g)
    parts = unspectrum((jnp.stack([g[0] for g in gs]), jnp.stack([g[1] for g in gs])), table)
    dw = []
    for m in range(4):
        total = None
        for n in range(m, 4):
            term = mul_conj(at(x, n - m), at(c, n))
            total = term if total is None else add(total, term)
        dw.append(total)
    for n in range(4, 7):
        dw[0] = add(dw[0], mul_conj(at(x, n), at(c, n)))
    dd = [add(dw[m], turn_back(dw[m + 1], sign)) if m < 3 else dw[m] for m in range(4)]
    taps = unspectrum((jnp.stack([g[0] for g in dd]), jnp.stack([g[1] for g in dd])), table)
    return join_docs(parts, seg), taps.reshape(-1, taps.shape[2])


def to_channels(rows):
    n = lax.axis_size("mp")
    return lax.all_to_all(rows.reshape(rows.shape[0], n, -1), "mp", 1, 0)


def to_tokens(blocks):
    got = lax.all_to_all(blocks, "mp", 0, 1)
    return got.reshape(got.shape[0], -1)


def dot_tn(a, b):
    return lax.dot_general(a, b, (((0,), (0,)), ((), ())), preferred_element_type=F32)


def dot_nt(a, b):
    return lax.dot_general(a, b, (((1,), (1,)), ((), ())), preferred_element_type=F32)


def per_device(
    stream_in, segments, norm_gain, norm_bias, w_in, w_out, sub_kernels, w_up, w_down, cotangent
):
    layers = w_in.shape[0]
    quarter = segments.shape[1] // 4
    seg = segments.reshape(4, quarter)
    table = jnp.asarray(transform_matrix(quarter)).astype(BF)
    sign = jnp.asarray(1.0 - 2.0 * (np.arange(quarter)[:, None] % 2), F32)
    w_in = lax.all_gather(w_in, "mp", axis=3, tiled=True)
    w_out = lax.all_gather(w_out, "mp", axis=1, tiled=True)
    w_up = lax.all_gather(w_up, "mp", axis=2, tiled=True)
    w_down = lax.all_gather(w_down, "mp", axis=1, tiled=True)
    stream = stream_in
    kept = []
    for l in range(layers):
        hidden = norm_rows(stream, norm_gain[l, 0], norm_bias[l, 0]).astype(BF)
        conv_input = jnp.dot(hidden, w_in[l, :, 0], preferred_element_type=F32).astype(BF)
        gate_pre = jnp.dot(hidden, w_in[l, :, 1], preferred_element_type=F32)
        kernel = build_kernel(sub_kernels[l]).astype(BF)
        convolved, x = conv(to_channels(conv_input), kernel, seg, table, sign)
        convolved = to_tokens(convolved.astype(BF)).astype(F32)
        gated = (jax.nn.gelu(gate_pre) * convolved).astype(BF)
        middle = stream + jnp.dot(gated, w_out[l], preferred_element_type=F32)
        hidden_mid = norm_rows(middle, norm_gain[l, 1], norm_bias[l, 1]).astype(BF)
        up_pre = jnp.dot(hidden_mid, w_up[l], preferred_element_type=F32)
        active = jax.nn.gelu(up_pre).astype(BF)
        out = middle + jnp.dot(active, w_down[l], preferred_element_type=F32)
        kept.append((stream, hidden, gate_pre, kernel, x, convolved, gated, middle, hidden_mid, up_pre, active))
        stream = out
    grad = cotangent
    collected = []
    for l in reversed(range(layers)):
        layer_in, hidden, gate_pre, kernel, x, convolved, gated, middle, hidden_mid, up_pre, active = kept[l]
        branch_grad = grad.astype(BF)
        g_down = dot_tn(active, branch_grad)
        up_grad = jax.vjp(jax.nn.gelu, up_pre)[1](dot_nt(branch_grad, w_down[l]))[0].astype(BF)
        g_up = dot_tn(hidden_mid, up_grad)
        hidden_grad = dot_nt(up_grad, w_up[l])
        pull = jax.vjp(norm_rows, middle, norm_gain[l, 1], norm_bias[l, 1])[1]
        norm_grad, gain1, bias1 = pull(hidden_grad)
        middle_grad = grad + norm_grad
        out_grad = middle_grad.astype(BF)
        g_out = dot_tn(gated, out_grad)
        gated_grad = dot_nt(out_grad, w_out[l])
        act, gate_pull = jax.vjp(jax.nn.gelu, gate_pre)
        conv_grad = (gated_grad * act).astype(BF)
        gate_grad = gate_pull(gated_grad * convolved)[0].astype(BF)
        input_grad, taps = conv_back(to_channels(conv_grad), x, kernel, seg, table, sign)
        input_grad = to_tokens(input_grad.astype(BF))
        g_sub = jax.vjp(build_kernel, sub_kernels[l])[1](taps)[0]
        g_in = jnp.stack([dot_tn(hidden, input_grad), dot_tn(hidden, gate_grad)], axis=1)
        hidden_grad = dot_nt(input_grad, w_in[l, :, 0]) + dot_nt(gate_grad, w_in[l, :, 1])
        pull = jax.vjp(norm_rows, layer_in, norm_gain[l, 0], norm_bias[l, 0])[1]
        norm_grad, gain0, bias0 = pull(hidden_grad)
        grad = middle_grad + norm_grad
        collected.insert(0, (jnp.stack([gain0, gain1]), jnp.stack([bias0, bias1]), g_in, g_out, g_sub, g_up, g_down))
    gain, bias, g_in, g_out, g_sub, g_up, g_down = [jnp.stack([c[i] for c in collected]) for i in range(7)]
    g_in = lax.psum_scatter(g_in.astype(BF), "mp", scatter_dimension=3, tiled=True)
    g_out = lax.psum_scatter(g_out.astype(BF), "mp", scatter_dimension=1, tiled=True)
    g_up = lax.psum_scatter(g_up.astype(BF), "mp", scatter_dimension=2, tiled=True)
    g_down = lax.psum_scatter(g_down.astype(BF), "mp", scatter_dimension=1, tiled=True)
    g_in, g_out, g_sub, g_up, g_down = lax.psum(
        (g_in.astype(F32), g_out.astype(F32), g_sub, g_up.astype(F32), g_down.astype(F32)), "dp"
    )
    gain, bias = lax.psum((gain, bias), ("dp", "mp"))
    return stream, grad, gain, bias, g_in, g_out, g_sub, g_up, g_down


def solution(mesh):
    rows = P(("dp", "mp"), None)
    last = P(None, None, None, "mp")
    mid = P(None, "mp", None)
    return jax.shard_map(
        per_device,
        mesh=mesh,
        in_specs=(rows, P("dp", None), P(), P(), last, mid, last, P(None, None, "mp"), mid, rows),
        out_specs=(rows, rows, P(), P(), last, mid, last, P(None, None, "mp"), mid),
        check_vma=False,
    )
```

time: 5090 us -> 815 us (0.16)
  local copies, waits for them, and re-layouts: 2790 us -> 50.9 us
  matrix products: 822 us -> 88.4 us
  loops' own time: 525 us -> 0 us
  waiting for transfers between devices: 571 us -> 339 us
  other arithmetic: 285 us -> 87.3 us
  blocking collectives: 39.7 us -> 197 us
    dot_general x216 -> x42, matrix products: 822 us -> 88.4 us  [the longest x10 22.4 us: dot_nt(): lax.dot_general(a, b, (((1,), (1,)), ((), ())), preferred_element_type=F32)]
    reshape x65 -> x1, local copies, waits for them, and re-layouts: 668 us -> 0.01 us  [per_device(): seg = segments.reshape(4, quarter)]
    while x130 -> x0, local copies, waits for them, and re-layouts: 566 us -> none
    another operation x6 -> x0, loops' own time: 525 us -> none  [the longest x2 203 us: conv_blocks(): total, _ = lax.scan(lag_step, total, jnp.arange(1, blocks, dtype=jnp.int32))]
    rev x64 -> x0, local copies, waits for them, and re-layouts: 462 us -> none  [diagonal_sums(): flipped = tile[:, ::-1]]
    dynamic_slice x310 -> x0, local copies, waits for them, and re-layouts: 434 us -> none  [the longest x124 218 us: lag_step(): lax.dynamic_slice_in_dim(padded_source, blocks - lag_block, blocks, 1)]
    unnamed x592 -> x251, local copies, waits for them, and re-layouts: 311 us -> 38.7 us
    reduce_sum x66 -> x0, other arithmetic: 191 us -> none  [the longest x64 187 us: diagonal_sums(): jnp.sum(flat.reshape(block_rows, 2 * block_rows - 1, channels), axis=0)]
  transfers between devices with their start and end apart: 17 -> 15, of which waited for: 14 -> 11; matrix products, arithmetic and copies ran while one was open for 34% -> 18% of each run, Pallas kernels for 0% -> 0%
where the time goes in v1:
time: 815 us; the launch traced here: 807 us
  waiting for transfers between devices  339 us (42%)
  blocking collectives  197 us (24%)
  matrix products  88.4 us (11%)
  other arithmetic  87.3 us (11%)
  local copies, waits for them, and re-layouts  50.9 us (6%)
  starting transfers between devices  25.7 us (3%)
  between operations  18.3 us (2%)
    psum x1, blocking collectives, per_device(): lax.psum((g_in.astype(F32), g_out.astype(F32), g_sub, g_up.astype(F32), g...  120 us
    reduce_scatter x1, waiting for transfers between devices, per_device(): lax.psum_scatter(g_up.astype(BF), 'mp', scatter_dimension=2, tiled=True)  79.6 us
    all_gather x1, waiting for transfers between devices, per_device(): w_down = lax.all_gather(w_down, 'mp', axis=1, tiled=True)  76.1 us
    all_gather x1, waiting for transfers between devices, per_device(): w_up = lax.all_gather(w_up, 'mp', axis=2, tiled=True)  47 us
    all_to_all x3, waiting for transfers between devices, to_tokens(): got = lax.all_to_all(blocks, 'mp', 0, 1)  45.6 us
    psum x1, blocking collectives, per_device(): gain, bias = lax.psum((gain, bias), ('dp', 'mp'))  43.3 us
    all_to_all x3, waiting for transfers between devices, to_channels(): return lax.all_to_all(rows.reshape(rows.shape[0], n, -1), 'mp', 1, 0)  41.2 us
    all_gather x1, waiting for transfers between devices, per_device(): w_in = lax.all_gather(w_in, 'mp', axis=3, tiled=True)  40.1 us
  transfers between devices with their start and end apart: 15, of which 11 were waited for; matrix products, arithmetic and copies ran while one was open for 18% of the time, Pallas kernels for 0%

profile of v1, /device:TPU:0, one launch (start us, length us, event | category | flops | bytes accessed | tf_op | source)
XLA Modules:
  0.0 806.7 jit_solution(9169208446464100005)
XLA Ops:
  19.1 40.1 %all-gather.5.cloned.1.call-done = bf16[2,512,2,512]{3,1,2,0:T(8,128)(2,1)} async-done(((bf16[2,512,2,128]{3,1,2,0:T(8,128)(2,1)}), bf16[2,512,2,512]{3,1,2,0:T(8,128)(2,1)}) %all-gather.5.cloned.1.call-update) | async-done | bytes 2097168 | tf_op jit(solution)/shard_map/all_gather | solution.py:170
  69.0 23.4 %all-to-all-done = bf16[1,512,4,128]{1,3,0,2:T(8,128)(2,1)} async-done(((bf16[1,512,4,128]{1,3,0,2:T(8,128)(2,1)}), bf16[1,512,4,128]{1,3,0,2:T(8,128)(2,1)}, u32[]{:S(2)}, u32[]{:S(2)}) %all-to-all-start) | async-done | bytes 524320 | tf_op jit(solution)/shard_map/all_to_all | solution.py:146
  107.4 4.4 all-to-all-start.1
  112.5 23.8 %all-to-all-done.1 = bf16[4,512,1,128]{1,3,2,0:T(8,128)(2,1)} async-done(((bf16[4,512,1,128]{1,3,2,0:T(8,128)(2,1)}), bf16[4,512,1,128]{1,3,2,0:T(8,128)(2,1)}, u32[]{:S(2)}, u32[]{:S(2)}) %all-to-all-start.1) | async-done | bytes 524320 | tf_op jit(solution)/shard_map/all_to_all | solution.py:150
  142.5 47.0 %all-gather.9.cloned.1.call-done = bf16[2,512,2048]{2,1,0:T(8,128)(2,1)} async-done(((bf16[2,512,512]{2,1,0:T(8,128)(2,1)}), bf16[2,512,2048]{2,1,0:T(8,128)(2,1)}) %all-gather.9.cloned.1.call-update) | async-done | bytes 4194320 | tf_op jit(solution)/shard_map/all_gather | solution.py:172
  189.5 5.4 fusion.19
  194.9 76.1 %all-gather.11.cloned.1.call-done = bf16[2,2048,512]{2,1,0:T(8,128)(2,1)} async-done(((bf16[2,512,512]{2,1,0:T(8,128)(2,1)}), bf16[2,2048,512]{2,1,0:T(8,128)(2,1)}) %all-gather.11.cloned.1.call-update) | async-done | bytes 4194320 | tf_op jit(solution)/shard_map/all_gather | solution.py:173
  271.0 4.8 fusion.209
  290.0 9.1 %all-to-all-done.2 = bf16[1,512,4,128]{1,3,0,2:T(8,128)(2,1)} async-done(((bf16[1,512,4,128]{1,3,0,2:T(8,128)(2,1)}), bf16[1,512,4,128]{1,3,0,2:T(8,128)(2,1)}, u32[]{:S(2)}, u32[]{:S(2)}) %all-to-all-start.2) | async-done | bytes 524320 | tf_op jit(solution)/shard_map/all_to_all | solution.py:146
  312.6 4.5 all-to-all-start.3
  319.7 11.5 %all-to-all-done.3 = bf16[4,512,1,128]{1,3,2,0:T(8,128)(2,1)} async-done(((bf16[4,512,1,128]{1,3,2,0:T(8,128)(2,1)}), bf16[4,512,1,128]{1,3,2,0:T(8,128)(2,1)}, u32[]{:S(2)}, u32[]{:S(2)}) %all-to-all-start.3) | async-done | bytes 524320 | tf_op jit(solution)/shard_map/all_to_all | solution.py:150
  354.8 16.6 %all_to_all.108 = bf16[1,512,4,128]{1,3,0,2:T(8,128)(2,1)S(1)} all-to-all(bf16[1,512,4,128]{1,3,0,2:T(8,128)(2,1)S(1)} %bitcast.518), channel_id=1, replica_groups=mesh['dp'=8,'mp'=4] {'mp'}, dimensions={2} | all-to-all | bytes 1048576 | tf_op jit(solution)/shard_map/all_to_all | solution.py:146
  377.5 16.7 %all_to_all.109 = bf16[4,512,1,128]{1,3,2,0:T(8,128)(2,1)S(1)} all-to-all(bf16[4,512,1,128]{1,3,2,0:T(8,128)(2,1)S(1)} %pad_maximum_fusion.6), channel_id=1, replica_groups=mesh['dp'=8,'mp'=4] {'mp'}, dimensions={0} | all-to-all | bytes 1048576 | tf_op jit(solution)/shard_map/all_to_all | solution.py:150
  415.5 4.1 all-to-all-start.6
  424.5 8.7 %all-to-all-done.6 = bf16[1,512,4,128]{1,3,0,2:T(8,128)(2,1)} async-done(((bf16[1,512,4,128]{1,3,0,2:T(8,128)(2,1)}), bf16[1,512,4,128]{1,3,0,2:T(8,128)(2,1)}, u32[]{:S(2)}, u32[]{:S(2)}) %all-to-all-start.6) | async-done | bytes 524320 | tf_op jit(solution)/shard_map/all_to_all | solution.py:146
  453.5 10.3 %all-to-all-done.7 = bf16[4,512,1,128]{1,3,2,0:T(8,128)(2,1)S(1)} async-done(((bf16[4,512,1,128]{1,3,2,0:T(8,128)(2,1)}), bf16[4,512,1,128]{1,3,2,0:T(8,128)(2,1)S(1)}, u32[]{:S(2)}, u32[]{:S(2)}) %all-to-all-start.7) | async-done | bytes 524320 | tf_op jit(solution)/shard_map/all_to_all | solution.py:150
  469.4 4.6 reshape.2967
  474.0 4.2 fusion.17
  494.9 4.8 fusion.52
  501.0 4.2 add_convert_fusion.6
  543.7 43.3 %all-reduce.12 = (f32[2,2,512]{2,1,0:T(2,128)}, f32[2,2,512]{2,1,0:T(2,128)}) all-reduce(f32[2,2,512]{2,1,0:T(2,128)S(1)} %pad_maximum_fusion.9, f32[2,2,512]{2,1,0:T(2,128)S(1)} %pad_maximum_fusion.10), channel_id=1, replica_groups=mesh['dp'=8,'mp'=4] {'dp','mp'}, use_global_device_ids=true, to_apply=%region_22.23 | all-reduce | flops 4096 | bytes 32768 | tf_op jit(solution)/shard_map/psum | solution.py:226
  589.0 7.4 reduce-scatter.11.cloned.1.call-done
  596.5 79.6 %reduce-scatter.9.cloned.1.call-done = bf16[2,512,512]{2,1,0:T(8,128)(2,1)} async-done(((bf16[2,512,2048]{2,1,0:T(8,128)(2,1)}), bf16[2,512,512]{2,1,0:T(8,128)(2,1)}) %reduce-scatter.9.cloned.1.call-update) | async-done | bytes 1048592 | tf_op jit(solution)/shard_map/reduce_scatter | solution.py:221
  676.1 120.4 %all-reduce.18 = (f32[2,512,2,128]{3,1,2,0:T(8,128)S(1)}, f32[2,128,512]{2,1,0:T(8,128)}, f32[2,512,512]{2,1,0:T(8,128)}, f32[2,512,512]{2,1,0:T(8,128)}) all-reduce(bf16[2,512,2,128]{3,1,2,0:T(8,128)(2,1)S(1)} %copy.92, bf16[2,128,512]{2,1,0:T(8,128)(2,1)} %reduce-scatter.7.cloned.1.call-done, ...), channel_id=1, replica_groups=mesh['dp'=8,'mp'=4] {'dp'}, use_global_device_ids=true, to_apply=%region_29.30 | all-reduce | flops 1441792 | bytes 8650752 | tf_op jit(solution)/shard_map/psum | solution.py:223
  (498 shorter events, 213.3 us)
Async XLA Ops:
  7.2 51.9 %all-gather.5.cloned.1.call-start = ((), (), s32[]{:S(2)}) async-start(), calls=%async_computation.12 | async-start | bytes 2621440 | tf_op jit(solution)/shard_map/all_gather | solution.py:170
  9.3 130.3 %all-gather.7.cloned.1.call-start = ((), (), s32[]{:S(2)}) async-start(), calls=%async_computation.13 | async-start | bytes 1310720 | tf_op jit(solution)/shard_map/all_gather | solution.py:171
  10.0 179.5 %all-gather.9.cloned.1.call-start = ((), (), s32[]{:S(2)}) async-start(), calls=%async_computation.14 | async-start | bytes 5242880 | tf_op jit(solution)/shard_map/all_gather | solution.py:172
  10.8 260.2 %all-gather.11.cloned.1.call-start = ((), (), s32[]{:S(2)}) async-start(), calls=%async_computation.15 | async-start | bytes 5242880 | tf_op jit(solution)/shard_map/all_gather | solution.py:173
  11.7 127.9 %copy-start.10 = (f32[512,512]{0,1:T(8,128)}, f32[512,512]{0,1:T(8,128)S(1)}, u32[]{:S(2)}) copy-start(f32[512,512]{0,1:T(8,128)S(1)} %copy.62) | copy-start | bytes 3145732
  11.9 49.6 %copy-start.83 = (f32[512]{0:T(512)}, f32[512]{0:T(512)S(1)}, u32[]{:S(2)}) copy-start(f32[512]{0:T(512)S(1)} %broadcast_multiply_fusion.3) | copy-start | bytes 6148
  15.7 45.8 %copy-start.88 = (f32[1,1,512]{2,1,0:T(1,128)}, f32[1,1,512]{2,1,0:T(1,128)S(1)}, u32[]{:S(2)}) copy-start(f32[1,1,512]{2,1,0:T(1,128)S(1)} %get-tuple-element.164) | copy-start | bytes 6148
  16.6 44.9 %copy-start.93 = (f32[512]{0:T(512)}, f32[512]{0:T(512)S(1)}, u32[]{:S(2)}) copy-start(f32[512]{0:T(512)S(1)} %multiply_reduce_fusion.15) | copy-start | bytes 6148
  16.7 44.8 %copy-start.91 = (f32[512]{0:T(512)}, f32[512]{0:T(512)S(1)}, u32[]{:S(2)}) copy-start(f32[512]{0:T(512)S(1)} %fusion.190) | copy-start | bytes 6148
  18.8 47.8 %copy-start.22 = (f32[2048,128]{1,0:T(8,128)}, f32[2048,128]{1,0:T(8,128)S(1)}, u32[]{:S(2)}) copy-start(f32[2048,128]{1,0:T(8,128)S(1)} %constant_dynamic-update-slice_fusion) | copy-start | bytes 3145732
  19.1 47.6 %copy-start.38 = (bf16[512,512]{0,1:T(8,128)(2,1)}, bf16[512,512]{0,1:T(8,128)(2,1)S(1)}, u32[]{:S(2)}) copy-start(bf16[512,512]{0,1:T(8,128)(2,1)S(1)} %add_convert_fusion.3) | copy-start | bytes 1572868
  61.5 30.9 %all-to-all-start = ((bf16[1,512,4,128]{1,3,0,2:T(8,128)(2,1)}), bf16[1,512,4,128]{1,3,0,2:T(8,128)(2,1)}, u32[]{:S(2)}, u32[]{:S(2)}) async-start(bf16[1,512,4,128]{1,3,0,2:T(8,128)(2,1)} %bitcast.21), calls=%async_computation | async-start | bytes 1048576 | tf_op jit(solution)/shard_map/all_to_all | solution.py:146
  107.4 29.0 %all-to-all-start.1 = ((bf16[4,512,1,128]{1,3,2,0:T(8,128)(2,1)}), bf16[4,512,1,128]{1,3,2,0:T(8,128)(2,1)}, u32[]{:S(2)}, u32[]{:S(2)}) async-start(bf16[4,512,1,128]{1,3,2,0:T(8,128)(2,1)} %pad_maximum_fusion.4), calls=%async_computation.1 | async-start | bytes 1048576 | tf_op jit(solution)/shard_map/all_to_all | solution.py:150
  189.5 81.5 %copy-start.18 = (f32[512,512]{0,1:T(8,128)S(1)}, f32[512,512]{0,1:T(8,128)}, u32[]{:S(2)}) copy-start(f32[512,512]{0,1:T(8,128)} %copy-done.17) | copy-start | bytes 3145732
  280.1 19.0 %all-to-all-start.2 = ((bf16[1,512,4,128]{1,3,0,2:T(8,128)(2,1)}), bf16[1,512,4,128]{1,3,0,2:T(8,128)(2,1)}, u32[]{:S(2)}, u32[]{:S(2)}) async-start(bf16[1,512,4,128]{1,3,0,2:T(8,128)(2,1)} %bitcast.517), calls=%async_computation.2 | async-start | bytes 1048576 | tf_op jit(solution)/shard_map/all_to_all | solution.py:146
  312.6 18.6 %all-to-all-start.3 = ((bf16[4,512,1,128]{1,3,2,0:T(8,128)(2,1)}), bf16[4,512,1,128]{1,3,2,0:T(8,128)(2,1)}, u32[]{:S(2)}, u32[]{:S(2)}) async-start(bf16[4,512,1,128]{1,3,2,0:T(8,128)(2,1)} %pad_maximum_fusion.5), calls=%async_computation.3 | async-start | bytes 1048576 | tf_op jit(solution)/shard_map/all_to_all | solution.py:150
  354.8 39.8 %copy-start.68 = (bf16[512,512]{0,1:T(8,128)(2,1)}, bf16[512,512]{0,1:T(8,128)(2,1)S(1)}, u32[]{:S(2)}) copy-start(bf16[512,512]{0,1:T(8,128)(2,1)S(1)} %get-tuple-element.128) | copy-start | bytes 1572868
  415.5 17.7 %all-to-all-start.6 = ((bf16[1,512,4,128]{1,3,0,2:T(8,128)(2,1)}), bf16[1,512,4,128]{1,3,0,2:T(8,128)(2,1)}, u32[]{:S(2)}, u32[]{:S(2)}) async-start(bf16[1,512,4,128]{1,3,0,2:T(8,128)(2,1)} %bitcast.516), calls=%async_computation.6 | async-start | bytes 1048576 | tf_op jit(solution)/shard_map/all_to_all | solution.py:146
  419.6 167.4 %reduce-scatter.7.cloned.1.call-start = ((), (), s32[]{:S(2)}) async-start(), calls=%async_computation.16 | async-start | bytes 1310720 | tf_op jit(solution)/shard_map/reduce_scatter | solution.py:220
  446.4 17.4 %all-to-all-start.7 = ((bf16[4,512,1,128]{1,3,2,0:T(8,128)(2,1)}), bf16[4,512,1,128]{1,3,2,0:T(8,128)(2,1)S(1)}, u32[]{:S(2)}, u32[]{:S(2)}) async-start(bf16[4,512,1,128]{1,3,2,0:T(8,128)(2,1)} %pad_maximum_fusion.7), calls=%async_computation.7 | async-start | bytes 1048576 | tf_op jit(solution)/shard_map/all_to_all | solution.py:150
  449.9 137.2 %reduce-scatter.13.cloned.1.call-start = ((), (), s32[]{:S(2)}) async-start(), calls=%async_computation.20 | async-start | bytes 2621440
  473.9 122.5 %reduce-scatter.11.cloned.1.call-start = ((), (), s32[]{:S(2)}) async-start(), calls=%async_computation.19 | async-start | bytes 5242880 | tf_op jit(solution)/shard_map/reduce_scatter | solution.py:222
  482.7 193.4 %reduce-scatter.9.cloned.1.call-start = ((), (), s32[]{:S(2)}) async-start(), calls=%async_computation.18 | async-start | bytes 5242880 | tf_op jit(solution)/shard_map/reduce_scatter | solution.py:221
  490.7 307.6 %all-reduce.17.cloned.1.call-start = ((), (), s32[]{:S(2)}) async-start(), calls=%async_computation.17 | async-start | bytes 393216 | tf_op jit(solution)/shard_map/psum | solution.py:223
  (106 other events, 549.4 us)
Sparse Core Ops, SparseCore 0:
  10.2 48.9 all-gather.4
  60.7 36.1 all-gather.6
  98.5 90.9 all-gather.8
  190.9 80.0 all-gather.10
  424.6 28.4 reduce-scatter.6
  474.0 42.9 reduce-scatter.12
  519.3 77.1 reduce-scatter.10
  598.9 77.1 reduce-scatter.8
  679.7 54.7 all-reduce.16

commit v2 on v1

--- a/solution.py
+++ b/solution.py
@@ -4,12 +4,501 @@
 import jax.numpy as jnp
 import numpy as np
 from jax import lax
+from jax.experimental import pallas as pl
+from jax.experimental.pallas import tpu as pltpu
 from jax.sharding import PartitionSpec as P
 
 DECAY_RATE = 0.5
 EPSILON = 1e-05
 BF = jnp.bfloat16
 F32 = jnp.float32
+GROUP = 8
+MESH = pl.DeviceIdType.MESH
+VMEM = pl.BlockSpec(memory_space=pltpu.VMEM)
+ANY = pl.BlockSpec(memory_space=pl.ANY)
+GELU_A = float(np.sqrt(2.0 / np.pi))
+GELU_B = 0.044715
+
+
+def dot(a, b):
+    return jnp.dot(a, b, preferred_element_type=F32)
+
+
+def dot_nt(a, b):
+    return lax.dot_general(a, b, (((1,), (1,)), ((), ())), preferred_element_type=F32)
+
+
+def dot_tn(a, b):
+    return lax.dot_general(a, b, (((0,), (0,)), ((), ())), preferred_element_type=F32)
+
+
+def gelu(u):
+    return 0.5 * u * (1.0 + jnp.tanh(GELU_A * (u + GELU_B * (u * u * u))))
+
+
+def gelu_both(u):
+    square = u * u
+    t = jnp.tanh(GELU_A * (u + GELU_B * (square * u)))
+    half = 0.5 * (1.0 + t)
+    slope = half + (0.5 * u) * (1.0 - t * t) * (GELU_A + (3.0 * GELU_A * GELU_B) * square)
+    return u * half, slope
+
+
+def loop(count, body):
+    lax.fori_loop(0, count, lambda j, c: (body(j), c)[1], 0)
+
+
+def rows_of(j, size):
+    return pl.ds(pl.multiple_of(j * size, size), size)
+
+
+def transform_table(quarter):
+    freq = np.arange(quarter)[:, None] + 0.5
+    angle = np.pi * freq * np.arange(quarter)[None, :] / quarter
+    return np.concatenate([np.cos(angle), -np.sin(angle)], axis=0)
+
+
+def spread_matrix(scales, taps):
+    lags = []
+    for level in range(scales):
+        lags += [level * taps + j for j in range(taps) for _ in range(2 ** max(level, 1))]
+    spread = np.zeros((len(lags), scales * taps))
+    spread[np.arange(len(lags)), lags] = 1.0
+    return spread
+
+
+def tap_tables(quarter, scales, taps):
+    table = transform_table(quarter)
+    spread = spread_matrix(scales, taps).reshape(4, quarter, scales * taps)
+    return np.einsum("fp,mpt->mft", table, spread)
+
+
+def tap_scales(scales, taps, channels):
+    level = np.repeat(np.arange(scales), taps)
+    decay = DECAY_RATE**level
+    repeats = 2.0 ** np.maximum(level, 1)
+    both = np.stack([decay, repeats])[:, :, None]
+    return np.broadcast_to(both, (2, scales * taps, channels)).astype(np.float32)
+
+
+def doc_masks(segments, channels):
+    quarter = segments.shape[1] // 4
+    seg = segments.reshape(4, quarter)
+    long_doc = seg[1, 0]
+    rows = [seg[n] == long_doc for n in range(4)]
+    for k in range(3):
+        doc = k + (k >= long_doc).astype(jnp.int32)
+        rows += [seg[0] == doc, seg[3] == doc]
+    stacked = jnp.stack(rows).astype(BF)
+    return jnp.broadcast_to(stacked[:, :, None], (10, quarter, channels))
+
+
+class Place:
+    def __init__(self, n):
+        self.n = n
+        self.q = lax.axis_index("mp")
+        dp = lax.axis_index("dp")
+        self.i = lax.rem(dp, GROUP)
+        self.base = dp - self.i
+        self.core = lax.rem(self.i, 2)
+        self.chip = self.i // 2
+
+    def column(self, k):
+        q = lax.rem(self.q + k, self.n)
+        return q, {"dp": self.base + self.i, "mp": q}
+
+    def mate(self, k):
+        i = lax.rem(self.chip + k, GROUP // 2) * 2 + self.core
+        return i, {"dp": self.base + i, "mp": self.q}
+
+    def sibling(self):
+        return {"dp": self.base + self.chip * 2 + (1 - self.core), "mp": self.q}
+
+    def peers(self):
+        others = [self.column(k)[1] for k in range(1, self.n)]
+        others += [self.mate(k)[1] for k in range(1, GROUP // 2)]
+        return others + [self.sibling()]
+
+
+def greet(place):
+    barrier = pltpu.get_barrier_semaphore()
+    peers = place.peers()
+    for peer in peers:
+        pl.semaphore_signal(barrier, inc=1, device_id=peer, device_id_type=MESH)
+    pl.semaphore_wait(barrier, len(peers))
+
+
+def send(src, dst, send_sem, recv_sem, peer):
+    pltpu.make_async_remote_copy(
+        src_ref=src, dst_ref=dst, send_sem=send_sem, recv_sem=recv_sem, device_id=peer, device_id_type=MESH
+    ).start()
+
+
+def await_bytes(ref, sem):
+    pltpu.make_async_copy(ref, ref, sem).wait()
+
+
+class Weight:
+    def __init__(self, whole, layer, kind, n):
+        self.whole, self.kind, self.layer, self.n = whole, kind, layer, n
+        shape = whole.shape
+        if kind == "in":
+            self.rows, self.cols = shape[2] // GROUP, shape[3] // n
+        elif kind == "up":
+            self.rows, self.cols = shape[1] // GROUP, shape[2] // n
+        else:
+            self.rows, self.cols = shape[1] // n // GROUP, shape[2]
+
+    def piece(self, i, q):
+        r, c = self.rows, self.cols
+        if self.kind == "in":
+            return self.whole.at[self.layer, :, pl.ds(i * r, r), pl.ds(q * c, c)]
+        if self.kind == "up":
+            return self.whole.at[self.layer, pl.ds(i * r, r), pl.ds(q * c, c)]
+        return self.whole.at[self.layer, pl.ds((q * GROUP + i) * r, r), :]
+
+    def shard(self, q):
+        r, c = self.rows, self.cols
+        if self.kind == "in":
+            return self.whole.at[self.layer, :, :, pl.ds(q * c, c)]
+        if self.kind == "up":
+            return self.whole.at[self.layer, :, pl.ds(q * c, c)]
+        return self.whole.at[self.layer, pl.ds(q * GROUP * r, GROUP * r), :]
+
+    def local_piece(self, shard, i):
+        r = self.rows
+        if self.kind == "in":
+            return shard.at[self.layer, :, pl.ds(i * r, r), :]
+        return shard.at[self.layer, pl.ds(i * r, r), :]
+
+    def span(self, members):
+        r, c, k = self.rows, self.cols, self.n - 1
+        if self.kind == "in":
+            return self.whole.at[self.layer, :, pl.ds(0, members * r), pl.ds(0, k * c)]
+        if self.kind == "up":
+            return self.whole.at[self.layer, pl.ds(0, members * r), pl.ds(0, k * c)]
+        return self.whole.at[self.layer, pl.ds(0, members * k * r), :]
+
+
+class Gather:
+    def __init__(self, place, weight, shard, sems, slot):
+        self.p, self.w, self.shard_ref, self.sems, self.slot = place, weight, shard, sems, slot
+
+    def sem(self, k):
+        return self.sems.at[self.slot, k]
+
+    def own(self):
+        return pltpu.make_async_copy(
+            self.shard_ref.at[self.w.layer], self.w.shard(self.p.q), self.sem(6)
+        )
+
+    def start(self):
+        p, w = self.p, self.w
+        for k in range(1, p.n):
+            send(w.local_piece(self.shard_ref, p.i), w.piece(p.i, p.q), self.sem(0), self.sem(1), p.column(k)[1])
+        self.own().start()
+
+    def to_chips(self):
+        p, w = self.p, self.w
+        await_bytes(w.span(1), self.sem(1))
+        for k in range(1, p.n):
+            for c in range(1, GROUP // 2):
+                piece = w.piece(p.i, p.column(k)[0])
+                send(piece, piece, self.sem(2), self.sem(3), p.mate(c)[1])
+
+    def to_core(self):
+        p, w = self.p, self.w
+        await_bytes(w.span(GROUP // 2 - 1), self.sem(3))
+        for k in range(1, p.n):
+            for c in range(GROUP // 2):
+                piece = w.piece(p.mate(c)[0], p.column(k)[0])
+                send(piece, piece, self.sem(4), self.sem(5), p.sibling())
+
+    def arrive(self):
+        self.own().wait()
+        await_bytes(self.w.span(GROUP // 2), self.sem(5))
+
+    def finish(self):
+        await_bytes(self.w.span(1), self.sem(0))
+        await_bytes(self.w.span(GROUP // 2 - 1), self.sem(2))
+        await_bytes(self.w.span(GROUP // 2), self.sem(4))
+
+
+def norm_strip(v, gain, bias):
+    centred = v - jnp.mean(v, axis=-1, keepdims=True)
+    variance = jnp.mean(centred * centred, axis=-1, keepdims=True)
+    return centred * lax.rsqrt(variance + EPSILON) * gain + bias
+
+
+def norm_all(src, dst, gain, bias):
+    def strip(j):
+        r = rows_of(j, 32)
+        dst[r, :] = norm_strip(src[r, :], gain, bias).astype(BF)
+
+    loop(dst.shape[0] // 32, strip)
+
+
+def make_windows(sub_ref, scale_ref, tap_ref, spec, layer, wins):
+    raw = sub_ref[layer] * scale_ref[0]
+    total = jnp.sum(raw * raw * scale_ref[1], axis=0, keepdims=True)
+    taps = (raw * lax.rsqrt(total + EPSILON)).astype(BF)
+    channels = taps.shape[1]
+    quarter = wins.shape[3]
+    for m in range(4):
+        spec[:, m * channels : (m + 1) * channels] = dot(tap_ref[m], taps)
+
+    def strip(j):
+        r = rows_of(j, 16)
+        s = rows_of(j + quarter // 16, 16)
+        sign = (1 - 2 * lax.rem(lax.broadcasted_iota(jnp.int32, (16, channels), 0), 2)).astype(F32)
+        for m in range(4):
+            here = slice(m * channels, (m + 1) * channels)
+            re, im = spec[r, here], spec[s, here]
+            if m:
+                before = slice((m - 1) * channels, m * channels)
+                re, im = re - sign * spec[s, before], im + sign * spec[r, before]
+            wins[layer, m, 0, r, :] = re
+            wins[layer, m, 1, r, :] = im
+
+    loop(quarter // 16, strip)
+
+
+def spread_blocks(blocks, layer, masks, out):
+    channels = masks.shape[2]
+    for n in range(4):
+        out[:, n * channels : (n + 1) * channels] = blocks[layer, n] * masks[n]
+    for k in range(3):
+        out[:, (4 + k) * channels : (5 + k) * channels] = (
+            blocks[layer, 0] * masks[4 + 2 * k] + blocks[layer, 3] * masks[5 + 2 * k]
+        )
+
+
+def join_blocks(parts, r, masks, n):
+    channels = masks.shape[2]
+    total = parts[:, n * channels : (n + 1) * channels] * masks[n, r, :].astype(F32)
+    if n in (0, 3):
+        for k in range(3):
+            mask = masks[4 + 2 * k + (n == 3), r, :].astype(F32)
+            total += parts[:, (4 + k) * channels : (5 + k) * channels] * mask
+    return total
+
+
+def fwd_products(spec, wins, layer, out, channels):
+    quarter = wins.shape[3]
+
+    def strip(j):
+        r = rows_of(j, 16)
+        s = rows_of(j + quarter // 16, 16)
+        xs = [(spec[r, n * channels : (n + 1) * channels], spec[s, n * channels : (n + 1) * channels]) for n in range(7)]
+        ws = [(wins[layer, m, 0, r, :], wins[layer, m, 1, r, :]) for m in range(4)]
+        for n in range(7):
+            re = im = None
+            for m in range(n + 1 if n < 4 else 1):
+                w, x = ws[m], xs[n - m]
+                a = w[0] * x[0] - w[1] * x[1]
+                b = w[0] * x[1] + w[1] * x[0]
+                re, im = (a, b) if re is None else (re + a, im + b)
+            out[r, n * channels : (n + 1) * channels] = re.astype(BF)
+            out[s, n * channels : (n + 1) * channels] = im.astype(BF)
+
+    loop(quarter // 16, strip)
+
+
+def forward_kernel(
+    n, layers,
+    stream_in, masks, gains, biases, subs, scales, table, table_t, tap_table, win, wout, wup, wdn,
+    out_stream, streams_o, gate_o, conv_in_o, conv_out_o, middle_o, win_o, wout_o, wup_o, wdn_o,
+    stream, hidden, gate, middle, send_a, recv_a, send_b, recv_b,
+    spread, spec, spec_y, wins, gated, up, active, win_f, wout_f, wup_f, wdn_f,
+    gather_sems, a2a_sems, save_sems,
+):
+    place = Place(n)
+    me = place.q
+    tokens, width = stream_in.shape
+    channels = width // n
+    quarter = tokens
+    greet(place)
+    gathers = []
+    for l in range(layers):
+        for kind, whole, shard in (("in", win_f, win), ("out", wout_f, wout), ("up", wup_f, wup), ("down", wdn_f, wdn)):
+            slot = len(gathers)
+            gathers.append(Gather(place, Weight(whole, l, kind, n), shard, gather_sems, slot))
+    saves = []
+
+    def save(src, dst):
+        copy = pltpu.make_async_copy(src, dst, save_sems.at[len(saves)])
+        copy.start()
+        saves.append(copy)
+
+    def exchange_start(slot, src, dst, layer):
+        for k in range(1, n):
+            q, peer = place.column(k)
+            send(src.at[layer, q], dst.at[layer, me], a2a_sems.at[slot, 0], a2a_sems.at[slot, 1], peer)
+
+    def exchange_wait(slot, src, dst, layer):
+        await_bytes(src.at[layer, pl.ds(0, n - 1)], a2a_sems.at[slot, 0])
+        await_bytes(dst.at[layer, pl.ds(0, n - 1)], a2a_sems.at[slot, 1])
+
+    for g in gathers[:4]:
+        g.start()
+    norm_all(stream_in, hidden, gains[0, 0], biases[0, 0])
+    gathers[0].to_chips()
+    for l in range(layers):
+        make_windows(subs, scales, tap_table, spec, l, wins)
+    gathers[0].to_core()
+    gathers[0].arrive()
+
+    for l in range(layers):
+        here = stream_in if l == 0 else stream.at[l - 1]
+        rest = gathers[4 * l + 1 : 4 * l + 4]
+        if l:
+            norm_all(here, hidden, gains[l, 0], biases[l, 0])
+            gathers[4 * l].to_core()
+            gathers[4 * l].arrive()
+
+        def project(j):
+            r = rows_of(j, 256)
+            got = dot(hidden[r, :], win_f[l, 0]).astype(BF)
+            for q in range(n):
+                send_a[l, q, r, :] = got[:, q * channels : (q + 1) * channels]
+
+        loop(tokens // 256, project)
+        exchange_start(2 * l, send_a, recv_a, l)
+        recv_a[l, me] = send_a[l, me]
+        for g in rest:
+            g.to_chips()
+
+        def project_gate(j):
+            r = rows_of(j, 256)
+            gate[l, r, :] = dot(hidden[r, :], win_f[l, 1])
+
+        loop(tokens // 256, project_gate)
+        save(gate.at[l], gate_o.at[l])
+        for g in rest:
+            g.to_core()
+        exchange_wait(2 * l, send_a, recv_a, l)
+        save(recv_a.at[l], conv_in_o.at[l])
+        spread_blocks(recv_a, l, masks, spread)
+
+        def transform(j):
+            r = rows_of(j, 256)
+            spec[r, :] = dot(table[r, :], spread[...])
+
+        loop(2 * quarter // 256, transform)
+        fwd_products(spec, wins, l, spec_y, channels)
+
+        def untransform(j):
+            r = rows_of(j, 128)
+            parts = dot(table_t[r, :], spec_y[...])
+            for q in range(n):
+                send_b[l, q, r, :] = join_blocks(parts, r, masks, q).astype(BF)
+
+        loop(quarter // 128, untransform)
+        exchange_start(2 * l + 1, send_b, recv_b, l)
+        recv_b[l, me] = send_b[l, me]
+        for g in rest:
+            g.arrive()
+        if l + 1 < layers:
+            for g in gathers[4 * l + 4 : 4 * l + 8]:
+                g.start()
+        exchange_wait(2 * l + 1, send_b, recv_b, l)
+        save(recv_b.at[l], conv_out_o.at[l])
+
+        def mix(j):
+            r = rows_of(j, 16)
+            for q in range(n):
+                c = slice(q * channels, (q + 1) * channels)
+                gated[r, c] = (gelu(gate[l, r, c]) * recv_b[l, q, r, :].astype(F32)).astype(BF)
+
+        loop(tokens // 16, mix)
+
+        def attach(j):
+            r = rows_of(j, 256)
+            middle[l, r, :] = here[r, :] + dot(gated[r, :], wout_f[l])
+
+        loop(tokens // 256, attach)
+        save(middle.at[l], middle_o.at[l])
+        norm_all(middle.at[l], hidden, gains[l, 1], biases[l, 1])
+        if l + 1 < layers:
+            gathers[4 * l + 4].to_chips()
+
+        def widen(j):
+            r = rows_of(j, 256)
+            up[r, :] = dot(hidden[r, :], wup_f[l])
+
+        loop(tokens // 256, widen)
+
+        def activate(j):
+            r = rows_of(j, 8)
+            active[r, :] = gelu(up[r, :]).astype(BF)
+
+        def activate16(j):
+            r = rows_of(j, 16)
+            active[r, :] = gelu(up[r, :]).astype(BF)
+
+        loop(tokens // 16, activate16)
+
+        def narrow(j):
+            r = rows_of(j, 256)
+            stream[l, r, :] = middle[l, r, :] + dot(active[r, :], wdn_f[l])
+
+        loop(tokens // 256, narrow)
+        save(stream.at[l], out_stream if l + 1 == layers else streams_o.at[l])
+    for src, dst in ((win_f, win_o), (wout_f, wout_o), (wup_f, wup_o), (wdn_f, wdn_o)):
+        save(src, dst)
+    for g in gathers:
+        g.finish()
+    for copy in saves:
+        copy.wait()
+
+
+def forward(n, stream_in, masks, gains, biases, subs, scales, table, table_t, tap_table, win, wout, wup, wdn):
+    layers = win.shape[0]
+    tokens, width = stream_in.shape
+    channels = width // n
+    ff = wup.shape[2] * n
+    length_freq = 2 * tokens
+
+    def sds(*shape, dtype=BF):
+        return jax.ShapeDtypeStruct(shape, dtype)
+
+    wshapes = [(layers, 2, width, width), (layers, width, width), (layers, width, ff), (layers, ff, width)]
+    outs = [
+        sds(tokens, width, dtype=F32),
+        sds(max(layers - 1, 1), tokens, width, dtype=F32),
+        sds(layers, tokens, width, dtype=F32),
+        sds(layers, n, tokens, channels),
+        sds(layers, n, tokens, channels),
+        sds(layers, tokens, width, dtype=F32),
+    ] + [sds(*s) for s in wshapes]
+    a2a = pltpu.VMEM((layers, n, tokens, channels), BF)
+    scratch = [
+        pltpu.VMEM((layers, tokens, width), F32),
+        pltpu.VMEM((tokens, width), BF),
+        pltpu.VMEM((layers, tokens, width), F32),
+        pltpu.VMEM((layers, tokens, width), F32),
+        a2a, a2a, a2a, a2a,
+        pltpu.VMEM((tokens, 7 * channels), BF),
+        pltpu.VMEM((length_freq, 7 * channels), F32),
+        pltpu.VMEM((length_freq, 7 * channels), BF),
+        pltpu.VMEM((layers, 4, 2, tokens, channels), F32),
+        pltpu.VMEM((tokens, width), BF),
+        pltpu.VMEM((tokens, ff), F32),
+        pltpu.VMEM((tokens, ff), BF),
+    ] + [pltpu.VMEM(s, BF) for s in wshapes] + [
+        pltpu.SemaphoreType.DMA((4 * layers, 7)),
+        pltpu.SemaphoreType.DMA((2 * layers, 2)),
+        pltpu.SemaphoreType.DMA((5 * layers + 4,)),
+    ]
+    return pl.pallas_call(
+        functools.partial(forward_kernel, n, layers),
+        out_shape=outs,
+        in_specs=[VMEM] * 9 + [ANY] * 4,
+        out_specs=[ANY] * 10,
+        scratch_shapes=scratch,
+        compiler_params=pltpu.CompilerParams(collective_id=1, has_side_effects=True, vmem_limit_bytes=60 * 2**20),
+        name="forward",
+    )(stream_in, masks, gains, biases, subs, scales, table, table_t, tap_table, win, wout, wup, wdn)
 
 
 def norm_rows(values, gain_row, bias_row):
@@ -162,47 +651,48 @@
 def per_device(
     stream_in, segments, norm_gain, norm_bias, w_in, w_out, sub_kernels, w_up, w_down, cotangent
 ):
-    layers = w_in.shape[0]
+    layers, scales, taps_n, channels = sub_kernels.shape
+    n = lax.axis_size("mp")
     quarter = segments.shape[1] // 4
     seg = segments.reshape(4, quarter)
-    table = jnp.asarray(transform_matrix(quarter)).astype(BF)
+    table_np = transform_table(quarter)
+    table = jnp.asarray(table_np, F32).astype(BF)
     sign = jnp.asarray(1.0 - 2.0 * (np.arange(quarter)[:, None] % 2), F32)
-    w_in = lax.all_gather(w_in, "mp", axis=3, tiled=True)
-    w_out = lax.all_gather(w_out, "mp", axis=1, tiled=True)
-    w_up = lax.all_gather(w_up, "mp", axis=2, tiled=True)
-    w_down = lax.all_gather(w_down, "mp", axis=1, tiled=True)
-    stream = stream_in
+    masks = doc_masks(segments, channels)
+    tap_table = jnp.asarray(tap_tables(quarter, scales, taps_n) / quarter, F32).astype(BF)
+    consts = jnp.asarray(tap_scales(scales, taps_n, channels))
+    out, streams, gate_all, conv_in, conv_out, middle_all, w_in_f, w_out_f, w_up_f, w_down_f = forward(
+        n, stream_in, masks, norm_gain[:, :, None], norm_bias[:, :, None], sub_kernels.reshape(layers, -1, channels), consts,
+        table, table.T, tap_table, w_in.transpose(0, 2, 1, 3), w_out, w_up, w_down)
     kept = []
     for l in range(layers):
-        hidden = norm_rows(stream, norm_gain[l, 0], norm_bias[l, 0]).astype(BF)
-        conv_input = jnp.dot(hidden, w_in[l, :, 0], preferred_element_type=F32).astype(BF)
-        gate_pre = jnp.dot(hidden, w_in[l, :, 1], preferred_element_type=F32)
+        layer_in = stream_in if l == 0 else streams[l - 1]
+        hidden = norm_rows(layer_in, norm_gain[l, 0], norm_bias[l, 0]).astype(BF)
+        convolved = conv_out[l].transpose(1, 0, 2).reshape(quarter, -1).astype(F32)
+        gate_pre = gate_all[l]
+        gated = (jax.nn.gelu(gate_pre) * convolved).astype(BF)
+        middle = middle_all[l]
+        hidden_mid = norm_rows(middle, norm_gain[l, 1], norm_bias[l, 1]).astype(BF)
+        up_pre = jnp.dot(hidden_mid, w_up_f[l], preferred_element_type=F32)
+        active = jax.nn.gelu(up_pre).astype(BF)
         kernel = build_kernel(sub_kernels[l]).astype(BF)
-        convolved, x = conv(to_channels(conv_input), kernel, seg, table, sign)
-        convolved = to_tokens(convolved.astype(BF)).astype(F32)
-        gated = (jax.nn.gelu(gate_pre) * convolved).astype(BF)
-        middle = stream + jnp.dot(gated, w_out[l], preferred_element_type=F32)
-        hidden_mid = norm_rows(middle, norm_gain[l, 1], norm_bias[l, 1]).astype(BF)
-        up_pre = jnp.dot(hidden_mid, w_up[l], preferred_element_type=F32)
-        active = jax.nn.gelu(up_pre).astype(BF)
-        out = middle + jnp.dot(active, w_down[l], preferred_element_type=F32)
-        kept.append((stream, hidden, gate_pre, kernel, x, convolved, gated, middle, hidden_mid, up_pre, active))
-        stream = out
+        x = spectrum(split_docs(conv_in[l], seg), table)
+        kept.append((layer_in, hidden, gate_pre, kernel, x, convolved, gated, middle, hidden_mid, up_pre, active))
     grad = cotangent
     collected = []
     for l in reversed(range(layers)):
         layer_in, hidden, gate_pre, kernel, x, convolved, gated, middle, hidden_mid, up_pre, active = kept[l]
         branch_grad = grad.astype(BF)
         g_down = dot_tn(active, branch_grad)
-        up_grad = jax.vjp(jax.nn.gelu, up_pre)[1](dot_nt(branch_grad, w_down[l]))[0].astype(BF)
+        up_grad = jax.vjp(jax.nn.gelu, up_pre)[1](dot_nt(branch_grad, w_down_f[l]))[0].astype(BF)
         g_up = dot_tn(hidden_mid, up_grad)
-        hidden_grad = dot_nt(up_grad, w_up[l])
+        hidden_grad = dot_nt(up_grad, w_up_f[l])
         pull = jax.vjp(norm_rows, middle, norm_gain[l, 1], norm_bias[l, 1])[1]
         norm_grad, gain1, bias1 = pull(hidden_grad)
         middle_grad = grad + norm_grad
         out_grad = middle_grad.astype(BF)
         g_out = dot_tn(gated, out_grad)
-        gated_grad = dot_nt(out_grad, w_out[l])
+        gated_grad = dot_nt(out_grad, w_out_f[l])
         act, gate_pull = jax.vjp(jax.nn.gelu, gate_pre)
         conv_grad = (gated_grad * act).astype(BF)
         gate_grad = gate_pull(gated_grad * convolved)[0].astype(BF)
@@ -210,7 +700,7 @@
         input_grad = to_tokens(input_grad.astype(BF))
         g_sub = jax.vjp(build_kernel, sub_kernels[l])[1](taps)[0]
         g_in = jnp.stack([dot_tn(hidden, input_grad), dot_tn(hidden, gate_grad)], axis=1)
-        hidden_grad = dot_nt(input_grad, w_in[l, :, 0]) + dot_nt(gate_grad, w_in[l, :, 1])
+        hidden_grad = dot_nt(input_grad, w_in_f[l, 0]) + dot_nt(gate_grad, w_in_f[l, 1])
         pull = jax.vjp(norm_rows, layer_in, norm_gain[l, 0], norm_bias[l, 0])[1]
         norm_grad, gain0, bias0 = pull(hidden_grad)
         grad = middle_grad + norm_grad
@@ -224,7 +714,7 @@
         (g_in.astype(F32), g_out.astype(F32), g_sub, g_up.astype(F32), g_down.astype(F32)), "dp"
     )
     gain, bias = lax.psum((gain, bias), ("dp", "mp"))
-    return stream, grad, gain, bias, g_in, g_out, g_sub, g_up, g_down
+    return out, grad, gain, bias, g_in, g_out, g_sub, g_up, g_down
 
 
 def solution(mesh):

time: 815 us -> 687 us (0.84)
  waiting for transfers between devices: 339 us -> 136 us
  Pallas kernels: 0 us -> 131 us
  blocking collectives: 197 us -> 159 us
  matrix products: 88.4 us -> 70.8 us
  local copies, waits for them, and re-layouts: 50.9 us -> 64.1 us
  other arithmetic: 87.3 us -> 76.8 us
    all_gather x4 -> x0, waiting for transfers between devices: 163 us -> none  [the longest x1 76.1 us: per_device(): w_down = lax.all_gather(w_down, 'mp', axis=1, tiled=True)]
    pallas_call x0 -> x1, Pallas kernels: none -> 131 us  [forward(): pl.pallas_call(functools.partial(forward_kernel, n, layers), out_shape=ou...]
    all_to_all x2 -> x0, blocking collectives: 33.2 us -> none  [the longest x1 16.7 us: to_tokens(): got = lax.all_to_all(blocks, 'mp', 0, 1)]
    all_to_all x3 -> x2, waiting for transfers between devices: 45.6 us -> 14.8 us  [to_tokens(): got = lax.all_to_all(blocks, 'mp', 0, 1)]
    all_to_all x3 -> x2, waiting for transfers between devices: 41.2 us -> 13.8 us  [to_channels(): return lax.all_to_all(rows.reshape(rows.shape[0], n, -1), 'mp', 1, 0)]
    dot_general x10 -> x2, matrix products: 31 us -> 8.87 us  [per_device(): up_pre = jnp.dot(hidden_mid, w_up_f[l], preferred_element_type=F32)]
    reduce_scatter x1, waiting for transfers between devices: 7.43 us -> 27.4 us  [per_device(): lax.psum_scatter(g_down.astype(BF), 'mp', scatter_dimension=1, tiled=True)]
    convert_element_type x0 -> x6, local copies, waits for them, and re-layouts: none -> 8.31 us  [the longest x4 5.95 us: per_device(): convolved = conv_out[l].transpose(1, 0, 2).reshape(quarter, -1).astype(F32)]
  transfers between devices with their start and end apart: 15 -> 9, of which waited for: 11 -> 6; matrix products, arithmetic and copies ran while one was open for 18% -> 19% of each run, Pallas kernels for 0% -> 0%
where the time goes in v2:
time: 687 us; the launch traced here: 677 us
  blocking collectives  159 us (23%)
  waiting for transfers between devices  136 us (20%)
  Pallas kernels  131 us (19%)
  other arithmetic  76.8 us (11%)
  matrix products  70.8 us (10%)
  local copies, waits for them, and re-layouts  64.1 us (9%)
  starting transfers between devices  20 us (3%)
  between operations  19.6 us (3%)
    pallas_call x1, Pallas kernels, forward(): pl.pallas_call(functools.partial(forward_kernel, n, layers), out_shape=ou...  131 us
    psum x1, blocking collectives, per_device(): lax.psum((g_in.astype(F32), g_out.astype(F32), g_sub, g_up.astype(F32), g...  118 us
    reduce_scatter x1, waiting for transfers between devices, per_device(): lax.psum_scatter(g_up.astype(BF), 'mp', scatter_dimension=2, tiled=True)  79.6 us
    psum x1, blocking collectives, per_device(): gain, bias = lax.psum((gain, bias), ('dp', 'mp'))  40.9 us
    unnamed x252, local copies, waits for them, and re-layouts  31.8 us
    reduce_scatter x1, waiting for transfers between devices, per_device(): lax.psum_scatter(g_down.astype(BF), 'mp', scatter_dimension=1, tiled=True)  27.4 us
    dot_general x10, matrix products, dot_nt(): lax.dot_general(a, b, (((1,), (1,)), ((), ())), preferred_element_type=F32)  23.6 us
    unnamed x31, other arithmetic  23.6 us
  transfers between devices with their start and end apart: 9, of which 6 were waited for; matrix products, arithmetic and copies ran while one was open for 19% of the time, Pallas kernels for 0%

profile of v2, /device:TPU:0, one launch (start us, length us, event | category | flops | bytes accessed | tf_op | source)
XLA Modules:
  0.0 676.7 jit_solution(15382343891552578754)
XLA Ops:
  22.9 130.6 %forward.1 = (f32[512,512]{1,0:T(8,128)}, f32[1,512,512]{2,1,0:T(8,128)}, f32[2,512,512]{2,1,0:T(8,128)}, bf16[2,4,512,128]{3,2,1,0:T(8,128)(2,1)}, bf16[2,4,512...) custom-call(f32[512,512]{1,0:T(8,128)} %stream_in.1, ...), custom_call_target="tpu_custom_call" | custom-call | tf_op jit(solution)/shard_map/forward/pallas_call | solution.py:493
  161.4 3.4 fusion.29
  164.9 3.9 fusion.6
  176.4 6.3 all-to-all-start
  189.4 8.1 %all-to-all-done = bf16[1,512,4,128]{3,1,0,2:T(8,128)(2,1)} async-done(((bf16[1,512,4,128]{3,1,0,2:T(8,128)(2,1)}), bf16[1,512,4,128]{3,1,0,2:T(8,128)(2,1)}, u32[]{:S(2)}, u32[]{:S(2)}) %all-to-all-start) | async-done | bytes 524320 | tf_op jit(solution)/shard_map/all_to_all | solution.py:635
  215.9 4.3 all-to-all-start.1
  221.1 5.4 fusion.23
  226.6 8.3 %all-to-all-done.1 = bf16[4,512,1,128]{3,1,2,0:T(8,128)(2,1)} async-done(((bf16[4,512,1,128]{3,1,2,0:T(8,128)(2,1)}), bf16[4,512,1,128]{3,1,2,0:T(8,128)(2,1)}, u32[]{:S(2)}, u32[]{:S(2)}) %all-to-all-start.1) | async-done | bytes 524320 | tf_op jit(solution)/shard_map/all_to_all | solution.py:639
  238.6 2.7 multiply_reduce_fusion.3
  243.6 3.7 fusion.13
  258.2 4.1 all-to-all-start.2
  265.0 2.7 fusion.67
  270.7 5.7 all-to-all-done.2
  310.1 4.1 all-to-all-start.3
  321.8 6.6 all-to-all-done.3
  334.9 6.2 copy.150
  341.0 4.5 reshape.2526
  345.8 4.3 fusion.20
  354.7 3.6 fusion.18
  374.2 4.1 add_convert_fusion.12
  396.6 40.9 %all-reduce.12 = (f32[2,2,512]{2,1,0:T(2,128)}, f32[2,2,512]{2,1,0:T(2,128)}) all-reduce(f32[2,2,512]{2,1,0:T(2,128)S(1)} %pad_maximum_fusion.7, f32[2,2,512]{2,1,0:T(2,128)S(1)} %pad_maximum_fusion.8), channel_id=1, replica_groups=mesh['dp'=8,'mp'=4] {'dp','mp'}, use_global_device_ids=true, to_apply=%region_22.23 | all-reduce | flops 4096 | bytes 32768 | tf_op jit(solution)/shard_map/psum | solution.py:716
  439.6 27.4 %reduce-scatter.11.cloned.1.call-done = bf16[2,512,512]{2,1,0:T(8,128)(2,1)} async-done(((bf16[2,2048,512]{2,1,0:T(8,128)(2,1)}), bf16[2,512,512]{2,1,0:T(8,128)(2,1)}) %reduce-scatter.11.cloned.1.call-update) | async-done | bytes 1048592 | tf_op jit(solution)/shard_map/reduce_scatter | solution.py:712
  466.9 79.6 %reduce-scatter.9.cloned.1.call-done = bf16[2,512,512]{2,1,0:T(8,128)(2,1)} async-done(((bf16[2,512,2048]{2,1,0:T(8,128)(2,1)}), bf16[2,512,512]{2,1,0:T(8,128)(2,1)}) %reduce-scatter.9.cloned.1.call-update) | async-done | bytes 1048592 | tf_op jit(solution)/shard_map/reduce_scatter | solution.py:711
  546.5 118.3 %all-reduce.18 = (f32[2,512,2,128]{3,1,2,0:T(8,128)S(1)}, f32[2,128,512]{2,1,0:T(8,128)}, f32[2,512,512]{2,1,0:T(8,128)}, f32[2,512,512]{2,1,0:T(8,128)}) all-reduce(bf16[2,512,2,128]{3,1,2,0:T(8,128)(2,1)S(1)} %copy.151, bf16[2,128,512]{2,1,0:T(8,128)(2,1)} %reduce-scatter.7.cloned.1.call-done, ...), channel_id=1, replica_groups=mesh['dp'=8,'mp'=4] {'dp'}, use_global_device_ids=true, to_apply=%region_29.30 | all-reduce | flops 1441792 | bytes 8650752 | tf_op jit(solution)/shard_map/psum | solution.py:713
  (441 shorter events, 168.5 us)
Async XLA Ops:
  10.7 160.4 %copy-start.66 = (f32[1,1,512]{2,1,0:T(1,128)}, f32[1,1,512]{2,1,0:T(1,128)S(1)}, u32[]{:S(2)}) copy-start(f32[1,1,512]{2,1,0:T(1,128)S(1)} %get-tuple-element.201) | copy-start | bytes 6148
  10.7 230.7 %copy-start.72 = (f32[1,1,512]{2,1,0:T(1,128)}, f32[1,1,512]{2,1,0:T(1,128)S(1)}, u32[]{:S(2)}) copy-start(f32[1,1,512]{2,1,0:T(1,128)S(1)} %get-tuple-element.200) | copy-start | bytes 6148
  10.7 238.7 %copy-start.64 = (f32[1,1,512]{2,1,0:T(1,128)}, f32[1,1,512]{2,1,0:T(1,128)S(1)}, u32[]{:S(2)}) copy-start(f32[1,1,512]{2,1,0:T(1,128)S(1)} %get-tuple-element.202) | copy-start | bytes 6148
  13.3 207.8 %copy-start.73 = (f32[1,1,512]{2,1,0:T(1,128)}, f32[1,1,512]{2,1,0:T(1,128)S(1)}, u32[]{:S(2)}) copy-start(f32[1,1,512]{2,1,0:T(1,128)S(1)} %get-tuple-element.196) | copy-start | bytes 6148
  19.2 257.3 %copy-start.93 = (pred[512]{0:T(512)(128)(4,1)}, pred[512]{0:T(512)(128)(4,1)S(1)}, u32[]{:S(2)}) copy-start(pred[512]{0:T(512)(128)(4,1)S(1)} %get-tuple-element.213) | copy-start | bytes 1540
  19.2 258.4 %copy-start.91 = (pred[512]{0:T(512)(128)(4,1)}, pred[512]{0:T(512)(128)(4,1)S(1)}, u32[]{:S(2)}) copy-start(pred[512]{0:T(512)(128)(4,1)S(1)} %get-tuple-element.211) | copy-start | bytes 1540
  19.2 259.5 %copy-start.77 = (pred[512]{0:T(512)(128)(4,1)}, pred[512]{0:T(512)(128)(4,1)S(1)}, u32[]{:S(2)}) copy-start(pred[512]{0:T(512)(128)(4,1)S(1)} %get-tuple-element.217) | copy-start | bytes 1540
  19.2 260.6 %copy-start.95 = (pred[512]{0:T(512)(128)(4,1)}, pred[512]{0:T(512)(128)(4,1)S(1)}, u32[]{:S(2)}) copy-start(pred[512]{0:T(512)(128)(4,1)S(1)} %get-tuple-element.215) | copy-start | bytes 1540
  19.2 262.5 %copy-start.81 = (pred[512]{0:T(512)(128)(4,1)}, pred[512]{0:T(512)(128)(4,1)S(1)}, u32[]{:S(2)}) copy-start(pred[512]{0:T(512)(128)(4,1)S(1)} %get-tuple-element.203) | copy-start | bytes 1540
  19.2 262.5 %copy-start.85 = (pred[512]{0:T(512)(128)(4,1)}, pred[512]{0:T(512)(128)(4,1)S(1)}, u32[]{:S(2)}) copy-start(pred[512]{0:T(512)(128)(4,1)S(1)} %get-tuple-element.207) | copy-start | bytes 1540
  19.2 264.7 %copy-start.83 = (pred[512]{0:T(512)(128)(4,1)}, pred[512]{0:T(512)(128)(4,1)S(1)}, u32[]{:S(2)}) copy-start(pred[512]{0:T(512)(128)(4,1)S(1)} %get-tuple-element.205) | copy-start | bytes 1540
  19.2 264.7 %copy-start.87 = (pred[512]{0:T(512)(128)(4,1)}, pred[512]{0:T(512)(128)(4,1)S(1)}, u32[]{:S(2)}) copy-start(pred[512]{0:T(512)(128)(4,1)S(1)} %get-tuple-element.209) | copy-start | bytes 1540
  19.2 266.9 %copy-start.79 = (pred[512]{0:T(512)(128)(4,1)}, pred[512]{0:T(512)(128)(4,1)S(1)}, u32[]{:S(2)}) copy-start(pred[512]{0:T(512)(128)(4,1)S(1)} %get-tuple-element.109) | copy-start | bytes 1540
  19.2 266.9 %copy-start.89 = (pred[512]{0:T(512)(128)(4,1)}, pred[512]{0:T(512)(128)(4,1)S(1)}, u32[]{:S(2)}) copy-start(pred[512]{0:T(512)(128)(4,1)S(1)} %get-tuple-element.219) | copy-start | bytes 1540
  176.4 21.1 %all-to-all-start = ((bf16[1,512,4,128]{3,1,0,2:T(8,128)(2,1)}), bf16[1,512,4,128]{3,1,0,2:T(8,128)(2,1)}, u32[]{:S(2)}, u32[]{:S(2)}) async-start(bf16[1,512,4,128]{3,1,0,2:T(8,128)(2,1)} %copy.102), calls=%async_computation | async-start | bytes 1048576 | tf_op jit(solution)/shard_map/all_to_all | solution.py:635
  215.9 18.9 %all-to-all-start.1 = ((bf16[4,512,1,128]{3,1,2,0:T(8,128)(2,1)}), bf16[4,512,1,128]{3,1,2,0:T(8,128)(2,1)}, u32[]{:S(2)}, u32[]{:S(2)}) async-start(bf16[4,512,1,128]{3,1,2,0:T(8,128)(2,1)} %pad_maximum_fusion.4), calls=%async_computation.1 | async-start | bytes 1048576 | tf_op jit(solution)/shard_map/all_to_all | solution.py:639
  258.2 18.2 %all-to-all-start.2 = ((bf16[1,512,4,128]{3,1,0,2:T(8,128)(2,1)}), bf16[1,512,4,128]{3,1,0,2:T(8,128)(2,1)}, u32[]{:S(2)}, u32[]{:S(2)}) async-start(bf16[1,512,4,128]{3,1,0,2:T(8,128)(2,1)} %copy.119), calls=%async_computation.2 | async-start | bytes 1048576 | tf_op jit(solution)/shard_map/all_to_all | solution.py:635
  262.4 175.2 %reduce-scatter.7.cloned.1.call-start = ((), (), s32[]{:S(2)}) async-start(), calls=%async_computation.8 | async-start | bytes 1310720 | tf_op jit(solution)/shard_map/reduce_scatter | solution.py:710
  310.1 18.2 %all-to-all-start.3 = ((bf16[4,512,1,128]{3,1,2,0:T(8,128)(2,1)}), bf16[4,512,1,128]{3,1,2,0:T(8,128)(2,1)}, u32[]{:S(2)}, u32[]{:S(2)}) async-start(bf16[4,512,1,128]{3,1,2,0:T(8,128)(2,1)} %pad_maximum_fusion.5), calls=%async_computation.3 | async-start | bytes 1048576 | tf_op jit(solution)/shard_map/all_to_all | solution.py:639
  314.3 123.3 %reduce-scatter.13.cloned.1.call-start = ((), (), s32[]{:S(2)}) async-start(), calls=%async_computation.12 | async-start | bytes 2621440
  345.5 121.4 %reduce-scatter.11.cloned.1.call-start = ((), (), s32[]{:S(2)}) async-start(), calls=%async_computation.11 | async-start | bytes 5242880 | tf_op jit(solution)/shard_map/reduce_scatter | solution.py:712
  354.1 192.5 %reduce-scatter.9.cloned.1.call-start = ((), (), s32[]{:S(2)}) async-start(), calls=%async_computation.10 | async-start | bytes 5242880 | tf_op jit(solution)/shard_map/reduce_scatter | solution.py:711
  362.3 304.3 %all-reduce.17.cloned.1.call-start = ((), (), s32[]{:S(2)}) async-start(), calls=%async_computation.9 | async-start | bytes 393216 | tf_op jit(solution)/shard_map/psum | solution.py:713
  396.6 269.9 %copy-start.37 = (f32[512,512]{1,0:T(8,128)S(1)}, f32[512,512]{1,0:T(8,128)}, u32[]{:S(2)}) copy-start(f32[512,512]{1,0:T(8,128)} %get-tuple-element.266) | copy-start | bytes 3145732
  (102 other events, 743.2 us)
Sparse Core Ops, SparseCore 0:
  270.8 27.3 reduce-scatter.6
  345.6 41.8 reduce-scatter.12
  389.8 77.1 reduce-scatter.10
  469.2 77.2 reduce-scatter.8
Sparse Core Ops, SparseCore 1:
  391.5 51.0 all-reduce.16

commit v3 on v2

--- a/solution.py
+++ b/solution.py
@@ -114,6 +114,9 @@
     def sibling(self):
         return {"dp": self.base + self.chip * 2 + (1 - self.core), "mp": self.q}
 
+    def member(self, k):
+        return {"dp": self.base + lax.rem(self.i + k, GROUP), "mp": self.q}
+
     def peers(self):
         others = [self.column(k)[1] for k in range(1, self.n)]
         others += [self.mate(k)[1] for k in range(1, GROUP // 2)]
@@ -123,6 +126,14 @@
 def greet(place):
     barrier = pltpu.get_barrier_semaphore()
     peers = place.peers()
+    for peer in peers:
+        pl.semaphore_signal(barrier, inc=1, device_id=peer, device_id_type=MESH)
+    pl.semaphore_wait(barrier, len(peers))
+
+
+def greet_all(place):
+    barrier = pltpu.get_barrier_semaphore()
+    peers = [place.column(k)[1] for k in range(1, place.n)] + [place.member(k) for k in range(1, GROUP)]
     for peer in peers:
         pl.semaphore_signal(barrier, inc=1, device_id=peer, device_id_type=MESH)
     pl.semaphore_wait(barrier, len(peers))
@@ -263,13 +274,13 @@
     loop(quarter // 16, strip)
 
 
-def spread_blocks(blocks, layer, masks, out):
+def spread_blocks(blocks, masks, out):
     channels = masks.shape[2]
     for n in range(4):
-        out[:, n * channels : (n + 1) * channels] = blocks[layer, n] * masks[n]
+        out[:, n * channels : (n + 1) * channels] = blocks[n] * masks[n]
     for k in range(3):
         out[:, (4 + k) * channels : (5 + k) * channels] = (
-            blocks[layer, 0] * masks[4 + 2 * k] + blocks[layer, 3] * masks[5 + 2 * k]
+            blocks[0] * masks[4 + 2 * k] + blocks[3] * masks[5 + 2 * k]
         )
 
 
@@ -307,7 +318,7 @@
 def forward_kernel(
     n, layers,
     stream_in, masks, gains, biases, subs, scales, table, table_t, tap_table, win, wout, wup, wdn,
-    out_stream, streams_o, gate_o, conv_in_o, conv_out_o, middle_o, win_o, wout_o, wup_o, wdn_o,
+    out_stream, streams_o, gate_o, conv_in_o, conv_out_o, middle_o, wins_o, win_o, wout_o, wup_o, wdn_o,
     stream, hidden, gate, middle, send_a, recv_a, send_b, recv_b,
     spread, spec, spec_y, wins, gated, up, active, win_f, wout_f, wup_f, wdn_f,
     gather_sems, a2a_sems, save_sems,
@@ -378,7 +389,7 @@
             g.to_core()
         exchange_wait(2 * l, send_a, recv_a, l)
         save(recv_a.at[l], conv_in_o.at[l])
-        spread_blocks(recv_a, l, masks, spread)
+        spread_blocks(recv_a.at[l], masks, spread)
 
         def transform(j):
             r = rows_of(j, 256)
@@ -444,7 +455,7 @@
 
         loop(tokens // 256, narrow)
         save(stream.at[l], out_stream if l + 1 == layers else streams_o.at[l])
-    for src, dst in ((win_f, win_o), (wout_f, wout_o), (wup_f, wup_o), (wdn_f, wdn_o)):
+    for src, dst in ((wins, wins_o), (win_f, win_o), (wout_f, wout_o), (wup_f, wup_o), (wdn_f, wdn_o)):
         save(src, dst)
     for g in gathers:
         g.finish()
@@ -470,6 +481,7 @@
         sds(layers, n, tokens, channels),
         sds(layers, n, tokens, channels),
         sds(layers, tokens, width, dtype=F32),
+        sds(layers, 4, 2, tokens, channels, dtype=F32),
     ] + [sds(*s) for s in wshapes]
     a2a = pltpu.VMEM((layers, n, tokens, channels), BF)
     scratch = [
@@ -488,233 +500,573 @@
     ] + [pltpu.VMEM(s, BF) for s in wshapes] + [
         pltpu.SemaphoreType.DMA((4 * layers, 7)),
         pltpu.SemaphoreType.DMA((2 * layers, 2)),
-        pltpu.SemaphoreType.DMA((5 * layers + 4,)),
+        pltpu.SemaphoreType.DMA((5 * layers + 5,)),
     ]
     return pl.pallas_call(
         functools.partial(forward_kernel, n, layers),
         out_shape=outs,
         in_specs=[VMEM] * 9 + [ANY] * 4,
-        out_specs=[ANY] * 10,
+        out_specs=[ANY] * 11,
         scratch_shapes=scratch,
         compiler_params=pltpu.CompilerParams(collective_id=1, has_side_effects=True, vmem_limit_bytes=60 * 2**20),
         name="forward",
     )(stream_in, masks, gains, biases, subs, scales, table, table_t, tap_table, win, wout, wup, wdn)
 
 
-def norm_rows(values, gain_row, bias_row):
-    centred = values - jnp.mean(values, axis=-1, keepdims=True)
-    variance = jnp.mean(centred * centred, axis=-1, keepdims=True)
-    return centred * lax.rsqrt(variance + EPSILON) * gain_row + bias_row
-
-
-def build_kernel(sub_taps):
-    pieces = []
-    for level_index in range(sub_taps.shape[0]):
-        repeats = 2 ** max(level_index, 1)
-        pieces.append(jnp.repeat(sub_taps[level_index], repeats, axis=0) * DECAY_RATE**level_index)
-    raw_taps = jnp.concatenate(pieces, axis=0)
-    return raw_taps * lax.rsqrt(jnp.sum(raw_taps * raw_taps, axis=0, keepdims=True) + EPSILON)
-
-
-def transform_matrix(quarter):
-    freq = np.arange(quarter)[:, None] + 0.5
-    angle = np.pi * freq * np.arange(quarter)[None, :] / quarter
-    return np.concatenate([np.cos(angle), -np.sin(angle)], axis=0).astype(np.float32)
-
-
-def mul(a, b):
-    return (a[0] * b[0] - a[1] * b[1], a[0] * b[1] + a[1] * b[0])
-
-
-def mul_conj(a, b):
-    return (a[0] * b[0] + a[1] * b[1], a[0] * b[1] - a[1] * b[0])
-
-
-def add(a, b):
-    return (a[0] + b[0], a[1] + b[1])
-
-
-def turn(a, sign):
-    return (-sign * a[1], sign * a[0])
-
-
-def turn_back(a, sign):
-    return (sign * a[1], -sign * a[0])
-
-
-def split_docs(blocks, seg):
-    long_doc = seg[1, 0]
-    kept = [jnp.where((seg[n] == long_doc)[:, None], blocks[n], 0) for n in range(4)]
-    for k in range(3):
-        doc = k + (k >= long_doc).astype(jnp.int32)
-        kept.append(
-            jnp.where((seg[0] == doc)[:, None], blocks[0], 0)
-            + jnp.where((seg[3] == doc)[:, None], blocks[3], 0)
+PIECE_UP, PIECE_DOWN, PIECE_OUT, PIECE_IN, PIECE_ROWS = 0, 64, 128, 144, 176
+
+
+def norm_back(upstream, src, base, gain, out, rounded):
+    width = src.shape[1]
+
+    def strip(j, sums):
+        r = rows_of(j, 16)
+        v = src[r, :]
+        centred = v - jnp.mean(v, axis=-1, keepdims=True)
+        inverse = lax.rsqrt(jnp.mean(centred * centred, axis=-1, keepdims=True) + EPSILON)
+        xhat = centred * inverse
+        up = upstream[r, :]
+        q = gain * up
+        both = q - jnp.mean(q, axis=-1, keepdims=True) - xhat * jnp.mean(q * xhat, axis=-1, keepdims=True)
+        got = base[r, :] + both * inverse
+        out[r, :] = got
+        if rounded is not None:
+            rounded[r, :] = got.astype(BF)
+        p = up * xhat
+        return sums[0] + p[:8] + p[8:], sums[1] + up[:8] + up[8:]
+
+    zero = jnp.zeros((8, width), F32)
+    return lax.fori_loop(0, src.shape[0] // 16, strip, (zero, zero))
+
+
+def back_products(spec_x, spec_c, wins, out_g, out_d, channels):
+    quarter = wins.shape[2]
+    half = out_g.shape[1] // 2
+
+    def strip(j):
+        r = rows_of(j, 16)
+        s = rows_of(j + quarter // 16, 16)
+        cols = [slice(n * channels, (n + 1) * channels) for n in range(7)]
+        cols2 = [slice(half + n * channels, half + (n + 1) * channels) for n in range(7)]
+        cs = [(spec_c[r, c], spec_c[s, c]) for c in cols]
+        for n in range(7):
+            re = im = None
+            for m in range(4 - n if n < 4 else 1):
+                w, x = (wins[m, 0, r, :], wins[m, 1, r, :]), cs[n + m]
+                a = w[0] * x[0] + w[1] * x[1]
+                b = w[0] * x[1] - w[1] * x[0]
+                re, im = (a, b) if re is None else (re + a, im + b)
+            out_g[r, cols[n]] = re.astype(BF)
+            out_g[r, cols2[n]] = im.astype(BF)
+        sign = (1 - 2 * lax.rem(lax.broadcasted_iota(jnp.int32, (16, channels), 0), 2)).astype(F32)
+        later = None
+        for m in (3, 2, 1, 0):
+            pairs = [(n - m, n) for n in range(m, 4)] + ([(n, n) for n in range(4, 7)] if m == 0 else [])
+            re = im = None
+            for i, n in pairs:
+                x, c = (spec_x[r, cols[i]], spec_x[s, cols[i]]), cs[n]
+                a = x[0] * c[0] + x[1] * c[1]
+                b = x[0] * c[1] - x[1] * c[0]
+                re, im = (a, b) if re is None else (re + a, im + b)
+            dre, dim = (re, im) if later is None else (re + sign * later[1], im - sign * later[0])
+            later = (re, im)
+            out_d[r, cols[m]] = dre.astype(BF)
+            out_d[r, cols2[m]] = dim.astype(BF)
+
+    loop(quarter // 16, strip)
+
+
+class Reduce:
+    def __init__(self, place, bufs, sems, slot, layer, first, rows):
+        self.p, self.layer, self.slot, self.sems = place, layer, slot, sems
+        self.r = pl.ds(first, rows)
+        self.first, self.rows = first, rows
+        self.grads, self.r0, self.r1, self.r2, self.res = bufs
+        self.spare = self.grads.shape[0] - 1
+
+    def sem(self, k):
+        return self.sems.at[self.slot, k]
+
+    def strips(self, body):
+        loop(self.rows // 16, lambda j: body(pl.ds(pl.multiple_of(self.first + j * 16, 16), 16)))
+
+    def s0(self):
+        send(self.grads.at[self.spare, :, :, self.r], self.r0.at[self.layer, :, :, self.r], self.sem(0), self.sem(1), self.p.sibling())
+
+    def s1(self):
+        p, l = self.p, self.layer
+        await_bytes(self.r0.at[l, :, :, self.r], self.sem(0))
+        await_bytes(self.r0.at[l, :, :, self.r], self.sem(1))
+
+        def add(j):
+            def strip(r):
+                c, q = j // p.n, lax.rem(j, p.n)
+                total = self.grads[l, c, q, r, :].astype(F32) + self.r0[l, c, q, r, :].astype(F32)
+                self.grads[l, c, q, r, :] = total.astype(BF)
+
+            self.strips(strip)
+
+        loop(GROUP // 2 * p.n, add)
+        for k in range(1, GROUP // 2):
+            other = lax.rem(p.chip + k, GROUP // 2)
+            send(self.grads.at[l, other, :, self.r], self.r1.at[l, k - 1, :, self.r], self.sem(2), self.sem(3), p.mate(k)[1])
+
+    def s2(self):
+        p, l = self.p, self.layer
+        await_bytes(self.r1.at[l, :, :, self.r], self.sem(2))
+        await_bytes(self.r1.at[l, :, :, self.r], self.sem(3))
+
+        def add(q):
+            def strip(r):
+                total = self.grads[l, p.chip, q, r, :].astype(F32)
+                for k in range(GROUP // 2 - 1):
+                    total += self.r1[l, k, q, r, :].astype(F32)
+                self.grads[l, p.chip, q, r, :] = total.astype(BF)
+
+            self.strips(strip)
+
+        loop(p.n, add)
+        for k in range(1, p.n):
+            q, peer = p.column(k)
+            send(self.grads.at[l, p.chip, q, self.r], self.r2.at[l, k - 1, self.r], self.sem(4), self.sem(5), peer)
+
+    def s3(self):
+        p, l = self.p, self.layer
+        await_bytes(self.r2.at[l, :, self.r], self.sem(4))
+        await_bytes(self.r2.at[l, :, self.r], self.sem(5))
+
+        def strip(r):
+            total = self.grads[l, p.chip, p.q, r, :].astype(F32)
+            for k in range(p.n - 1):
+                total += self.r2[l, k, r, :].astype(F32)
+            self.res[l, p.i, r, :] = total.astype(BF)
+
+        self.strips(strip)
+        for k in range(1, GROUP // 2):
+            piece = self.res.at[l, p.i, self.r]
+            send(piece, piece, self.sem(6), self.sem(7), p.mate(k)[1])
+
+    def s4(self):
+        p, l = self.p, self.layer
+        await_bytes(self.res.at[l, pl.ds(0, GROUP // 2 - 1), self.r], self.sem(6))
+        await_bytes(self.res.at[l, pl.ds(0, GROUP // 2 - 1), self.r], self.sem(7))
+        for k in range(GROUP // 2):
+            piece = self.res.at[l, p.mate(k)[0], self.r]
+            send(piece, piece, self.sem(8), self.sem(9), p.sibling())
+
+    def end(self):
+        half = self.res.at[self.layer, pl.ds(0, GROUP // 2), self.r]
+        await_bytes(half, self.sem(8))
+        await_bytes(half, self.sem(9))
+
+
+def backward_kernel(
+    n, layers,
+    masks, gains, subs, scales, table, table_t, tap_t,
+    cotangent, stream_in, streams, gates, conv_ins, conv_outs, middles, wins_h, win_h, wout_h, wup_h, wdn_h,
+    biases,
+    grad_o, res_o, sub_o, norm_o,
+    grad, middle_grad, stream, gate, conv_in, conv_out, middle, wins, win, wout, wup, wdn,
+    grads, r0, r1, r2, res,
+    hidden, hidden_mid, active, up_grad, gated, out_grad, branch, joined, big_a, big_b, spread,
+    send_c, recv_c, send_d, recv_d, sub_s, sub_r, norm_s, norm_r, norm_t, norm_u,
+    load_sems, a2a_sems, red_sems, small_sems, out_sems,
+):
+    place = Place(n)
+    me, core = place.q, place.core
+    tokens, width = grad.shape
+    channels = width // n
+    quarter = tokens
+    ff = wup.shape[1]
+    half = ff // 2
+    spare = grads.shape[0] - 1
+    greet_all(place)
+
+    loads = {}
+
+    def load(name, l):
+        src, dst = {
+            "stream": (streams.at[l - 1] if l else stream_in, stream), "gate": (gates.at[l], gate),
+            "conv_in": (conv_ins.at[l], conv_in), "conv_out": (conv_outs.at[l], conv_out),
+            "middle": (middles.at[l], middle), "wins": (wins_h.at[l], wins), "in": (win_h.at[l], win),
+            "out": (wout_h.at[l], wout), "up": (wup_h.at[l], wup), "down": (wdn_h.at[l], wdn),
+            "grad": (cotangent, grad),
+        }[name]
+        copy = pltpu.make_async_copy(src, dst, load_sems.at[l, len([k for k in loads if k[1] == l])])
+        copy.start()
+        loads[name, l] = copy
+
+    def ready(name, l):
+        loads[name, l].wait()
+
+    def next_load(name, l):
+        if l:
+            load(name, l - 1)
+
+    def exchange_start(slot, src, dst, l):
+        for k in range(1, n):
+            q, peer = place.column(k)
+            send(src.at[q], dst.at[l, me], a2a_sems.at[slot, 0], a2a_sems.at[slot, 1], peer)
+
+    def exchange_wait(slot, src, dst, l):
+        await_bytes(src.at[pl.ds(0, n - 1)], a2a_sems.at[slot, 0])
+        await_bytes(dst.at[l, pl.ds(0, n - 1)], a2a_sems.at[slot, 1])
+
+    def holder(parity, l):
+        mine = 1 - (parity - core) * (parity - core)
+        return l * mine + spare * (1 - mine)
+
+    bufs = (grads, r0, r1, r2, res)
+    first = [Reduce(place, bufs, red_sems, 2 * l, l, 0, PIECE_IN) for l in range(layers)]
+    second = [Reduce(place, bufs, red_sems, 2 * l + 1, l, PIECE_IN, PIECE_ROWS - PIECE_IN) for l in range(layers)]
+
+    top = layers - 1
+    for name in ("middle", "grad", "up", "down", "out", "gate", "conv_out", "conv_in", "wins", "stream", "in"):
+        load(name, top)
+
+    for l in reversed(range(layers)):
+        ready("middle", l)
+        norm_all(middle, hidden_mid, gains[l, 1], biases[l, 1])
+        if l == top:
+            ready("grad", l)
+
+        def round_grad(j):
+            r = rows_of(j, 32)
+            branch[r, :] = grad[r, :].astype(BF)
+
+        loop(tokens // 32, round_grad)
+        ready("up", l)
+        ready("down", l)
+
+        def widen(j):
+            r = rows_of(j, 256)
+            for h in range(2):
+                c = slice(h * half, (h + 1) * half)
+                t = slice(h * 256, (h + 1) * 256)
+                big_a[t, :] = dot(hidden_mid[r, :], wup[:, c])
+                big_b[t, :] = dot_nt(branch[r, :], wdn[c, :])
+
+            def activate(k):
+                for h in range(2):
+                    c = slice(h * half, (h + 1) * half)
+                    t = pl.ds(pl.multiple_of(h * 256 + k * 16, 16), 16)
+                    s = pl.ds(pl.multiple_of(j * 256 + k * 16, 16), 16)
+                    act, slope = gelu_both(big_a[t, :])
+                    active[s, c] = act.astype(BF)
+                    up_grad[s, c] = (big_b[t, :] * slope).astype(BF)
+
+            loop(256 // 16, activate)
+
+        loop(tokens // 256, widen)
+
+        def narrow(j):
+            r = rows_of(j, 256)
+            big_a[r, 0:width] = dot_nt(up_grad[r, :], wup[...])
+
+        loop(tokens // 256, narrow)
+        next_load("up", l)
+        next_load("down", l)
+        sums_mid = norm_back(big_a.at[:, 0:width], middle, grad, gains[l, 1], middle_grad, out_grad)
+        next_load("middle", l)
+
+        ready("out", l)
+
+        def gated_back(j):
+            r = rows_of(j, 256)
+            big_b[r, 0:width] = dot_nt(out_grad[r, :], wout[...])
+
+        loop(tokens // 256, gated_back)
+        next_load("out", l)
+        ready("gate", l)
+        ready("conv_out", l)
+
+        def unmix(j):
+            r = rows_of(j, 16)
+            for q in range(n):
+                c = slice(q * channels, (q + 1) * channels)
+                act, slope = gelu_both(gate[r, c])
+                up, conv = big_b[r, c], conv_out[q, r, :].astype(F32)
+                send_c[q, r, :] = (up * act).astype(BF)
+                joined[r, slice(width + q * channels, width + (q + 1) * channels)] = (up * conv * slope).astype(BF)
+                gated[r, c] = (act * conv).astype(BF)
+
+        loop(tokens // 16, unmix)
+        next_load("gate", l)
+        next_load("conv_out", l)
+        exchange_start(2 * l, send_c, recv_c, l)
+        recv_c[l, me] = send_c[me]
+
+        if l < top:
+            second[l + 1].s1()
+
+        def grad_up(c):
+            got = dot_tn(hidden_mid[:, rows_of(c, 128)], up_grad[...]).astype(BF)
+            for par in range(2):
+                for q in range(n):
+                    grads[holder(par, l), c, q, PIECE_UP:PIECE_DOWN, :] = got[par * 64 : par * 64 + 64, q * (ff // n) : (q + 1) * (ff // n)]
+
+        loop(GROUP // 2, grad_up)
+
+        def grad_down(q):
+            got = dot_tn(active[:, rows_of(q, ff // n)], branch[...]).astype(BF)
+            for i in range(GROUP):
+                grads[holder(i % 2, l), i // 2, q, PIECE_DOWN:PIECE_OUT, :] = got[i * 64 : (i + 1) * 64]
+
+        loop(n, grad_down)
+
+        def grad_out(q):
+            got = dot_tn(gated[:, rows_of(q, channels)], out_grad[...]).astype(BF)
+            for i in range(GROUP):
+                grads[holder(i % 2, l), i // 2, q, PIECE_OUT:PIECE_IN, :] = got[i * 16 : (i + 1) * 16]
+
+        loop(n, grad_out)
+        first[l].s0()
+        if l < top:
+            first[l + 1].s3()
+
+        def grad_in(h):
+            def block(c):
+                got = dot_tn(hidden[:, rows_of(c, 128)], joined[:, h * width : (h + 1) * width]).astype(BF)
+                for par in range(2):
+                    for q in range(n):
+                        for t in range(2):
+                            grads[holder(par, l), c, q, PIECE_IN:PIECE_ROWS, h * 256 + t * 128 : h * 256 + (t + 1) * 128] = got[
+                                par * 64 + t * 32 : par * 64 + (t + 1) * 32, q * channels : (q + 1) * channels
+                            ]
+
+            loop(GROUP // 2, block)
+
+        ready("stream", l)
+        norm_all(stream, hidden, gains[l, 0], biases[l, 0])
+        grad_in(1)
+        ready("conv_in", l)
+        spread_blocks(conv_in, masks, spread)
+
+        def transform_x(j):
+            r = rows_of(j, 256)
+            big_a[r, 0 : 7 * channels] = dot(table[r, :], spread[...])
+
+        loop(2 * quarter // 256, transform_x)
+        next_load("conv_in", l)
+        first[l].s1()
+        if l < top:
+            first[l + 1].s4()
+        exchange_wait(2 * l, send_c, recv_c, l)
+        spread_blocks(recv_c.at[l], masks, spread)
+
+        def transform_c(j):
+            r = rows_of(j, 256)
+            big_b[r, 0 : 7 * channels] = dot(table[r, :], spread[...])
+
+        loop(2 * quarter // 256, transform_c)
+        ready("wins", l)
+        back_products(big_a, big_b, wins, active, up_grad, channels)
+        next_load("wins", l)
+
+        def untransform(j):
+            r = rows_of(j, 128)
+            parts = dot(table_t[r, 0:quarter], active[:, 0 : 7 * channels])
+            parts += dot(table_t[r, quarter : 2 * quarter], active[:, half : half + 7 * channels])
+            for q in range(n):
+                send_d[q, r, :] = join_blocks(parts, r, masks, q).astype(BF)
+
+        loop(quarter // 128, untransform)
+        exchange_start(2 * l + 1, send_d, recv_d, l)
+        recv_d[l, me] = send_d[me]
+
+        taps = None
+        for m in range(4):
+            c = slice(m * channels, (m + 1) * channels)
+            d = slice(half + m * channels, half + (m + 1) * channels)
+            got = dot(tap_t[m, :, 0:quarter], up_grad[:, c]) + dot(tap_t[m, :, quarter : 2 * quarter], up_grad[:, d])
+            taps = got if taps is None else taps + got
+        raw = subs[l] * scales[0]
+        inverse = lax.rsqrt(jnp.sum(raw * raw * scales[1], axis=0, keepdims=True) + EPSILON)
+        k = raw * inverse
+        along = jnp.sum(taps * k, axis=0, keepdims=True)
+        sub_s[l] = scales[0] * (taps - scales[1] * k * along) * inverse
+        for j in range(1, GROUP):
+            send(sub_s.at[l], sub_r.at[l, j - 1], small_sems.at[l, 0], small_sems.at[l, 1], place.member(j))
+
+        def project_back_gate(j):
+            r = rows_of(j, 256)
+            big_a[r, 0:width] = dot_nt(joined[r, width : 2 * width], win[1])
+
+        ready("in", l)
+        loop(tokens // 256, project_back_gate)
+        exchange_wait(2 * l + 1, send_d, recv_d, l)
+        first[l].s2()
+        if l < top:
+            second[l + 1].s2()
+
+        def collect(j):
+            r = rows_of(j, 32)
+            for q in range(n):
+                joined[r, q * channels : (q + 1) * channels] = recv_d[l, q, r, :]
+
+        loop(tokens // 32, collect)
+
+        def project_back(j):
+            r = rows_of(j, 256)
+            big_a[r, 0:width] = big_a[r, 0:width] + dot_nt(joined[r, 0:width], win[0])
+
+        if l == 0:
+            grad_in(0)
+            second[l].s0()
+        loop(tokens // 256, project_back)
+        next_load("in", l)
+        sums_in = norm_back(big_a.at[:, 0:width], stream, middle_grad, gains[l, 0], grad, None)
+        next_load("stream", l)
+        norm_s[l] = jnp.concatenate(
+            [jnp.sum(s, axis=0, keepdims=True) for s in (sums_in[0], sums_mid[0], sums_in[1], sums_mid[1])]
+            + [jnp.zeros((4, width), F32)],
+            axis=0,
         )
-    return jnp.stack(kept)
-
-
-def join_docs(parts, seg):
-    long_doc = seg[1, 0]
-    out = [jnp.where((seg[n] == long_doc)[:, None], parts[n], 0) for n in range(4)]
-    for k in range(3):
-        doc = k + (k >= long_doc).astype(jnp.int32)
-        for n in (0, 3):
-            out[n] = out[n] + jnp.where((seg[n] == doc)[:, None], parts[4 + k], 0)
-    return jnp.stack(out)
-
-
-def spectrum(blocks, table):
-    both = jnp.einsum("fp,npc->nfc", table, blocks.astype(BF), preferred_element_type=F32)
-    quarter = blocks.shape[1]
-    return both[:, :quarter], both[:, quarter:]
-
-
-def unspectrum(pair, table):
-    both = jnp.concatenate(pair, axis=1).astype(BF)
-    return jnp.einsum("fp,nfc->npc", table, both, preferred_element_type=F32) / table.shape[1]
-
-
-def at(pair, n):
-    return (pair[0][n], pair[1][n])
-
-
-def windows(kernel, table, sign):
-    length, channels = kernel.shape
-    quarter = length // 4
-    d = spectrum(kernel.reshape(4, quarter, channels), table)
-    out = [at(d, 0)]
-    for m in range(1, 4):
-        out.append(add(at(d, m), turn(at(d, m - 1), sign)))
-    return out
-
-
-def conv(values, kernel, seg, table, sign):
-    w = windows(kernel, table, sign)
-    x = spectrum(split_docs(values, seg), table)
-    ys = []
-    for n in range(7):
-        if n < 4:
-            y = mul(w[0], at(x, n))
-            for m in range(1, n + 1):
-                y = add(y, mul(w[m], at(x, n - m)))
-        else:
-            y = mul(w[0], at(x, n))
-        ys.append(y)
-    parts = unspectrum((jnp.stack([y[0] for y in ys]), jnp.stack([y[1] for y in ys])), table)
-    return join_docs(parts, seg), x
-
-
-def conv_back(upstream, x, kernel, seg, table, sign):
-    w = windows(kernel, table, sign)
-    c = spectrum(split_docs(upstream, seg), table)
-    gs = []
-    for n in range(7):
-        g = mul_conj(w[0], at(c, n))
-        if n < 4:
-            for m in range(1, 4 - n):
-                g = add(g, mul_conj(w[m], at(c, n + m)))
-        gs.append(g)
-    parts = unspectrum((jnp.stack([g[0] for g in gs]), jnp.stack([g[1] for g in gs])), table)
-    dw = []
-    for m in range(4):
-        total = None
-        for n in range(m, 4):
-            term = mul_conj(at(x, n - m), at(c, n))
-            total = term if total is None else add(total, term)
-        dw.append(total)
-    for n in range(4, 7):
-        dw[0] = add(dw[0], mul_conj(at(x, n), at(c, n)))
-    dd = [add(dw[m], turn_back(dw[m + 1], sign)) if m < 3 else dw[m] for m in range(4)]
-    taps = unspectrum((jnp.stack([g[0] for g in dd]), jnp.stack([g[1] for g in dd])), table)
-    return join_docs(parts, seg), taps.reshape(-1, taps.shape[2])
-
-
-def to_channels(rows):
-    n = lax.axis_size("mp")
-    return lax.all_to_all(rows.reshape(rows.shape[0], n, -1), "mp", 1, 0)
-
-
-def to_tokens(blocks):
-    got = lax.all_to_all(blocks, "mp", 0, 1)
-    return got.reshape(got.shape[0], -1)
-
-
-def dot_tn(a, b):
-    return lax.dot_general(a, b, (((0,), (0,)), ((), ())), preferred_element_type=F32)
-
-
-def dot_nt(a, b):
-    return lax.dot_general(a, b, (((1,), (1,)), ((), ())), preferred_element_type=F32)
+        for j in range(1, GROUP):
+            send(norm_s.at[l], norm_r.at[l, j - 1], small_sems.at[l, 2], small_sems.at[l, 3], place.member(j))
+        if l:
+            grad_in(0)
+            second[l].s0()
+
+    out = pltpu.make_async_copy(grad, grad_o, out_sems.at[0])
+    out.start()
+    second[0].s1()
+    if layers > 1:
+        second[1].s3()
+    first[0].s3()
+    for l in reversed(range(layers)):
+        await_bytes(norm_r.at[l], small_sems.at[l, 2])
+        await_bytes(norm_r.at[l], small_sems.at[l, 3])
+        norm_t[l] = sum_members(norm_s[l], norm_r, l, place)
+        for k in range(1, n):
+            send(norm_t.at[l], norm_u.at[l, k - 1], small_sems.at[l, 4], small_sems.at[l, 5], place.column(k)[1])
+    second[0].s2()
+    first[0].s4()
+    if layers > 1:
+        second[1].s4()
+    for l in reversed(range(layers)):
+        await_bytes(sub_r.at[l], small_sems.at[l, 0])
+        await_bytes(sub_r.at[l], small_sems.at[l, 1])
+        sub_s[l] = sum_members(sub_s[l], sub_r, l, place)
+    second[0].s3()
+    for l in reversed(range(layers)):
+        await_bytes(norm_u.at[l], small_sems.at[l, 4])
+        await_bytes(norm_u.at[l], small_sems.at[l, 5])
+        norm_s[l] = sum_columns(norm_t[l], norm_u, l, place)
+    out_sub = pltpu.make_async_copy(sub_s, sub_o, out_sems.at[1])
+    out_sub.start()
+    out_norm = pltpu.make_async_copy(norm_s, norm_o, out_sems.at[2])
+    out_norm.start()
+    second[0].s4()
+    for r in first + second:
+        if r is not second[0]:
+            r.end()
+    second[0].end()
+    out_res = pltpu.make_async_copy(res, res_o, out_sems.at[3])
+    out_res.start()
+    out.wait()
+    out_sub.wait()
+    out_norm.wait()
+    out_res.wait()
+
+
+def in_order(own, others, l, here, count):
+    total = None
+    for j in range(count):
+        k = lax.rem(here - j + count, count)
+        value = jnp.where(k == 0, own, others[l, lax.max(k - 1, 0)])
+        total = value if total is None else total + value
+    return total
+
+
+def sum_members(own, others, l, place):
+    return in_order(own, others, l, place.i, GROUP)
+
+
+def sum_columns(own, others, l, place):
+    return in_order(own, others, l, place.q, place.n)
+
+
+def backward(n, masks, gains, biases, subs, scales, table, table_t, tap_t, cotangent, stream_in, kept):
+    streams, gates, conv_ins, conv_outs, middles, wins, win, wout, wup, wdn = kept
+    layers = win.shape[0]
+    tokens, width = cotangent.shape
+    channels = width // n
+    ff = wup.shape[2]
+    taps = subs.shape[1]
+
+    def sds(*shape, dtype=F32):
+        return jax.ShapeDtypeStruct(shape, dtype)
+
+    outs = [sds(tokens, width), sds(layers, GROUP, PIECE_ROWS, width, dtype=BF), sds(layers, taps, channels), sds(layers, 8, width)]
+    f32 = lambda *s: pltpu.VMEM(s, F32)
+    bf = lambda *s: pltpu.VMEM(s, BF)
+    scratch = [
+        f32(tokens, width), f32(tokens, width), f32(tokens, width), f32(tokens, width),
+        bf(n, tokens, channels), bf(n, tokens, channels), f32(tokens, width), f32(4, 2, tokens, channels),
+        bf(2, width, width), bf(width, width), bf(width, ff), bf(ff, width),
+        bf(layers + 1, GROUP // 2, n, PIECE_ROWS, width),
+        bf(layers, GROUP // 2, n, PIECE_ROWS, width),
+        bf(layers, GROUP // 2 - 1, n, PIECE_ROWS, width),
+        bf(layers, n - 1, PIECE_ROWS, width),
+        bf(layers, GROUP, PIECE_ROWS, width),
+        bf(tokens, width), bf(tokens, width), bf(tokens, ff), bf(tokens, ff), bf(tokens, width), bf(tokens, width), bf(tokens, width),
+        bf(tokens, 2 * width), f32(2 * tokens, ff // 2), f32(2 * tokens, ff // 2), bf(tokens, 7 * channels),
+        bf(n, tokens, channels), bf(layers, n, tokens, channels), bf(n, tokens, channels), bf(layers, n, tokens, channels),
+        f32(layers, taps, channels), f32(layers, GROUP - 1, taps, channels),
+        f32(layers, 8, width), f32(layers, GROUP - 1, 8, width), f32(layers, 8, width), f32(layers, n - 1, 8, width),
+        pltpu.SemaphoreType.DMA((layers, 11)),
+        pltpu.SemaphoreType.DMA((2 * layers, 2)),
+        pltpu.SemaphoreType.DMA((2 * layers, 10)),
+        pltpu.SemaphoreType.DMA((layers, 6)),
+        pltpu.SemaphoreType.DMA((4,)),
+    ]
+    return pl.pallas_call(
+        functools.partial(backward_kernel, n, layers),
+        out_shape=outs,
+        in_specs=[VMEM] * 7 + [ANY] * 12 + [VMEM],
+        out_specs=[ANY] * 4,
+        scratch_shapes=scratch,
+        compiler_params=pltpu.CompilerParams(collective_id=2, has_side_effects=True, vmem_limit_bytes=int(63.5 * 2**20)),
+        name="backward",
+    )(masks, gains, subs, scales, table, table_t, tap_t, cotangent, stream_in, streams, gates, conv_ins, conv_outs, middles, wins, win, wout, wup, wdn, biases)
 
 
 def per_device(
     stream_in, segments, norm_gain, norm_bias, w_in, w_out, sub_kernels, w_up, w_down, cotangent
 ):
-    layers, scales, taps_n, channels = sub_kernels.shape
+    layers, scales, taps, channels = sub_kernels.shape
     n = lax.axis_size("mp")
     quarter = segments.shape[1] // 4
-    seg = segments.reshape(4, quarter)
-    table_np = transform_table(quarter)
-    table = jnp.asarray(table_np, F32).astype(BF)
-    sign = jnp.asarray(1.0 - 2.0 * (np.arange(quarter)[:, None] % 2), F32)
+    table = transform_table(quarter)
+    tap_table = tap_tables(quarter, scales, taps) / quarter
+
+    def const(a):
+        return jnp.asarray(a, F32).astype(BF)
+
     masks = doc_masks(segments, channels)
-    tap_table = jnp.asarray(tap_tables(quarter, scales, taps_n) / quarter, F32).astype(BF)
-    consts = jnp.asarray(tap_scales(scales, taps_n, channels))
-    out, streams, gate_all, conv_in, conv_out, middle_all, w_in_f, w_out_f, w_up_f, w_down_f = forward(
-        n, stream_in, masks, norm_gain[:, :, None], norm_bias[:, :, None], sub_kernels.reshape(layers, -1, channels), consts,
-        table, table.T, tap_table, w_in.transpose(0, 2, 1, 3), w_out, w_up, w_down)
-    kept = []
-    for l in range(layers):
-        layer_in = stream_in if l == 0 else streams[l - 1]
-        hidden = norm_rows(layer_in, norm_gain[l, 0], norm_bias[l, 0]).astype(BF)
-        convolved = conv_out[l].transpose(1, 0, 2).reshape(quarter, -1).astype(F32)
-        gate_pre = gate_all[l]
-        gated = (jax.nn.gelu(gate_pre) * convolved).astype(BF)
-        middle = middle_all[l]
-        hidden_mid = norm_rows(middle, norm_gain[l, 1], norm_bias[l, 1]).astype(BF)
-        up_pre = jnp.dot(hidden_mid, w_up_f[l], preferred_element_type=F32)
-        active = jax.nn.gelu(up_pre).astype(BF)
-        kernel = build_kernel(sub_kernels[l]).astype(BF)
-        x = spectrum(split_docs(conv_in[l], seg), table)
-        kept.append((layer_in, hidden, gate_pre, kernel, x, convolved, gated, middle, hidden_mid, up_pre, active))
-    grad = cotangent
-    collected = []
-    for l in reversed(range(layers)):
-        layer_in, hidden, gate_pre, kernel, x, convolved, gated, middle, hidden_mid, up_pre, active = kept[l]
-        branch_grad = grad.astype(BF)
-        g_down = dot_tn(active, branch_grad)
-        up_grad = jax.vjp(jax.nn.gelu, up_pre)[1](dot_nt(branch_grad, w_down_f[l]))[0].astype(BF)
-        g_up = dot_tn(hidden_mid, up_grad)
-        hidden_grad = dot_nt(up_grad, w_up_f[l])
-        pull = jax.vjp(norm_rows, middle, norm_gain[l, 1], norm_bias[l, 1])[1]
-        norm_grad, gain1, bias1 = pull(hidden_grad)
-        middle_grad = grad + norm_grad
-        out_grad = middle_grad.astype(BF)
-        g_out = dot_tn(gated, out_grad)
-        gated_grad = dot_nt(out_grad, w_out_f[l])
-        act, gate_pull = jax.vjp(jax.nn.gelu, gate_pre)
-        conv_grad = (gated_grad * act).astype(BF)
-        gate_grad = gate_pull(gated_grad * convolved)[0].astype(BF)
-        input_grad, taps = conv_back(to_channels(conv_grad), x, kernel, seg, table, sign)
-        input_grad = to_tokens(input_grad.astype(BF))
-        g_sub = jax.vjp(build_kernel, sub_kernels[l])[1](taps)[0]
-        g_in = jnp.stack([dot_tn(hidden, input_grad), dot_tn(hidden, gate_grad)], axis=1)
-        hidden_grad = dot_nt(input_grad, w_in_f[l, 0]) + dot_nt(gate_grad, w_in_f[l, 1])
-        pull = jax.vjp(norm_rows, layer_in, norm_gain[l, 0], norm_bias[l, 0])[1]
-        norm_grad, gain0, bias0 = pull(hidden_grad)
-        grad = middle_grad + norm_grad
-        collected.insert(0, (jnp.stack([gain0, gain1]), jnp.stack([bias0, bias1]), g_in, g_out, g_sub, g_up, g_down))
-    gain, bias, g_in, g_out, g_sub, g_up, g_down = [jnp.stack([c[i] for c in collected]) for i in range(7)]
-    g_in = lax.psum_scatter(g_in.astype(BF), "mp", scatter_dimension=3, tiled=True)
-    g_out = lax.psum_scatter(g_out.astype(BF), "mp", scatter_dimension=1, tiled=True)
-    g_up = lax.psum_scatter(g_up.astype(BF), "mp", scatter_dimension=2, tiled=True)
-    g_down = lax.psum_scatter(g_down.astype(BF), "mp", scatter_dimension=1, tiled=True)
-    g_in, g_out, g_sub, g_up, g_down = lax.psum(
-        (g_in.astype(F32), g_out.astype(F32), g_sub, g_up.astype(F32), g_down.astype(F32)), "dp"
+    factors = jnp.asarray(tap_scales(scales, taps, channels))
+    subs = sub_kernels.reshape(layers, -1, channels)
+    gains, biases = norm_gain[:, :, None], norm_bias[:, :, None]
+    out, *kept = forward(
+        n, stream_in, masks, gains, biases, subs, factors, const(table), const(table.T), const(tap_table),
+        w_in.transpose(0, 2, 1, 3), w_out, w_up, w_down,
     )
-    gain, bias = lax.psum((gain, bias), ("dp", "mp"))
-    return out, grad, gain, bias, g_in, g_out, g_sub, g_up, g_down
+    grad, res, sub, norms = backward(
+        n, masks, gains, biases, subs, factors, const(table), const(table.T), const(tap_table.transpose(0, 2, 1)),
+        cotangent, stream_in, kept,
+    )
+    res = res.astype(F32)
+    if lax.axis_size("dp") > GROUP:
+        groups = lax.axis_size("dp") // GROUP
+        res, sub, norms = [v * (1.0 / GROUP) for v in lax.psum((res, sub, norms), "dp")]
+    width = stream_in.shape[1]
+    up = res[:, :, PIECE_UP:PIECE_DOWN].reshape(w_up.shape)
+    down = res[:, :, PIECE_DOWN:PIECE_OUT].reshape(w_down.shape)
+    out_w = res[:, :, PIECE_OUT:PIECE_IN].reshape(w_out.shape)
+    in_w = res[:, :, PIECE_IN:].reshape(layers, GROUP, PIECE_ROWS - PIECE_IN, 2, 2, channels)
+    in_w = in_w.transpose(0, 1, 4, 2, 3, 5).reshape(w_in.shape)
+    return out, grad, norms[:, 0:2], norms[:, 2:4], in_w, out_w, sub.reshape(sub_kernels.shape), up, down
 
 
 def solution(mesh):

time: 687 us -> 340 us (0.49); the launches traced: 677 us -> 339 us
  Pallas kernels: 131 us -> 309 us
  blocking collectives: 159 us -> 0 us
  waiting for transfers between devices: 136 us -> 0 us
  other arithmetic: 76.8 us -> 2.77 us
  matrix products: 70.8 us -> 0 us
  local copies, waits for them, and re-layouts: 64.1 us -> 24.3 us
  starting transfers between devices: 20 us -> 0 us
  between operations: 19.6 us -> 2.63 us
    pallas_call x0 -> x1, Pallas kernels: none -> 177 us  [backward(): pl.pallas_call(functools.partial(backward_kernel, n, layers), out_shape=o...]
    psum x2 -> x0, blocking collectives: 159 us -> none  [the longest x1 118 us: per_device(): lax.psum((g_in.astype(F32), g_out.astype(F32), g_sub, g_up.astype(F32), g...]
    reduce_scatter x3 -> x0, waiting for transfers between devices: 107 us -> none  [the longest x1 79.6 us: per_device(): lax.psum_scatter(g_up.astype(BF), 'mp', scatter_dimension=2, tiled=True)]
    dot_general x32 -> x0, matrix products: 70.8 us -> none  [the longest x10 23.6 us: dot_nt(): lax.dot_general(a, b, (((1,), (1,)), ((), ())), preferred_element_type=F32)]
    another operation x34 -> x0, other arithmetic: 29.5 us -> none  [the longest x15 11.6 us: per_device(): jnp.stack([c[i] for c in collected])]
    all_to_all x4 -> x0, waiting for transfers between devices: 28.6 us -> none  [the longest x2 14.8 us: to_tokens(): got = lax.all_to_all(blocks, 'mp', 0, 1)]
    unnamed x252 -> x13, local copies, waits for them, and re-layouts: 31.8 us -> 5.67 us
    unnamed x31 -> x1, other arithmetic: 23.6 us -> 1.36 us
  transfers between devices with their start and end apart: 9 -> 0, of which waited for: 6 -> 0; matrix products, arithmetic and copies ran while one was open for 19% -> 0% of each run, Pallas kernels for 0% -> 0%
where the time goes in v3:
time: 340 us; the launch traced here: 339 us
  Pallas kernels  309 us (91%)
  local copies, waits for them, and re-layouts  24.3 us (7%)
    pallas_call x1, Pallas kernels, backward(): pl.pallas_call(functools.partial(backward_kernel, n, layers), out_shape=o...  177 us
    pallas_call x1, Pallas kernels, forward(): pl.pallas_call(functools.partial(forward_kernel, n, layers), out_shape=ou...  132 us

profile of v3, /device:TPU:0, one launch (start us, length us, event | category | flops | bytes accessed | tf_op | source)
XLA Modules:
  0.0 339.1 jit_solution(4257130710082622022)
XLA Ops:
  0.6 0.5 broadcast.13
  1.2 1.4 reduce.3
  2.5 0.5 slice.54
  5.0 1.3 broadcast_in_dim.13.gains
  6.3 1.3 broadcast_in_dim.14.biases
  7.6 1.4 broadcast_compare_fusion
  9.0 0.1 stack.2
  9.1 1.9 copy.29
  11.0 1.7 broadcast_in_dim.12.masks
  12.6 132.0 %forward.1 = (f32[512,512]{1,0:T(8,128)}, f32[1,512,512]{2,1,0:T(8,128)}, f32[2,512,512]{2,1,0:T(8,128)}, bf16[2,4,512,128]{3,2,1,0:T(8,128)(2,1)}, bf16[2,4,512...) custom-call(f32[512,512]{1,0:T(8,128)} %stream_in.3, ...), custom_call_target="tpu_custom_call" | custom-call | tf_op jit(solution)/shard_map/forward/pallas_call | solution.py:505
  144.7 177.4 %backward.1 = (f32[512,512]{1,0:T(8,128)}, bf16[2,8,176,512]{3,2,1,0:T(8,128)(2,1)}, f32[2,192,128]{2,1,0:T(8,128)}, f32[2,8,512]{2,1,0:T(8,128)}) custom-call(bf16[10,512,128]{2,1,0:T(8,128)(2,1)} %broadcast_in_dim.12.masks, f32[2,2,1,512]{3,2,1,0:T(1,128)} %broadcast_in_dim.13.gains, f32[2,192,128]{2,1,0:T(8,128)} %bitcast.19, ...), custom_call_target="tpu_custom_call" | custom-call | tf_op jit(solution)/shard_map/backward/pallas_call | solution.py:1024
  322.1 1.4 fusion.1
  323.5 1.8 slice.56
  325.3 2.1 slice.55
  327.5 3.0 reshape.123
  330.5 2.7 copy.27
  333.2 0.0 copy-done
  333.2 2.6 fusion
  335.8 0.0 copy-done.1
  335.8 1.0 copy.33
  336.8 0.6 copy-done.2
  337.4 1.0 copy.34
  338.4 0.0 copy-done.3
  338.4 0.7 copy.35
  (6 shorter events, 0.0 us)
Async XLA Ops:
  327.5 5.7 %copy-start = (bf16[2,8,176,512]{3,2,1,0:T(8,128)(2,1)S(1)}, bf16[2,8,176,512]{3,2,1,0:T(8,128)(2,1)}, u32[]{:S(2)}) copy-start(bf16[2,8,176,512]{3,2,1,0:T(8,128)(2,1)} %get-tuple-element.37) | copy-start | bytes 8650756
  333.2 2.6 copy-start.1
  335.8 1.6 copy-start.2
  335.8 2.6 copy-start.3

commit v4 on v3

v4 whole, which is shorter than its diff:
```python
import functools

import jax
import jax.numpy as jnp
import numpy as np
from jax import lax
from jax.experimental import pallas as pl
from jax.experimental.pallas import tpu as pltpu
from jax.sharding import PartitionSpec as P

DECAY_RATE = 0.5
EPSILON = 1e-05
BF = jnp.bfloat16
F32 = jnp.float32
GROUP = 8
MESH = pl.DeviceIdType.MESH
VMEM = pl.BlockSpec(memory_space=pltpu.VMEM)
ANY = pl.BlockSpec(memory_space=pl.ANY)
GELU_A = float(np.sqrt(2.0 / np.pi))
GELU_B = 0.044715


def dot(a, b):
    return jnp.dot(a, b, preferred_element_type=F32)


def dot_nt(a, b):
    return lax.dot_general(a, b, (((1,), (1,)), ((), ())), preferred_element_type=F32)


def dot_tn(a, b):
    return lax.dot_general(a, b, (((0,), (0,)), ((), ())), preferred_element_type=F32)


def gelu(u):
    return 0.5 * u * (1.0 + jnp.tanh(GELU_A * (u + GELU_B * (u * u * u))))


def gelu_both(u):
    square = u * u
    t = jnp.tanh(GELU_A * (u + GELU_B * (square * u)))
    half = 0.5 * (1.0 + t)
    slope = half + (0.5 * u) * (1.0 - t * t) * (GELU_A + (3.0 * GELU_A * GELU_B) * square)
    return u * half, slope


def loop(count, body):
    lax.fori_loop(0, count, lambda j, c: (body(j), c)[1], 0)


def when(condition, body):
    pl.when(condition)(body)


def rows_of(j, size):
    return pl.ds(pl.multiple_of(j * size, size), size)


def transform_table(quarter):
    freq = np.arange(quarter)[:, None] + 0.5
    angle = np.pi * freq * np.arange(quarter)[None, :] / quarter
    return np.concatenate([np.cos(angle), -np.sin(angle)], axis=0)


def spread_matrix(scales, taps):
    lags = []
    for level in range(scales):
        lags += [level * taps + j for j in range(taps) for _ in range(2 ** max(level, 1))]
    spread = np.zeros((len(lags), scales * taps))
    spread[np.arange(len(lags)), lags] = 1.0
    return spread


def tap_tables(quarter, scales, taps):
    table = transform_table(quarter)
    spread = spread_matrix(scales, taps).reshape(4, quarter, scales * taps)
    return np.einsum("fp,mpt->mft", table, spread)


def tap_scales(scales, taps, channels):
    level = np.repeat(np.arange(scales), taps)
    decay = DECAY_RATE**level
    repeats = 2.0 ** np.maximum(level, 1)
    both = np.stack([decay, repeats])[:, :, None]
    return np.broadcast_to(both, (2, scales * taps, channels)).astype(np.float32)


class Place:
    def __init__(self, n):
        self.n = n
        self.q = lax.axis_index("mp")
        dp = lax.axis_index("dp")
        self.i = lax.rem(dp, GROUP)
        self.base = dp - self.i
        self.core = lax.rem(self.i, 2)
        self.x = lax.rem(self.i // 2, 2)
        self.y = self.i // 4
        self.s = self.x + 2 * self.core

    def device(self, i, q):
        return {"dp": self.base + i, "mp": q}

    def index(self, y, x, core):
        return 4 * y + 2 * x + core

    def column(self, k):
        q = lax.rem(self.q + k, self.n)
        return q, self.device(self.i, q)

    def member(self, k):
        return self.device(lax.rem(self.i + k, GROUP), self.q)

    def mate_x(self):
        i = self.index(self.y, 1 - self.x, self.core)
        return i, self.device(i, self.q)

    def mate_y(self):
        i = self.index(1 - self.y, self.x, self.core)
        return i, self.device(i, self.q)

    def mate_xy(self):
        i = self.index(1 - self.y, 1 - self.x, self.core)
        return i, self.device(i, self.q)

    def mates(self, order):
        return (self.mate_x(), self.mate_y()) if order == "xy" else (self.mate_y(), self.mate_x())

    def sibling(self):
        return self.device(self.index(self.y, self.x, 1 - self.core), self.q)

    def partner(self, k):
        s = lax.rem(self.s + k, self.n)
        return s, self.device(self.index(self.y, lax.rem(s, 2), s // 2), self.q)

    def row_target(self):
        return self.index(self.y, lax.rem(self.q, 2), self.q // 2), 2 * self.core + self.x

    def stays(self):
        i, q = self.row_target()
        return jnp.logical_and(i == self.i, q == self.q)


def greet_all(place):
    barrier = pltpu.get_barrier_semaphore()
    peers = [place.column(k)[1] for k in range(1, place.n)] + [place.member(k) for k in range(1, GROUP)]
    for peer in peers:
        pl.semaphore_signal(barrier, inc=1, device_id=peer, device_id_type=MESH)

    def across():
        other = place.device(*place.row_target())
        pl.semaphore_signal(barrier, inc=1, device_id=other, device_id_type=MESH)
        pl.semaphore_wait(barrier, len(peers) + 1)

    def here():
        pl.semaphore_wait(barrier, len(peers))

    when(jnp.logical_not(place.stays()), across)
    when(place.stays(), here)


def send(src, dst, send_sem, recv_sem, peer):
    pltpu.make_async_remote_copy(
        src_ref=src, dst_ref=dst, send_sem=send_sem, recv_sem=recv_sem, device_id=peer, device_id_type=MESH
    ).start()


def await_bytes(ref, sem):
    pltpu.make_async_copy(ref, ref, sem).wait()


class Move:
    def __init__(self, place, src, dst, relay, sems):
        self.p, self.src, self.dst, self.relay, self.sems = place, src, dst, relay, sems
        p = place
        turn = p.q == 1 + p.core
        self.stays = p.stays()
        self.via = jnp.logical_and(turn, p.x == p.core)
        self.passes = jnp.logical_and(turn, p.x != p.core)
        self.direct = jnp.logical_not(jnp.logical_or(self.stays, self.via))

    def start(self):
        p = self.p

        def across():
            send(self.src, self.dst, self.sems.at[0], self.sems.at[1], p.device(*p.row_target()))

        def aside():
            send(self.src, self.relay, self.sems.at[0], self.sems.at[2], p.mate_x()[1])

        def here():
            pltpu.make_async_copy(self.src, self.dst, self.sems.at[1]).start()

        when(self.direct, across)
        when(self.via, aside)
        when(self.stays, here)

    def pass_on(self):
        p = self.p

        def onward():
            await_bytes(self.relay, self.sems.at[2])
            send(self.relay, self.dst, self.sems.at[3], self.sems.at[1], p.device(p.i, 3 * p.core))

        when(self.passes, onward)

    def arrive(self):
        await_bytes(self.dst, self.sems.at[1])

    def finish(self):
        when(jnp.logical_not(self.stays), lambda: await_bytes(self.src, self.sems.at[0]))
        when(self.passes, lambda: await_bytes(self.relay, self.sems.at[3]))


class Weight:
    def __init__(self, whole, layer, kind, n):
        self.whole, self.kind, self.layer, self.n = whole, kind, layer, n
        shape = whole.shape
        if kind == "in":
            self.rows, self.cols = shape[2] // GROUP, shape[3] // n
        elif kind == "up":
            self.rows, self.cols = shape[1] // GROUP, shape[2] // n
        else:
            self.rows, self.cols = shape[1] // n // GROUP, shape[2]

    def piece(self, i, q):
        r, c = self.rows, self.cols
        if self.kind == "in":
            return self.whole.at[self.layer, :, pl.ds(i * r, r), pl.ds(q * c, c)]
        if self.kind == "up":
            return self.whole.at[self.layer, pl.ds(i * r, r), pl.ds(q * c, c)]
        return self.whole.at[self.layer, pl.ds((q * GROUP + i) * r, r), :]

    def shard(self, q):
        r, c = self.rows, self.cols
        if self.kind == "in":
            return self.whole.at[self.layer, :, :, pl.ds(q * c, c)]
        if self.kind == "up":
            return self.whole.at[self.layer, :, pl.ds(q * c, c)]
        return self.whole.at[self.layer, pl.ds(q * GROUP * r, GROUP * r), :]

    def local_piece(self, shard, i):
        r = self.rows
        if self.kind == "in":
            return shard.at[self.layer, :, pl.ds(i * r, r), :]
        return shard.at[self.layer, pl.ds(i * r, r), :]

    def span(self, members):
        r, c, k = self.rows, self.cols, self.n - 1
        if self.kind == "in":
            return self.whole.at[self.layer, :, pl.ds(0, members * r), pl.ds(0, k * c)]
        if self.kind == "up":
            return self.whole.at[self.layer, pl.ds(0, members * r), pl.ds(0, k * c)]
        return self.whole.at[self.layer, pl.ds(0, members * k * r), :]


class Gather:
    def __init__(self, place, weight, shard, sems, slot, order):
        self.p, self.w, self.shard_ref, self.sems, self.slot, self.order = place, weight, shard, sems, slot, order

    def sem(self, k):
        return self.sems.at[self.slot, k]

    def own(self):
        return pltpu.make_async_copy(
            self.shard_ref.at[self.w.layer], self.w.shard(self.p.q), self.sem(8)
        )

    def start(self):
        p, w = self.p, self.w
        for k in range(1, p.n):
            send(w.local_piece(self.shard_ref, p.i), w.piece(p.i, p.q), self.sem(0), self.sem(1), p.column(k)[1])
        self.own().start()

    def pass_on(self, i, send_sem, recv_sem, peer):
        p, w = self.p, self.w
        for k in range(1, p.n):
            piece = w.piece(i, p.column(k)[0])
            send(piece, piece, send_sem, recv_sem, peer)

    def hop1(self):
        p = self.p
        await_bytes(self.w.span(1), self.sem(1))
        first, second = p.mates(self.order)
        self.pass_on(p.i, self.sem(2), self.sem(3), first[1])
        self.pass_on(p.i, self.sem(4), self.sem(5), second[1])

    def hop2(self):
        first, second = self.p.mates(self.order)
        await_bytes(self.w.span(1), self.sem(3))
        self.pass_on(first[0], self.sem(4), self.sem(5), second[1])

    def hop3(self):
        p = self.p
        await_bytes(self.w.span(2), self.sem(5))
        for i in (p.i, p.mate_x()[0], p.mate_y()[0], p.mate_xy()[0]):
            self.pass_on(i, self.sem(6), self.sem(7), p.sibling())

    def arrive(self):
        self.own().wait()
        await_bytes(self.w.span(4), self.sem(7))

    def finish(self):
        await_bytes(self.w.span(1), self.sem(0))
        await_bytes(self.w.span(1), self.sem(2))
        await_bytes(self.w.span(2), self.sem(4))
        await_bytes(self.w.span(4), self.sem(6))


def norm_strip(v, gain, bias):
    centred = v - jnp.mean(v, axis=-1, keepdims=True)
    variance = jnp.mean(centred * centred, axis=-1, keepdims=True)
    return centred * lax.rsqrt(variance + EPSILON) * gain + bias


def norm_all(src, dst, gain, bias):
    def strip(j):
        r = rows_of(j, 128)
        dst[r, :] = norm_strip(src[r, :], gain, bias).astype(BF)

    loop(dst.shape[0] // 128, strip)


def normal_taps(sub_ref, scale_ref, layer):
    raw = sub_ref[layer] * scale_ref[0]
    total = jnp.sum(raw * raw * scale_ref[1], axis=0, keepdims=True)
    return raw, lax.rsqrt(total + EPSILON)


def make_masks(seg_rows, masks):
    quarter, channels = masks.shape[1:]
    ones = jnp.full((8, channels), 0.125, BF)

    def numbers(n):
        return dot_tn(seg_rows[:, n * quarter : (n + 1) * quarter].astype(BF), ones)

    def put(k, flag):
        masks[k] = jnp.where(flag, 1.0, 0.0).astype(BF)

    long_doc = numbers(1)[0:1, :]
    for n in range(4):
        here = numbers(n)
        put(n, here == long_doc)
        if n in (0, 3):
            for k in range(3):
                doc = jnp.where(long_doc <= k, k + 1.0, float(k))
                put(4 + 2 * k + (n == 3), here == doc)


def make_windows(taps, tap_ref, spec, layer, wins):
    channels = taps.shape[1]
    quarter = wins.shape[3]
    for m in range(4):
        spec[:, m * channels : (m + 1) * channels] = dot(tap_ref[m], taps)

    def strip(j):
        r = rows_of(j, 16)
        s = rows_of(j + quarter // 16, 16)
        sign = (1 - 2 * lax.rem(lax.broadcasted_iota(jnp.int32, (16, channels), 0), 2)).astype(F32)
        for m in range(4):
            here = slice(m * channels, (m + 1) * channels)
            re, im = spec[r, here], spec[s, here]
            if m:
                before = slice((m - 1) * channels, m * channels)
                re, im = re - sign * spec[s, before], im + sign * spec[r, before]
            wins[layer, m, 0, r, :] = re
            wins[layer, m, 1, r, :] = im

    loop(quarter // 16, strip)


def spread_blocks(blocks, masks, out):
    channels = masks.shape[2]
    for n in range(4):
        out[:, n * channels : (n + 1) * channels] = blocks[n] * masks[n]
    for k in range(3):
        out[:, (4 + k) * channels : (5 + k) * channels] = (
            blocks[0] * masks[4 + 2 * k] + blocks[3] * masks[5 + 2 * k]
        )


def join_blocks(parts, r, masks, n):
    channels = masks.shape[2]
    total = parts[:, n * channels : (n + 1) * channels] * masks[n, r, :].astype(F32)
    if n in (0, 3):
        for k in range(3):
            mask = masks[4 + 2 * k + (n == 3), r, :].astype(F32)
            total += parts[:, (4 + k) * channels : (5 + k) * channels] * mask
    return total


def fwd_products(spec, wins, layer, out, channels):
    quarter = wins.shape[3]

    def strip(j):
        r = rows_of(j, 16)
        s = rows_of(j + quarter // 16, 16)
        xs = [(spec[r, n * channels : (n + 1) * channels], spec[s, n * channels : (n + 1) * channels]) for n in range(7)]
        ws = [(wins[layer, m, 0, r, :], wins[layer, m, 1, r, :]) for m in range(4)]
        for n in range(7):
            re = im = None
            for m in range(n + 1 if n < 4 else 1):
                w, x = ws[m], xs[n - m]
                a = w[0] * x[0] - w[1] * x[1]
                b = w[0] * x[1] + w[1] * x[0]
                re, im = (a, b) if re is None else (re + a, im + b)
            out[r, n * channels : (n + 1) * channels] = re.astype(BF)
            out[s, n * channels : (n + 1) * channels] = im.astype(BF)

    loop(quarter // 16, strip)


FORWARD_PLAN = {
    (0, "start"): ("u0.start", "i0.hop1"),
    (0, "ready"): ("tok.pass_on", "i0.hop2", "i0.hop3"),
    (0, "project"): ("o0.start", "d0.start"),
    (0, "sent"): ("i1.start",),
    (0, "gate"): ("seg.pass_on",),
    (0, "came"): ("o1.start", "u1.start", "u0.hop1"),
    (0, "transform"): ("o0.hop1",),
    (0, "returned"): ("u0.hop2", "o0.hop2", "d0.hop1"),
    (0, "back"): ("u0.hop3", "i1.hop1", "cot.start", "o0.hop3"),
    (0, "attach"): ("d0.hop2",),
    (0, "norm"): ("i1.hop2",),
    (0, "widen"): ("u1.hop1",),
    (0, "activate"): ("d0.hop3", "i1.hop3"),
    (0, "narrow"): ("d1.start", "o1.hop1", "u1.hop2"),
    (1, "sent"): ("o1.hop2", "u1.hop3", "d1.hop1", "cot.pass_on"),
    (1, "gate"): ("o1.hop3",),
    (1, "returned"): ("d1.hop2", "d1.hop3"),
}


def forward_kernel(
    n, layers,
    stream_in, segs, gains, biases, subs, scales, cot_h, table_h, table_t_h, tap_table_h, win, wout, wup, wdn,
    out_o, streams_o, hidden_o, gact_o, gslope_o, conv_in_o, conv_out_o, gated_o, middle_o, hidden_mid_o, active_o, slope_o,
    wins_o, masks_o, cot_o, win_o, wout_o, wup_o, wdn_o,
    stream, hidden, gact, gslope, gated, middle, hidden_mid, active, slope, send_a, recv_a, send_b, recv_b,
    spread, spec, spec_y, wins, win_f, wout_f, wup_f, wdn_f,
    masks, tok_s, tok_r, tok_p, cot_in, cot_s, cot_p, seg_s, seg_r, seg_p, taps_s, taps_r, table, table_t, tap_table,
    gather_sems, a2a_sems, save_sems, move_sems, tap_sems, load_sems,
):
    place = Place(n)
    me = place.s
    tokens, width = stream_in.shape
    channels = width // n
    quarter = tokens
    half = wup_f.shape[2] // 2
    loads = [
        pltpu.make_async_copy(src, dst, load_sems.at[k])
        for k, (src, dst) in enumerate(((cot_h, cot_in), (tap_table_h, tap_table), (table_h, table), (table_t_h, table_t)))
    ]
    for copy in loads:
        copy.start()
    greet_all(place)
    saves = []

    def save(src, dst, l=None):
        if l is not None:
            src, dst = src.at[l], dst.at[l]
        copy = pltpu.make_async_copy(src, dst, save_sems.at[len(saves)])
        copy.start()
        saves.append(copy)

    def exchange_start(slot, src, dst, layer):
        for k in range(1, n):
            s, peer = place.partner(k)
            send(src.at[layer, s], dst.at[layer, me], a2a_sems.at[slot, 0], a2a_sems.at[slot, 1], peer)

    def exchange_wait(slot, src, dst, layer):
        await_bytes(src.at[layer, pl.ds(0, n - 1)], a2a_sems.at[slot, 0])
        await_bytes(dst.at[layer, pl.ds(0, n - 1)], a2a_sems.at[slot, 1])

    moving = {
        "seg": Move(place, seg_s, seg_r, seg_p, move_sems.at[0]),
        "tok": Move(place, tok_s, tok_r, tok_p, move_sems.at[1]),
        "cot": Move(place, cot_s, cot_o, cot_p, move_sems.at[2]),
    }
    gathers = {}
    for l in range(layers):
        for kind, whole, shard in (("in", win_f, win), ("out", wout_f, wout), ("up", wup_f, wup), ("down", wdn_f, wdn)):
            gathers[kind[0] + str(l)] = Gather(place, Weight(whole, l, kind, n), shard, gather_sems, len(gathers), "xy")
    moving.update(gathers)

    def visit(l, point):
        for step in FORWARD_PLAN.get((l, point), ()):
            what, action = step.split(".")
            getattr(moving[what], action)()

    gathers["i0"].start()

    def round_stream(j):
        r = rows_of(j, 64)
        tok_s[r, :] = stream_in[r, :].astype(BF)

    loop(tokens // 64, round_stream)
    moving["tok"].start()
    seg_s[...] = jnp.broadcast_to(segs[...].astype(F32), seg_s.shape)
    moving["seg"].start()
    for l in range(layers):
        raw, inverse = normal_taps(subs, scales, l)
        taps_s[l] = (raw * inverse).astype(BF)

    def give_taps():
        for k in range(1, n):
            send(taps_s, taps_r, tap_sems.at[0, k], tap_sems.at[1, k], place.column(k)[1])
        taps_r[...] = taps_s[...]

    def take_taps():
        ahead = lax.rem(place.q - place.s + n, n)
        await_bytes(taps_r, tap_sems.at[1, ahead])

    when(place.s == place.q, give_taps)
    loads[0].wait()

    def round_cotangent(j):
        r = rows_of(j, 64)
        cot_s[r, :] = cot_in[r, :].astype(BF)

    loop(tokens // 64, round_cotangent)
    visit(0, "start")
    visit(0, "ready")
    moving["tok"].arrive()

    def widen_stream(j):
        r = rows_of(j, 64)
        stream[0, r, :] = tok_r[r, :].astype(F32)

    loop(tokens // 64, widen_stream)
    save(stream, streams_o, 0)

    for l in range(layers):
        norm_all(stream.at[l], hidden.at[l], gains[l, 0:1, :], biases[l, 0:1, :])
        gathers["i" + str(l)].arrive()
        got = dot(hidden[l], win_f[l, 0]).astype(BF)
        for s in range(n):
            send_a[l, s] = got[:, s * channels : (s + 1) * channels]
        visit(l, "project")
        exchange_start(2 * l, send_a, recv_a, l)
        recv_a[l, me] = send_a[l, me]
        visit(l, "sent")
        save(hidden, hidden_o, l)
        save(win_f, win_o, l)
        spec[0:tokens, 0:width] = dot(hidden[l], win_f[l, 1])

        def open_gate(j):
            r = rows_of(j, 16)
            act, incline = gelu_both(spec[r, 0:width])
            gact[l, r, :] = act.astype(BF)
            gslope[l, r, :] = incline.astype(BF)

        loop(tokens // 16, open_gate)
        visit(l, "gate")
        save(gact, gact_o, l)
        save(gslope, gslope_o, l)
        if l == 0:
            moving["seg"].arrive()
            make_masks(seg_r, masks)
            save(masks, masks_o)
            when(place.s != place.q, take_taps)
            loads[1].wait()
            for m in range(layers):
                make_windows(taps_r[m], tap_table, spec, m, wins)
            save(wins, wins_o)
            loads[2].wait()
            loads[3].wait()
        exchange_wait(2 * l, send_a, recv_a, l)
        visit(l, "came")
        save(recv_a, conv_in_o, l)
        spread_blocks(recv_a.at[l], masks, spread)
        spec[:, 0 : 7 * channels] = dot(table[...], spread[...])
        visit(l, "transform")
        fwd_products(spec, wins, l, spec_y, channels)

        def untransform(j):
            r = rows_of(j, 256)
            parts = dot(table_t[r, :], spec_y[...])
            for s in range(n):
                send_b[l, s, r, :] = join_blocks(parts, r, masks, s).astype(BF)

        loop(quarter // 256, untransform)
        exchange_start(2 * l + 1, send_b, recv_b, l)
        recv_b[l, me] = send_b[l, me]
        visit(l, "returned")
        exchange_wait(2 * l + 1, send_b, recv_b, l)
        visit(l, "back")
        save(recv_b, conv_out_o, l)

        def mix(j):
            r = rows_of(j, 64)
            for s in range(n):
                c = slice(s * channels, (s + 1) * channels)
                gated[l, r, c] = (gact[l, r, c].astype(F32) * recv_b[l, s, r, :].astype(F32)).astype(BF)

        loop(tokens // 64, mix)
        gathers["o" + str(l)].arrive()
        save(gated, gated_o, l)
        save(wout_f, wout_o, l)
        middle[l] = stream[l] + dot(gated[l], wout_f[l])
        visit(l, "attach")
        save(middle, middle_o, l)
        norm_all(middle.at[l], hidden_mid.at[l], gains[l, 1:2, :], biases[l, 1:2, :])
        visit(l, "norm")
        gathers["u" + str(l)].arrive()
        save(hidden_mid, hidden_mid_o, l)
        save(wup_f, wup_o, l)
        for h in range(2):
            spec[h * tokens : (h + 1) * tokens, :] = dot(hidden_mid[l], wup_f[l, :, h * half : (h + 1) * half])
        visit(l, "widen")

        def activate(j):
            r = rows_of(j, 16)
            for h in range(2):
                t = pl.ds(pl.multiple_of(h * tokens + j * 16, 16), 16)
                act, incline = gelu_both(spec[t, :])
                active[l, r, h * half : (h + 1) * half] = act.astype(BF)
                slope[l, r, h * half : (h + 1) * half] = incline.astype(BF)

        loop(tokens // 16, activate)
        visit(l, "activate")
        save(active, active_o, l)
        save(slope, slope_o, l)
        gathers["d" + str(l)].arrive()
        save(wdn_f, wdn_o, l)
        if l + 1 < layers:
            stream[l + 1] = middle[l] + dot(active[l], wdn_f[l])
            save(stream, streams_o, l + 1)
        else:
            moving["tok"].finish()
            tok_s[...] = (middle[l] + dot(active[l], wdn_f[l])).astype(BF)
            save(tok_s, out_o)
        visit(l, "narrow")
    for g in gathers.values():
        g.finish()
    moving["cot"].arrive()
    for name in ("seg", "cot"):
        moving[name].finish()

    def taps_given():
        for k in range(1, n):
            await_bytes(taps_s, tap_sems.at[0, k])

    when(place.s == place.q, taps_given)
    for copy in saves:
        copy.wait()


def forward(n, stream_in, cotangent, segments, gains, biases, subs, scales, table, table_t, tap_table, win, wout, wup, wdn):
    layers = win.shape[0]
    tokens, width = stream_in.shape
    channels = width // n
    ff = wup.shape[2] * n
    taps = subs.shape[1]

    def sds(*shape, dtype=BF):
        return jax.ShapeDtypeStruct(shape, dtype)

    wshapes = [(layers, 2, width, width), (layers, width, width), (layers, width, ff), (layers, ff, width)]
    wide, blocks = (layers, tokens, width), (layers, n, tokens, channels)
    outs = [
        sds(tokens, width), sds(*wide, dtype=F32), sds(*wide), sds(*wide), sds(*wide), sds(*blocks), sds(*blocks), sds(*wide),
        sds(*wide, dtype=F32), sds(*wide), sds(layers, tokens, ff), sds(layers, tokens, ff),
        sds(layers, 4, 2, tokens, channels, dtype=F32), sds(10, tokens, channels), sds(tokens, width),
    ] + [sds(*s) for s in wshapes]
    f32 = lambda *s: pltpu.VMEM(s, F32)
    bf = lambda *s: pltpu.VMEM(s, BF)
    scratch = [
        f32(*wide), bf(*wide), bf(*wide), bf(*wide), bf(*wide), f32(*wide), bf(*wide), bf(layers, tokens, ff), bf(layers, tokens, ff),
        bf(*blocks), bf(*blocks), bf(*blocks), bf(*blocks),
        bf(tokens, 7 * channels), f32(2 * tokens, ff // 2), bf(2 * tokens, 7 * channels), f32(layers, 4, 2, tokens, channels),
    ] + [bf(*s) for s in wshapes] + [
        bf(10, tokens, channels), bf(tokens, width), bf(tokens, width), bf(tokens, width), f32(tokens, width), bf(tokens, width), bf(tokens, width),
        f32(8, 4 * tokens), f32(8, 4 * tokens), f32(8, 4 * tokens), bf(layers, taps, channels), bf(layers, taps, channels),
        bf(2 * tokens, tokens), bf(tokens, 2 * tokens), bf(4, 2 * tokens, taps),
        pltpu.SemaphoreType.DMA((4 * layers, 9)),
        pltpu.SemaphoreType.DMA((2 * layers, 2)),
        pltpu.SemaphoreType.DMA((15 * layers + 3,)),
        pltpu.SemaphoreType.DMA((3, 4)),
        pltpu.SemaphoreType.DMA((2, n)),
        pltpu.SemaphoreType.DMA((4,)),
    ]
    return pl.pallas_call(
        functools.partial(forward_kernel, n, layers),
        out_shape=outs,
        in_specs=[VMEM] * 6 + [ANY] * 8,
        out_specs=[ANY] * len(outs),
        scratch_shapes=scratch,
        compiler_params=pltpu.CompilerParams(collective_id=1, has_side_effects=True, vmem_limit_bytes=60 * 2**20),
        name="forward",
    )(stream_in, segments, gains, biases, subs, scales, cotangent, table, table_t, tap_table, win, wout, wup, wdn)


PIECE_DOWN, PIECE_UP, PIECE_OUT, PIECE_IN, PIECE_ROWS = 0, 64, 128, 144, 176


def norm_back(upstream, src, base, gain, out, rounded):
    width = src.shape[1]

    def strip(j, sums):
        r = rows_of(j, 128)
        v = src[r, :]
        centred = v - jnp.mean(v, axis=-1, keepdims=True)
        inverse = lax.rsqrt(jnp.mean(centred * centred, axis=-1, keepdims=True) + EPSILON)
        xhat = centred * inverse
        up = upstream[r, :]
        q = gain * up
        both = q - jnp.mean(q, axis=-1, keepdims=True) - xhat * jnp.mean(q * xhat, axis=-1, keepdims=True)
        got = base[r, :] + both * inverse
        out[r, :] = got
        if rounded is not None:
            rounded[r, :] = got.astype(BF)
        p = up * xhat
        first, second = sums
        for k in range(0, 128, 8):
            first, second = first + p[k : k + 8], second + up[k : k + 8]
        return first, second

    zero = jnp.zeros((8, width), F32)
    return lax.fori_loop(0, src.shape[0] // 128, strip, (zero, zero))


def back_products(spec_x, spec_c, wins, out_g, out_d, channels):
    quarter = wins.shape[2]
    half = out_g.shape[1] // 2

    def strip(j):
        r = rows_of(j, 16)
        s = rows_of(j + quarter // 16, 16)
        cols = [slice(n * channels, (n + 1) * channels) for n in range(7)]
        cols2 = [slice(half + n * channels, half + (n + 1) * channels) for n in range(7)]
        cs = [(spec_c[r, c], spec_c[s, c]) for c in cols]
        for n in range(7):
            re = im = None
            for m in range(4 - n if n < 4 else 1):
                w, x = (wins[m, 0, r, :], wins[m, 1, r, :]), cs[n + m]
                a = w[0] * x[0] + w[1] * x[1]
                b = w[0] * x[1] - w[1] * x[0]
                re, im = (a, b) if re is None else (re + a, im + b)
            out_g[r, cols[n]] = re.astype(BF)
            out_g[r, cols2[n]] = im.astype(BF)
        sign = (1 - 2 * lax.rem(lax.broadcasted_iota(jnp.int32, (16, channels), 0), 2)).astype(F32)
        later = None
        for m in (3, 2, 1, 0):
            pairs = [(n - m, n) for n in range(m, 4)] + ([(n, n) for n in range(4, 7)] if m == 0 else [])
            re = im = None
            for i, n in pairs:
                x, c = (spec_x[r, cols[i]], spec_x[s, cols[i]]), cs[n]
                a = x[0] * c[0] + x[1] * c[1]
                b = x[0] * c[1] - x[1] * c[0]
                re, im = (a, b) if re is None else (re + a, im + b)
            dre, dim = (re, im) if later is None else (re + sign * later[1], im - sign * later[0])
            later = (re, im)
            out_d[r, cols[m]] = dre.astype(BF)
            out_d[r, cols2[m]] = dim.astype(BF)

    loop(quarter // 16, strip)


class Reduce:
    def __init__(self, place, bufs, sems, slot, layer, first, rows, order):
        self.p, self.layer, self.slot, self.sems, self.order = place, layer, slot, sems, order
        self.r = pl.ds(first, rows)
        self.first, self.rows = first, rows
        self.grads, self.r0, self.r1, self.r2, self.res = bufs
        self.spare = self.grads.shape[0] - 1

    def sem(self, k):
        return self.sems.at[self.slot, k]

    def strips(self, body):
        step = next(s for s in (80, 64, 32, 16) if self.rows % s == 0)
        loop(self.rows // step, lambda j: body(pl.ds(pl.multiple_of(self.first + j * step, 16), step)))

    def add_to(self, place_of, others, r):
        total = self.grads[(self.layer, *place_of, r, slice(None))].astype(F32)
        for other in others:
            total += other[r, :].astype(F32)
        return total

    def s0(self):
        send(self.grads.at[self.spare, :, :, :, self.r], self.r0.at[self.layer, :, :, :, self.r], self.sem(0), self.sem(1), self.p.sibling())

    def s1(self):
        p, l = self.p, self.layer
        await_bytes(self.r0.at[l, :, :, :, self.r], self.sem(0))
        await_bytes(self.r0.at[l, :, :, :, self.r], self.sem(1))

        def add(j):
            y, x, q = j // (2 * p.n), lax.rem(j // p.n, 2), lax.rem(j, p.n)

            def strip(r):
                self.grads[l, y, x, q, r, :] = self.add_to((y, x, q), [self.r0.at[l, y, x, q]], r).astype(BF)

            self.strips(strip)

        loop(4 * p.n, add)
        if self.order == "yx":
            send(self.grads.at[l, 1 - p.y, :, :, self.r], self.r1.at[l, pl.ds(0, 2), :, self.r], self.sem(2), self.sem(3), p.mate_y()[1])
        elif self.order == "xy":
            send(self.grads.at[l, :, 1 - p.x, :, self.r], self.r1.at[l, pl.ds(0, 2), :, self.r], self.sem(2), self.sem(3), p.mate_x()[1])
        else:
            send(self.grads.at[l, p.y, 1 - p.x, :, self.r], self.r1.at[l, 0, :, self.r], self.sem(2), self.sem(3), p.mate_x()[1])
            send(self.grads.at[l, 1 - p.y, p.x, :, self.r], self.r1.at[l, 1, :, self.r], self.sem(2), self.sem(3), p.mate_y()[1])
            send(self.grads.at[l, 1 - p.y, 1 - p.x, :, self.r], self.r1.at[l, 2, :, self.r], self.sem(2), self.sem(3), p.mate_xy()[1])

    def s1b(self):
        p, l = self.p, self.layer
        both = self.r1.at[l, pl.ds(0, 2), :, self.r]
        await_bytes(both, self.sem(2))
        await_bytes(both, self.sem(3))

        def add(j):
            k, q = j // p.n, lax.rem(j, p.n)
            y, x = (p.y, k) if self.order == "yx" else (k, p.x)

            def strip(r):
                self.grads[l, y, x, q, r, :] = self.add_to((y, x, q), [self.r1.at[l, k, q]], r).astype(BF)

            self.strips(strip)

        loop(2 * p.n, add)
        if self.order == "yx":
            send(self.grads.at[l, p.y, 1 - p.x, :, self.r], self.r1.at[l, 2, :, self.r], self.sem(4), self.sem(5), p.mate_x()[1])
        else:
            send(self.grads.at[l, 1 - p.y, p.x, :, self.r], self.r1.at[l, 2, :, self.r], self.sem(4), self.sem(5), p.mate_y()[1])

    def s2(self):
        p, l = self.p, self.layer
        if self.order == "direct":
            slots = (0, 1, 2)
            await_bytes(self.r1.at[l, :, :, self.r], self.sem(2))
            await_bytes(self.r1.at[l, :, :, self.r], self.sem(3))
        else:
            slots = (2,)
            await_bytes(self.r1.at[l, 2, :, self.r], self.sem(4))
            await_bytes(self.r1.at[l, 2, :, self.r], self.sem(5))

        def add(q):
            def strip(r):
                self.grads[l, p.y, p.x, q, r, :] = self.add_to((p.y, p.x, q), [self.r1.at[l, k, q] for k in slots], r).astype(BF)

            self.strips(strip)

        loop(p.n, add)
        for k in range(1, p.n):
            q, peer = p.column(k)
            send(self.grads.at[l, p.y, p.x, q, self.r], self.r2.at[l, k - 1, self.r], self.sem(6), self.sem(7), peer)

    def s3(self):
        p, l = self.p, self.layer
        await_bytes(self.r2.at[l, :, self.r], self.sem(6))
        await_bytes(self.r2.at[l, :, self.r], self.sem(7))

        def strip(r):
            total = self.add_to((p.y, p.x, p.q), [self.r2.at[l, k] for k in range(p.n - 1)], r)
            self.res[l, p.i, r, :] = total.astype(BF)

        self.strips(strip)
        piece = self.res.at[l, p.i, self.r]
        for mate in (p.mate_x(), p.mate_y(), p.mate_xy()):
            send(piece, piece, self.sem(8), self.sem(9), mate[1])

    def s4(self):
        p, l = self.p, self.layer
        await_bytes(self.res.at[l, pl.ds(0, 3), self.r], self.sem(9))
        for i in (p.i, p.mate_x()[0], p.mate_y()[0], p.mate_xy()[0]):
            piece = self.res.at[l, i, self.r]
            send(piece, piece, self.sem(10), self.sem(11), p.sibling())

    def end(self):
        half = self.res.at[self.layer, pl.ds(0, GROUP // 2), self.r]
        await_bytes(self.res.at[self.layer, pl.ds(0, 3), self.r], self.sem(8))
        await_bytes(half, self.sem(10))
        await_bytes(half, self.sem(11))


def in_order(own, others, l, here, count):
    total = None
    for j in range(count):
        k = lax.rem(here - j + count, count)
        value = jnp.where(k == 0, own.astype(F32), others[l, lax.max(k - 1, 0)].astype(F32))
        total = value if total is None else total + value
    return total


BACKWARD_ORDER = {"d1": "yx", "u1": "direct", "i1": "yx", "d0": "yx", "u0": "yx", "i0": "yx"}
BACKWARD_PLAN = {
    (1, "sent"): ("d1.s1",),
    (1, "out"): ("o1.s1",),
    (1, "returned"): ("u1.s1",),
    (1, "project"): ("kg1.over_mp",),
    (0, "narrow"): ("d1.s1b",),
    (0, "down"): ("i1.s1",),
    (0, "sent"): ("u0.s1",),
    (0, "out"): ("o0.s1", "d1.s2", "i1.s1b", "d0.s1"),
    (0, "transform"): ("out.pass_on",),
    (0, "returned"): ("u1.s2", "kg0.over_mp"),
    (0, "in"): ("i1.s2", "u0.s1b"),
    (0, "end"): ("d1.s3", "i0.s1", "d0.s1b"),
    (0, "tail"): (
        "u0.s2", "u1.s3", "grad.pass_on", "kg0.over_y", "i1.s3", "d1.s4", "d0.s2", "o1.s2", "i0.s1b", "o0.s2", "u0.s3", "d0.s3",
        "i0.s2", "kg0.take", "norm.over_mp", "o0.s3", "o1.s3", "u0.s4", "u1.s4", "i0.s3", "d0.s4", "i1.s4", "o0.s4", "kg1.over_y",
        "o1.s4", "i0.s4", "norm.take", "kg1.take",
    ),
}


class KernelGrad:
    def __init__(self, place, layer, refs, sems):
        self.p, self.l, self.sems = place, layer, sems
        self.own, self.from_mp, self.mid, self.from_y, self.total, self.result = [r.at[layer] for r in refs]
        self.owner = place.s == place.q

    def sem(self, k):
        return self.sems.at[self.l, k]

    def start(self):
        p = self.p
        k = lax.rem(p.q - p.s + p.n, p.n)
        when(
            jnp.logical_not(self.owner),
            lambda: send(self.own, self.from_mp.at[lax.max(k - 1, 0)], self.sem(0), self.sem(1 + k), p.device(p.i, p.s)),
        )

    def over_mp(self):
        p = self.p

        def add():
            total = self.own[...].astype(F32)
            for k in range(1, p.n):
                await_bytes(self.from_mp.at[k - 1], self.sem(1 + k))
                total += self.from_mp[k - 1].astype(F32)
            self.mid[...] = total.astype(BF)
            send(self.mid, self.from_y, self.sem(5), self.sem(6), p.mate_y()[1])

        when(self.owner, add)

    def over_y(self):
        p = self.p

        def add():
            await_bytes(self.from_y, self.sem(6))
            both = (self.mid[...].astype(F32) + self.from_y[...].astype(F32)).astype(BF)
            self.total[...] = both
            self.result[...] = both
            for k in range(1, p.n):
                send(self.total, self.result, self.sem(6 + k), self.sem(9 + k), p.partner(k)[1])

        when(self.owner, add)

    def take(self):
        p = self.p
        k = lax.rem(p.s - p.q + p.n, p.n)
        when(jnp.logical_not(self.owner), lambda: await_bytes(self.result, self.sem(9 + k)))

    def finish(self):
        def given():
            await_bytes(self.mid, self.sem(5))
            for k in range(1, self.p.n):
                await_bytes(self.total, self.sem(6 + k))

        when(self.owner, given)
        when(jnp.logical_not(self.owner), lambda: await_bytes(self.own, self.sem(0)))


class NormGrad:
    def __init__(self, place, refs, sems):
        self.p, self.sems = place, sems
        self.own, self.from_group, self.mid, self.from_mp, self.result = refs
        self.layers = self.own.shape[0]

    def start(self, l):
        for k in range(1, GROUP):
            send(self.own.at[l], self.from_group.at[l, k - 1], self.sems.at[l, 0], self.sems.at[l, 1], self.p.member(k))

    def over_mp(self):
        p = self.p
        for l in reversed(range(self.layers)):
            await_bytes(self.from_group.at[l], self.sems.at[l, 0])
            await_bytes(self.from_group.at[l], self.sems.at[l, 1])
            self.mid[l] = in_order(self.own[l], self.from_group, l, p.i, GROUP)
            for k in range(1, p.n):
                send(self.mid.at[l], self.from_mp.at[l, k - 1], self.sems.at[l, 2], self.sems.at[l, 3], p.column(k)[1])

    def take(self):
        for l in reversed(range(self.layers)):
            await_bytes(self.from_mp.at[l], self.sems.at[l, 2])
            await_bytes(self.from_mp.at[l], self.sems.at[l, 3])
            self.result[l] = in_order(self.mid[l], self.from_mp, l, self.p.q, self.p.n)


def backward_kernel(
    n, layers,
    gains, subs, scales, masks_h, table_h, table_t_h, tap_t_h,
    out_in, cot, streams, hiddens, gacts, gslopes, conv_ins, conv_outs, gateds, middles, hidden_mids, actives, slopes,
    wins_h, win_h, wout_h, wup_h, wdn_h,
    out_o, grad_o, res_o, sub_o, norm_o, out_p, grad_p,
    grad, middle_grad, stream, hidden, gact, gslope, conv_in, conv_out, gated, middle, hidden_mid, active, slope, wins, win, wout, wup, wdn,
    grads, r0, r1, r2, res,
    up_grad, out_grad, branch, joined, big_a, big_b, spread,
    send_c, recv_c, send_d, recv_d, kg_s, kg_z, kg_t, kg_y, kg_u, kg_own, sub_s, masks, table, table_t, tap_t,
    norm_s, norm_r, norm_t, norm_u, norm_v,
    load_sems, a2a_sems, red_sems, kg_sems, norm_sems, out_sems, move_sems,
):
    place = Place(n)
    me, core = place.s, place.core
    tokens, width = grad.shape
    channels = width // n
    quarter = tokens
    ff = wup.shape[1]
    half = ff // 2
    spare = grads.shape[0] - 1
    loads = {}
    sources = {
        "stream": (streams, stream), "hidden": (hiddens, hidden), "gact": (gacts, gact), "gslope": (gslopes, gslope),
        "conv_in": (conv_ins, conv_in), "conv_out": (conv_outs, conv_out), "gated": (gateds, gated), "middle": (middles, middle),
        "hidden_mid": (hidden_mids, hidden_mid), "active": (actives, active), "slope": (slopes, slope), "wins": (wins_h, wins),
        "in": (win_h, win), "out": (wout_h, wout), "up": (wup_h, wup), "down": (wdn_h, wdn),
        "branch": (cot, branch), "masks": (masks_h, masks), "table": (table_h, table), "table_t": (table_t_h, table_t), "tap_t": (tap_t_h, tap_t),
    }
    once = ("branch", "masks", "table", "table_t", "tap_t")

    def load(name, l):
        src, dst = sources[name]
        copy = pltpu.make_async_copy(src if name in once else src.at[l], dst, load_sems.at[l, len([k for k in loads if k[1] == l])])
        copy.start()
        loads[name, l] = copy

    def ready(*names, l):
        for name in names:
            loads[name, l].wait()

    def next_load(*names, l):
        if l:
            for name in names:
                load(name, l - 1)

    top = layers - 1
    for name in (
        "branch", "down", "slope", "up", "active", "hidden_mid", "middle", "out", "gact", "gslope", "conv_out", "gated", "masks",
        "conv_in", "table", "wins", "table_t", "tap_t", "in", "hidden", "stream",
    ):
        load(name, top)
    greet_all(place)
    bufs = (grads, r0, r1, r2, res)
    bounds = (PIECE_DOWN, PIECE_UP, PIECE_OUT, PIECE_IN, PIECE_ROWS)
    groups = {}
    for l in range(layers):
        for k, letter in enumerate("duoi"):
            name = letter + str(l)
            order = BACKWARD_ORDER.get(name, "direct")
            groups[name] = Reduce(place, bufs, red_sems, len(groups), l, bounds[k], bounds[k + 1] - bounds[k], order)
    kernel_grads = [KernelGrad(place, l, (kg_s, kg_z, kg_t, kg_y, kg_u, kg_own), kg_sems) for l in range(layers)]
    norm_grads = NormGrad(place, (norm_s, norm_r, norm_t, norm_u, norm_v), norm_sems)
    out_move = Move(place, out_in, out_o, out_p, move_sems.at[0])
    grad_move = Move(place, branch, grad_o, grad_p, move_sems.at[1])
    moving = {"out": out_move, "grad": grad_move, "norm": norm_grads, **groups}
    moving.update({"kg" + str(l): kernel_grads[l] for l in range(layers)})

    def visit(l, point):
        for step in BACKWARD_PLAN.get((l, point), ()):
            what, action = step.split(".")
            getattr(moving[what], action)()

    def exchange_start(slot, src, dst, l):
        for k in range(1, n):
            s, peer = place.partner(k)
            send(src.at[s], dst.at[me], a2a_sems.at[slot, 0], a2a_sems.at[slot, 1], peer)

    def exchange_wait(slot, src, dst, l):
        await_bytes(src.at[pl.ds(0, n - 1)], a2a_sems.at[slot, 0])
        await_bytes(dst.at[pl.ds(0, n - 1)], a2a_sems.at[slot, 1])

    def holder(parity, l):
        mine = 1 - (parity - core) * (parity - core)
        return l * mine + spare * (1 - mine)

    out_move.start()
    ready("branch", l=top)

    def widen_grad(j):
        r = rows_of(j, 64)
        grad[r, :] = branch[r, :].astype(F32)

    loop(tokens // 64, widen_grad)

    for l in reversed(range(layers)):
        ready("down", "slope", l=l)
        for h in range(2):
            c = slice(h * half, (h + 1) * half)
            big_b[0:tokens, :] = dot_nt(branch[...], wdn[c, :])

            def activate(k):
                s = rows_of(k, 32)
                up_grad[s, c] = (big_b[s, :] * slope[s, c].astype(F32)).astype(BF)

            loop(tokens // 32, activate)
        next_load("down", "slope", l=l)
        visit(l, "activate")
        ready("up", "hidden_mid", "active", l=l)
        big_a[0:tokens, 0:width] = dot_nt(up_grad[...], wup[...])
        next_load("up", l=l)
        visit(l, "narrow")

        def grad_up(c):
            got = dot_tn(hidden_mid[:, rows_of(c, 128)], up_grad[...]).astype(BF)
            for par in range(2):
                for q in range(n):
                    grads[holder(par, l), c // 2, lax.rem(c, 2), q, PIECE_UP:PIECE_OUT, :] = got[par * 64 : par * 64 + 64, q * (ff // n) : (q + 1) * (ff // n)]

        def grad_down(q):
            got = dot_tn(active[:, rows_of(q, ff // n)], branch[...]).astype(BF)
            for i in range(GROUP):
                grads[holder(i % 2, l), i // 4, i // 2 % 2, q, PIECE_DOWN:PIECE_UP, :] = got[i * 64 : (i + 1) * 64]

        def grad_out(q):
            got = dot_tn(gated[:, rows_of(q, channels)], out_grad[...]).astype(BF)
            for i in range(GROUP):
                grads[holder(i % 2, l), i // 4, i // 2 % 2, q, PIECE_OUT:PIECE_IN, :] = got[i * 16 : (i + 1) * 16]

        def grad_in(h):
            def block(c):
                got = dot_tn(hidden[:, rows_of(c, 128)], joined[:, h * width : (h + 1) * width]).astype(BF)
                for par in range(2):
                    for q in range(n):
                        for t in range(2):
                            grads[holder(par, l), c // 2, lax.rem(c, 2), q, PIECE_IN:PIECE_ROWS, h * 256 + t * 128 : h * 256 + (t + 1) * 128] = got[
                                par * 64 + t * 32 : par * 64 + (t + 1) * 32, q * channels : (q + 1) * channels
                            ]

            loop(GROUP // 2, block)

        loop(n, grad_down)
        groups["d" + str(l)].s0()
        visit(l, "down")
        loop(GROUP // 2, grad_up)
        groups["u" + str(l)].s0()
        next_load("hidden_mid", l=l)
        visit(l, "up")
        ready("middle", l=l)
        sums_mid = norm_back(big_a.at[:, 0:width], middle, grad, gains[l, 1:2, :], middle_grad, out_grad)
        next_load("middle", l=l)

        ready("out", l=l)
        big_b[0:tokens, 0:width] = dot_nt(out_grad[...], wout[...])
        next_load("out", l=l)
        visit(l, "open")
        ready("gact", "gslope", "conv_out", l=l)

        def unmix(j):
            r = rows_of(j, 32)
            for s in range(n):
                c = slice(s * channels, (s + 1) * channels)
                up = big_b[r, c]
                send_c[s, r, :] = (up * gact[r, c].astype(F32)).astype(BF)
                joined[r, slice(width + s * channels, width + (s + 1) * channels)] = (
                    up * conv_out[s, r, :].astype(F32) * gslope[r, c].astype(F32)
                ).astype(BF)

        loop(tokens // 32, unmix)
        next_load("gact", "gslope", "conv_out", l=l)
        exchange_start(2 * l, send_c, recv_c, l)
        recv_c[me] = send_c[me]
        visit(l, "sent")
        ready("gated", l=l)
        loop(n, grad_out)
        groups["o" + str(l)].s0()
        next_load("gated", l=l)
        visit(l, "out")
        if l == top:
            ready("masks", "table", l=l)
        ready("conv_in", l=l)
        spread_blocks(conv_in, masks, spread)
        big_a[:, 0 : 7 * channels] = dot(table[...], spread[...])
        next_load("conv_in", l=l)
        visit(l, "transform")
        exchange_wait(2 * l, send_c, recv_c, l)
        spread_blocks(recv_c, masks, spread)
        big_b[:, 0 : 7 * channels] = dot(table[...], spread[...])
        visit(l, "came")
        ready("wins", l=l)
        back_products(big_a, big_b, wins, active, up_grad, channels)
        next_load("wins", l=l)
        visit(l, "products")
        if l == top:
            ready("table_t", "tap_t", l=l)

        def untransform(j):
            r = rows_of(j, 256)
            parts = dot(table_t[r, 0:quarter], active[:, 0 : 7 * channels])
            parts += dot(table_t[r, quarter : 2 * quarter], active[:, half : half + 7 * channels])
            for s in range(n):
                send_d[s, r, :] = join_blocks(parts, r, masks, s).astype(BF)

        loop(quarter // 256, untransform)
        exchange_start(2 * l + 1, send_d, recv_d, l)
        recv_d[me] = send_d[me]
        next_load("active", l=l)

        taps = None
        for m in range(4):
            c = slice(m * channels, (m + 1) * channels)
            d = slice(half + m * channels, half + (m + 1) * channels)
            got = dot(tap_t[m, :, 0:quarter], up_grad[:, c]) + dot(tap_t[m, :, quarter : 2 * quarter], up_grad[:, d])
            taps = got if taps is None else taps + got
        kg_s[l] = taps.astype(BF)
        kernel_grads[l].start()
        visit(l, "returned")
        ready("in", "hidden", "stream", l=l)
        big_a[0:tokens, 0:width] = dot_nt(joined[:, width : 2 * width], win[1])
        grad_in(1)
        visit(l, "in")
        exchange_wait(2 * l + 1, send_d, recv_d, l)

        def collect(j):
            r = rows_of(j, 64)
            for s in range(n):
                joined[r, s * channels : (s + 1) * channels] = recv_d[s, r, :]

        loop(tokens // 64, collect)
        if l == 0:
            grad_in(0)
            groups["i" + str(l)].s0()
        big_a[0:tokens, 0:width] = big_a[0:tokens, 0:width] + dot_nt(joined[:, 0:width], win[0])
        next_load("in", l=l)
        visit(l, "project")
        sums_in = norm_back(big_a.at[:, 0:width], stream, middle_grad, gains[l, 0:1, :], grad, branch)
        next_load("stream", l=l)
        if l == 0:
            grad_move.start()
        else:
            grad_in(0)
            groups["i" + str(l)].s0()
        next_load("hidden", l=l)
        norm_s[l] = jnp.concatenate(
            [jnp.sum(s, axis=0, keepdims=True) for s in (sums_in[0], sums_mid[0], sums_in[1], sums_mid[1])]
            + [jnp.zeros((4, width), F32)],
            axis=0,
        )
        norm_grads.start(l)
        visit(l, "end")

    visit(0, "tail")
    out_norm = pltpu.make_async_copy(norm_v, norm_o, out_sems.at[1])
    out_norm.start()
    for l in range(layers):
        raw, inverse = normal_taps(subs, scales, l)
        k = raw * inverse
        own = kg_own[l].astype(F32)
        along = jnp.sum(own * k, axis=0, keepdims=True)
        sub_s[l] = scales[0] * (own - scales[1] * k * along) * inverse
    out_sub = pltpu.make_async_copy(sub_s, sub_o, out_sems.at[0])
    out_sub.start()
    for group in groups.values():
        group.end()
    out_res = pltpu.make_async_copy(res, res_o, out_sems.at[2])
    out_res.start()
    for m in (out_move, grad_move):
        m.arrive()
        m.finish()
    for g in kernel_grads:
        g.finish()
    out_sub.wait()
    out_norm.wait()
    out_res.wait()


def backward(n, gains, subs, scales, masks, table, table_t, tap_t, out, cot, kept):
    layers, tokens, width = kept[0].shape
    channels = width // n
    ff = kept[-1].shape[1]
    taps = subs.shape[1]

    def sds(*shape, dtype=F32):
        return jax.ShapeDtypeStruct(shape, dtype)

    outs = [
        sds(tokens, width, dtype=BF), sds(tokens, width, dtype=BF), sds(layers, GROUP, PIECE_ROWS, width, dtype=BF),
        sds(layers, taps, channels), sds(layers, 8, width), sds(tokens, width, dtype=BF), sds(tokens, width, dtype=BF),
    ]
    f32 = lambda *s: pltpu.VMEM(s, F32)
    bf = lambda *s: pltpu.VMEM(s, BF)
    wide, blocks, small = (tokens, width), (n, tokens, channels), (layers, taps, channels)
    scratch = [
        f32(*wide), f32(*wide), f32(*wide), bf(*wide), bf(*wide), bf(*wide), bf(*blocks), bf(*blocks), bf(*wide), f32(*wide), bf(*wide),
        bf(tokens, ff), bf(tokens, ff), f32(4, 2, tokens, channels),
        bf(2, width, width), bf(width, width), bf(width, ff), bf(ff, width),
        bf(layers + 1, 2, 2, n, PIECE_ROWS, width),
        bf(layers, 2, 2, n, PIECE_ROWS, width),
        bf(layers, 3, n, PIECE_ROWS, width),
        bf(layers, n - 1, PIECE_ROWS, width),
        bf(layers, GROUP, PIECE_ROWS, width),
        bf(tokens, ff), bf(*wide), bf(*wide), bf(tokens, 2 * width),
        f32(2 * tokens, 7 * channels), f32(2 * tokens, ff // 2), bf(tokens, 7 * channels),
        bf(*blocks), bf(*blocks), bf(*blocks), bf(*blocks),
        bf(*small), bf(layers, n - 1, taps, channels), bf(*small), bf(*small), bf(*small), bf(*small), f32(*small),
        bf(10, tokens, channels), bf(2 * tokens, tokens), bf(tokens, 2 * tokens), bf(4, taps, 2 * tokens),
        f32(layers, 8, width), f32(layers, GROUP - 1, 8, width), f32(layers, 8, width), f32(layers, n - 1, 8, width), f32(layers, 8, width),
        pltpu.SemaphoreType.DMA((layers, 21)),
        pltpu.SemaphoreType.DMA((2 * layers, 2)),
        pltpu.SemaphoreType.DMA((4 * layers, 12)),
        pltpu.SemaphoreType.DMA((layers, 9 + n)),
        pltpu.SemaphoreType.DMA((layers, 4)),
        pltpu.SemaphoreType.DMA((3,)),
        pltpu.SemaphoreType.DMA((2, 4)),
    ]
    return pl.pallas_call(
        functools.partial(backward_kernel, n, layers),
        out_shape=outs,
        in_specs=[VMEM] * 3 + [ANY] * (6 + len(kept)),
        out_specs=[ANY] * len(outs),
        scratch_shapes=scratch,
        compiler_params=pltpu.CompilerParams(collective_id=2, has_side_effects=True, vmem_limit_bytes=int(63.5 * 2**20)),
        name="backward",
    )(gains, subs, scales, masks, table, table_t, tap_t, out, cot, *kept)


def finish_kernel(out_i, grad_i, res, out, grad, up, down, out_w, in_w):
    out[...] = out_i[...].astype(F32)
    grad[...] = grad_i[...].astype(F32)
    members = res.shape[1]
    for i in range(members):
        up[0, i * 64 : (i + 1) * 64, :] = res[0, i, PIECE_UP:PIECE_OUT, :].astype(F32)
        down[0, i * 64 : (i + 1) * 64, :] = res[0, i, PIECE_DOWN:PIECE_UP, :].astype(F32)
        out_w[0, i * 16 : (i + 1) * 16, :] = res[0, i, PIECE_OUT:PIECE_IN, :].astype(F32)
        for h in range(2):
            for t in range(2):
                c = h * 256 + t * 128
                in_w[0, h, i * 64 + t * 32 : i * 64 + (t + 1) * 32, :] = res[0, i, PIECE_IN:, c : c + 128].astype(F32)


def finish(out, grad, res):
    layers, members, _, width = res.shape
    tokens = out.shape[0]
    parts = 2
    m = members // parts
    steps = layers * parts
    rows = tokens // steps

    def sds(*shape):
        return jax.ShapeDtypeStruct(shape, F32)

    flat = pl.BlockSpec((rows, width), lambda j: (j, 0))

    def mid(*shape):
        return pl.BlockSpec((1, *shape, width), lambda j: (j // parts, j % parts, 0))

    return pl.pallas_call(
        finish_kernel,
        grid=(steps,),
        out_shape=[
            sds(tokens, width), sds(tokens, width), sds(layers, members * 64, width), sds(layers, members * 64, width),
            sds(layers, members * 16, width), sds(layers, 2, members * 64, 128),
        ],
        in_specs=[flat, flat, pl.BlockSpec((1, m, PIECE_ROWS, width), lambda j: (j // parts, j % parts, 0, 0))],
        out_specs=[flat, flat, mid(m * 64), mid(m * 64), mid(m * 16), pl.BlockSpec((1, 2, m * 64, 128), lambda j: (j // parts, 0, j % parts, 0))],
        name="finish",
    )(out, grad, res)


def per_device(
    stream_in, segments, norm_gain, norm_bias, w_in, w_out, sub_kernels, w_up, w_down, cotangent
):
    layers, scales, taps, channels = sub_kernels.shape
    n = lax.axis_size("mp")
    quarter = segments.shape[1] // 4
    table = transform_table(quarter)
    tap_table = tap_tables(quarter, scales, taps) / quarter

    def const(a):
        return jnp.asarray(a, F32).astype(BF)

    factors = jnp.asarray(tap_scales(scales, taps, channels))
    subs = sub_kernels.reshape(layers, -1, channels)
    out, *kept, masks, cot, win, wout, wup, wdn = forward(
        n, stream_in, cotangent, segments, norm_gain, norm_bias, subs, factors, const(table), const(table.T), const(tap_table),
        w_in.transpose(0, 2, 1, 3), w_out, w_up, w_down,
    )
    out, grad, res, sub, norms, *_ = backward(
        n, norm_gain, subs, factors, masks, const(table), const(table.T), const(tap_table.transpose(0, 2, 1)),
        out, cot, (*kept, win, wout, wup, wdn),
    )
    if lax.axis_size("dp") > GROUP:
        res, sub, norms = [v * (1.0 / GROUP) for v in lax.psum((res.astype(F32), sub, norms), "dp")]
        res = res.astype(BF)
    out, grad, up, down, out_w, in_w = finish(out, grad, res)
    return (
        out, grad, norms[:, 0:2], norms[:, 2:4], in_w.transpose(0, 2, 1, 3), out_w, sub.reshape(sub_kernels.shape), up, down,
    )


def solution(mesh):
    rows = P(("dp", "mp"), None)
    last = P(None, None, None, "mp")
    mid = P(None, "mp", None)
    return jax.shard_map(
        per_device,
        mesh=mesh,
        in_specs=(rows, P("dp", None), P(), P(), last, mid, last, P(None, None, "mp"), mid, rows),
        out_specs=(rows, rows, P(), P(), last, mid, last, P(None, None, "mp"), mid),
        check_vma=False,
    )
```

time: 340 us -> 244 us (0.72)
  Pallas kernels: 309 us -> 235 us
  local copies, waits for them, and re-layouts: 24.3 us -> 7.03 us
    pallas_call x1, Pallas kernels: 177 us -> 123 us  [backward(): pl.pallas_call(functools.partial(backward_kernel, n, layers), out_shape=o...]
    pallas_call x1, Pallas kernels: 132 us -> 106 us  [forward(): pl.pallas_call(functools.partial(forward_kernel, n, layers), out_shape=ou...]
    slice x4 -> x0, local copies, waits for them, and re-layouts: 7.06 us -> none  [the longest x1 2.59 us: per_device(): down = res[:, :, PIECE_DOWN:PIECE_OUT].reshape(w_down.shape)]
    pallas_call x0 -> x1, Pallas kernels: none -> 5.66 us  [finish(): pl.pallas_call(finish_kernel, grid=(steps,), out_shape=[sds(tokens, width...]
    broadcast_in_dim x3 -> x0, local copies, waits for them, and re-layouts: 4.26 us -> none  [the longest x2 2.6 us: per_device(): gains, biases = (norm_gain[:, :, None], norm_bias[:, :, None])]
where the time goes in v4:
time: 244 us; the launch traced here: 243 us
  Pallas kernels  235 us (96%)
  local copies, waits for them, and re-layouts  7.03 us (3%)
    pallas_call x1, Pallas kernels, backward(): pl.pallas_call(functools.partial(backward_kernel, n, layers), out_shape=o...  123 us
    pallas_call x1, Pallas kernels, forward(): pl.pallas_call(functools.partial(forward_kernel, n, layers), out_shape=ou...  106 us
    pallas_call x1, Pallas kernels, finish(): pl.pallas_call(finish_kernel, grid=(steps,), out_shape=[sds(tokens, width...  5.66 us
    unnamed x5, local copies, waits for them, and re-layouts  5.59 us

profile of v4, /device:TPU:0, one launch (start us, length us, event | category | flops | bytes accessed | tf_op | source)
XLA Modules:
  0.0 243.1 jit_solution(6777125777700064580)
XLA Ops:
  0.6 1.9 copy.29
  2.5 106.4 %forward.1 = (bf16[512,512]{1,0:T(8,128)(2,1)}, f32[2,512,512]{2,1,0:T(8,128)}, bf16[2,512,512]{2,1,0:T(8,128)(2,1)}, bf16[2,512,512]{2,1,0:T(8,128)(2,1)}, bf16...) custom-call(f32[512,512]{1,0:T(8,128)} %stream_in.1, ...), custom_call_target="tpu_custom_call" | custom-call | tf_op jit(solution)/shard_map/forward/pallas_call | solution.py:682
  108.9 123.4 %backward.1 = (bf16[512,512]{1,0:T(8,128)(2,1)}, bf16[512,512]{1,0:T(8,128)(2,1)}, bf16[2,8,176,512]{3,2,1,0:T(8,128)(2,1)}, f32[2,192,128]{2,1,0:T(8,128)}, f32...) custom-call(f32[2,2,512]{2,1,0:T(2,128)} %gains.3, f32[2,192,128]{2,1,0:T(8,128)} %bitcast.9, ...), custom_call_target="tpu_custom_call" | custom-call | tf_op jit(solution)/shard_map/backward/pallas_call | solution.py:1307
  232.3 1.4 fusion
  233.7 0.0 copy-start
  233.7 5.7 %finish.1 = (f32[512,512]{1,0:T(8,128)}, f32[512,512]{1,0:T(8,128)}, f32[2,512,512]{2,1,0:T(8,128)}, f32[2,512,512]{2,1,0:T(8,128)}, f32[2,128,512]{2,1,0:T(8,128)}, /*index=5*/f32[2,2,512,128]{3,2,1,0:T(8,128)}) custom-call(bf16[512,512]{1,0:T(8,128)(2,1)} %get-tuple-element.58.out_i, bf16[512,512]{1,0:T(8,128)(2,1)} %get-tuple-element.59.grad_i, ...), custom_call_target="tpu_custom_call" | custom-call | tf_op jit(solution)/shard_map/finish/pallas_call | solution.py:1348
  239.4 3.0 %copy.27 = f32[2,512,2,128]{3,2,1,0:T(2,128)} copy(f32[2,512,2,128]{3,1,2,0:T(8,128)} %bitcast.7) | data formatting | bytes 2097152
  242.4 0.0 copy-done
  242.4 0.7 copy.31
Async XLA Ops:
  233.7 8.7 %copy-start = (f32[2,192,128]{2,1,0:T(8,128)S(1)}, f32[2,192,128]{2,1,0:T(8,128)}, u32[]{:S(2)}) copy-start(f32[2,192,128]{2,1,0:T(8,128)} %get-tuple-element.66) | copy-start | bytes 589828

commit v5 on v4

--- a/solution.py
+++ b/solution.py
@@ -95,7 +95,7 @@
         self.core = lax.rem(self.i, 2)
         self.x = lax.rem(self.i // 2, 2)
         self.y = self.i // 4
-        self.s = self.x + 2 * self.core
+        self.s = lax.rem(self.q, 2) + 2 * self.core
 
     def device(self, i, q):
         return {"dp": self.base + i, "mp": q}
@@ -130,32 +130,26 @@
 
     def partner(self, k):
         s = lax.rem(self.s + k, self.n)
-        return s, self.device(self.index(self.y, lax.rem(s, 2), s // 2), self.q)
+        return s, self.device(self.index(self.y, self.x, s // 2), 2 * (self.q // 2) + lax.rem(s, 2))
 
     def row_target(self):
-        return self.index(self.y, lax.rem(self.q, 2), self.q // 2), 2 * self.core + self.x
+        return self.device(self.index(self.y, self.x, self.q // 2), 2 * self.core + lax.rem(self.q, 2))
+
+    def opposite(self):
+        return self.device(self.i, lax.rem(self.q + 2, self.n))
 
     def stays(self):
-        i, q = self.row_target()
-        return jnp.logical_and(i == self.i, q == self.q)
+        return self.q // 2 == self.core
 
 
 def greet_all(place):
     barrier = pltpu.get_barrier_semaphore()
     peers = [place.column(k)[1] for k in range(1, place.n)] + [place.member(k) for k in range(1, GROUP)]
+    across = place.index(place.y, place.x, 1 - place.core)
+    peers += [place.device(across, place.column(k)[0]) for k in range(1, place.n)]
     for peer in peers:
         pl.semaphore_signal(barrier, inc=1, device_id=peer, device_id_type=MESH)
-
-    def across():
-        other = place.device(*place.row_target())
-        pl.semaphore_signal(barrier, inc=1, device_id=other, device_id_type=MESH)
-        pl.semaphore_wait(barrier, len(peers) + 1)
-
-    def here():
-        pl.semaphore_wait(barrier, len(peers))
-
-    when(jnp.logical_not(place.stays()), across)
-    when(place.stays(), here)
+    pl.semaphore_wait(barrier, len(peers))
 
 
 def send(src, dst, send_sem, recv_sem, peer):
@@ -169,46 +163,19 @@
 
 
 class Move:
-    def __init__(self, place, src, dst, relay, sems):
-        self.p, self.src, self.dst, self.relay, self.sems = place, src, dst, relay, sems
-        p = place
-        turn = p.q == 1 + p.core
-        self.stays = p.stays()
-        self.via = jnp.logical_and(turn, p.x == p.core)
-        self.passes = jnp.logical_and(turn, p.x != p.core)
-        self.direct = jnp.logical_not(jnp.logical_or(self.stays, self.via))
+    def __init__(self, place, src, dst, sems):
+        self.p, self.src, self.dst, self.sems = place, src, dst, sems
 
     def start(self):
         p = self.p
-
-        def across():
-            send(self.src, self.dst, self.sems.at[0], self.sems.at[1], p.device(*p.row_target()))
-
-        def aside():
-            send(self.src, self.relay, self.sems.at[0], self.sems.at[2], p.mate_x()[1])
-
-        def here():
-            pltpu.make_async_copy(self.src, self.dst, self.sems.at[1]).start()
-
-        when(self.direct, across)
-        when(self.via, aside)
-        when(self.stays, here)
-
-    def pass_on(self):
-        p = self.p
-
-        def onward():
-            await_bytes(self.relay, self.sems.at[2])
-            send(self.relay, self.dst, self.sems.at[3], self.sems.at[1], p.device(p.i, 3 * p.core))
-
-        when(self.passes, onward)
+        when(jnp.logical_not(p.stays()), lambda: send(self.src, self.dst, self.sems.at[0], self.sems.at[1], p.row_target()))
+        when(p.stays(), lambda: pltpu.make_async_copy(self.src, self.dst, self.sems.at[1]).start())
 
     def arrive(self):
         await_bytes(self.dst, self.sems.at[1])
 
     def finish(self):
-        when(jnp.logical_not(self.stays), lambda: await_bytes(self.src, self.sems.at[0]))
-        when(self.passes, lambda: await_bytes(self.relay, self.sems.at[3]))
+        when(jnp.logical_not(self.p.stays()), lambda: await_bytes(self.src, self.sems.at[0]))
 
 
 class Weight:
@@ -277,22 +244,34 @@
             piece = w.piece(i, p.column(k)[0])
             send(piece, piece, send_sem, recv_sem, peer)
 
+    def first_second(self):
+        return self.p.mates("yx" if self.order == "yx" else "xy")
+
     def hop1(self):
         p = self.p
         await_bytes(self.w.span(1), self.sem(1))
-        first, second = p.mates(self.order)
+        first, second = self.first_second()
         self.pass_on(p.i, self.sem(2), self.sem(3), first[1])
         self.pass_on(p.i, self.sem(4), self.sem(5), second[1])
+        if self.order == "direct":
+            self.pass_on(p.i, self.sem(4), self.sem(5), p.mate_xy()[1])
+        self.pass_on(p.i, self.sem(6), self.sem(7), p.sibling())
 
     def hop2(self):
-        first, second = self.p.mates(self.order)
+        first, second = self.first_second()
         await_bytes(self.w.span(1), self.sem(3))
         self.pass_on(first[0], self.sem(4), self.sem(5), second[1])
+        self.pass_on(first[0], self.sem(6), self.sem(7), self.p.sibling())
 
     def hop3(self):
         p = self.p
+        first, second = self.first_second()
+        others = [second[0], p.mate_xy()[0]]
+        if self.order == "direct":
+            await_bytes(self.w.span(1), self.sem(3))
+            others.append(first[0])
         await_bytes(self.w.span(2), self.sem(5))
-        for i in (p.i, p.mate_x()[0], p.mate_y()[0], p.mate_xy()[0]):
+        for i in others:
             self.pass_on(i, self.sem(6), self.sem(7), p.sibling())
 
     def arrive(self):
@@ -326,12 +305,13 @@
     return raw, lax.rsqrt(total + EPSILON)
 
 
-def make_masks(seg_rows, masks):
+def make_masks(segs, masks):
     quarter, channels = masks.shape[1:]
     ones = jnp.full((8, channels), 0.125, BF)
 
     def numbers(n):
-        return dot_tn(seg_rows[:, n * quarter : (n + 1) * quarter].astype(BF), ones)
+        row = segs[:, n * quarter : (n + 1) * quarter].astype(F32)
+        return dot_tn(jnp.broadcast_to(row, (8, quarter)).astype(BF), ones)
 
     def put(k, flag):
         masks[k] = jnp.where(flag, 1.0, 0.0).astype(BF)
@@ -409,24 +389,24 @@
     loop(quarter // 16, strip)
 
 
+FORWARD_ORDER = {"d0": "direct", "d1": "direct", "i0": "direct", "i1": "direct", "o0": "xy", "o1": "direct", "u0": "direct", "u1": "direct"}
 FORWARD_PLAN = {
-    (0, "start"): ("u0.start", "i0.hop1"),
-    (0, "ready"): ("tok.pass_on", "i0.hop2", "i0.hop3"),
-    (0, "project"): ("o0.start", "d0.start"),
-    (0, "sent"): ("i1.start",),
-    (0, "gate"): ("seg.pass_on",),
-    (0, "came"): ("o1.start", "u1.start", "u0.hop1"),
-    (0, "transform"): ("o0.hop1",),
-    (0, "returned"): ("u0.hop2", "o0.hop2", "d0.hop1"),
-    (0, "back"): ("u0.hop3", "i1.hop1", "cot.start", "o0.hop3"),
-    (0, "attach"): ("d0.hop2",),
-    (0, "norm"): ("i1.hop2",),
-    (0, "widen"): ("u1.hop1",),
-    (0, "activate"): ("d0.hop3", "i1.hop3"),
-    (0, "narrow"): ("d1.start", "o1.hop1", "u1.hop2"),
-    (1, "sent"): ("o1.hop2", "u1.hop3", "d1.hop1", "cot.pass_on"),
-    (1, "gate"): ("o1.hop3",),
-    (1, "returned"): ("d1.hop2", "d1.hop3"),
+    (0, "start"): ("o0.start", "i0.hop1", "u0.start"),
+    (0, "start2"): ("i0.hop3",),
+    (0, "sent"): ("d0.start", "i1.start"),
+    (0, "gate"): ("o0.hop1",),
+    (0, "win0"): ("o0.hop2", "u0.hop1"),
+    (0, "win1"): ("o0.hop3",),
+    (0, "came"): ("d0.hop1",),
+    (0, "returned"): ("u0.hop3", "d1.start", "u1.start", "i1.hop1", "o1.start"),
+    (0, "widen"): ("d0.hop3",),
+    (0, "narrow"): ("i1.hop3",),
+    (1, "normed"): ("u1.hop1",),
+    (1, "sent"): ("cot.start",),
+    (1, "gate"): ("o1.hop1",),
+    (1, "transform"): ("d1.hop1",),
+    (1, "returned"): ("u1.hop3", "o1.hop3"),
+    (1, "widen"): ("d1.hop3",),
 }
 
 
@@ -437,7 +417,7 @@
     wins_o, masks_o, cot_o, win_o, wout_o, wup_o, wdn_o,
     stream, hidden, gact, gslope, gated, middle, hidden_mid, active, slope, send_a, recv_a, send_b, recv_b,
     spread, spec, spec_y, wins, win_f, wout_f, wup_f, wdn_f,
-    masks, tok_s, tok_r, tok_p, cot_in, cot_s, cot_p, seg_s, seg_r, seg_p, taps_s, taps_r, table, table_t, tap_table,
+    masks, tok_s, tok_r, cot_in, cot_s, seg_r, taps_s, taps_r, table, table_t, tap_table,
     gather_sems, a2a_sems, save_sems, move_sems, tap_sems, load_sems,
 ):
     place = Place(n)
@@ -450,8 +430,6 @@
         pltpu.make_async_copy(src, dst, load_sems.at[k])
         for k, (src, dst) in enumerate(((cot_h, cot_in), (tap_table_h, tap_table), (table_h, table), (table_t_h, table_t)))
     ]
-    for copy in loads:
-        copy.start()
     greet_all(place)
     saves = []
 
@@ -462,24 +440,26 @@
         copy.start()
         saves.append(copy)
 
-    def exchange_start(slot, src, dst, layer):
+    def exchange_start(slot, src, dst, layer, rows=None):
+        rows = pl.ds(0, tokens) if rows is None else rows
         for k in range(1, n):
             s, peer = place.partner(k)
-            send(src.at[layer, s], dst.at[layer, me], a2a_sems.at[slot, 0], a2a_sems.at[slot, 1], peer)
+            send(src.at[layer, s, rows], dst.at[layer, me, rows], a2a_sems.at[slot, 0], a2a_sems.at[slot, 1], peer)
 
     def exchange_wait(slot, src, dst, layer):
         await_bytes(src.at[layer, pl.ds(0, n - 1)], a2a_sems.at[slot, 0])
         await_bytes(dst.at[layer, pl.ds(0, n - 1)], a2a_sems.at[slot, 1])
 
     moving = {
-        "seg": Move(place, seg_s, seg_r, seg_p, move_sems.at[0]),
-        "tok": Move(place, tok_s, tok_r, tok_p, move_sems.at[1]),
-        "cot": Move(place, cot_s, cot_o, cot_p, move_sems.at[2]),
+        "seg": Move(place, segs, seg_r, move_sems.at[0]),
+        "tok": Move(place, tok_s, tok_r, move_sems.at[1]),
+        "cot": Move(place, cot_s, cot_o, move_sems.at[2]),
     }
     gathers = {}
     for l in range(layers):
         for kind, whole, shard in (("in", win_f, win), ("out", wout_f, wout), ("up", wup_f, wup), ("down", wdn_f, wdn)):
-            gathers[kind[0] + str(l)] = Gather(place, Weight(whole, l, kind, n), shard, gather_sems, len(gathers), "xy")
+            name = kind[0] + str(l)
+            gathers[name] = Gather(place, Weight(whole, l, kind, n), shard, gather_sems, len(gathers), FORWARD_ORDER.get(name, "xy"))
     moving.update(gathers)
 
     def visit(l, point):
@@ -495,22 +475,26 @@
 
     loop(tokens // 64, round_stream)
     moving["tok"].start()
-    seg_s[...] = jnp.broadcast_to(segs[...].astype(F32), seg_s.shape)
     moving["seg"].start()
     for l in range(layers):
         raw, inverse = normal_taps(subs, scales, l)
         taps_s[l] = (raw * inverse).astype(BF)
 
     def give_taps():
-        for k in range(1, n):
-            send(taps_s, taps_r, tap_sems.at[0, k], tap_sems.at[1, k], place.column(k)[1])
+        send(taps_s, taps_r, tap_sems.at[0], tap_sems.at[1], place.opposite())
+
+    def keep_taps():
         taps_r[...] = taps_s[...]
 
     def take_taps():
-        ahead = lax.rem(place.q - place.s + n, n)
-        await_bytes(taps_r, tap_sems.at[1, ahead])
-
-    when(place.s == place.q, give_taps)
+        await_bytes(taps_r, tap_sems.at[1])
+
+    own_taps = place.s == place.q
+    when(own_taps, give_taps)
+    for copy in loads:
+        copy.start()
+    when(own_taps, keep_taps)
+    visit(0, "start")
     loads[0].wait()
 
     def round_cotangent(j):
@@ -518,7 +502,7 @@
         cot_s[r, :] = cot_in[r, :].astype(BF)
 
     loop(tokens // 64, round_cotangent)
-    visit(0, "start")
+    visit(0, "start2")
     visit(0, "ready")
     moving["tok"].arrive()
 
@@ -531,6 +515,7 @@
 
     for l in range(layers):
         norm_all(stream.at[l], hidden.at[l], gains[l, 0:1, :], biases[l, 0:1, :])
+        visit(l, "normed")
         gathers["i" + str(l)].arrive()
         got = dot(hidden[l], win_f[l, 0]).astype(BF)
         for s in range(n):
@@ -542,6 +527,7 @@
         save(hidden, hidden_o, l)
         save(win_f, win_o, l)
         spec[0:tokens, 0:width] = dot(hidden[l], win_f[l, 1])
+        visit(l, "gate0")
 
         def open_gate(j):
             r = rows_of(j, 16)
@@ -557,10 +543,12 @@
             moving["seg"].arrive()
             make_masks(seg_r, masks)
             save(masks, masks_o)
-            when(place.s != place.q, take_taps)
+            visit(l, "masks")
+            when(jnp.logical_not(own_taps), take_taps)
             loads[1].wait()
             for m in range(layers):
                 make_windows(taps_r[m], tap_table, spec, m, wins)
+                visit(l, "win" + str(m))
             save(wins, wins_o)
             loads[2].wait()
             loads[3].wait()
@@ -571,15 +559,15 @@
         spec[:, 0 : 7 * channels] = dot(table[...], spread[...])
         visit(l, "transform")
         fwd_products(spec, wins, l, spec_y, channels)
-
-        def untransform(j):
-            r = rows_of(j, 256)
+        visit(l, "prod")
+        for j in range(2):
+            r = slice(j * (quarter // 2), (j + 1) * (quarter // 2))
             parts = dot(table_t[r, :], spec_y[...])
             for s in range(n):
                 send_b[l, s, r, :] = join_blocks(parts, r, masks, s).astype(BF)
-
-        loop(quarter // 256, untransform)
-        exchange_start(2 * l + 1, send_b, recv_b, l)
+            exchange_start(2 * l + 1, send_b, recv_b, l, pl.ds(j * (quarter // 2), quarter // 2))
+            if j == 0:
+                visit(l, "untr")
         recv_b[l, me] = send_b[l, me]
         visit(l, "returned")
         exchange_wait(2 * l + 1, send_b, recv_b, l)
@@ -593,6 +581,7 @@
                 gated[l, r, c] = (gact[l, r, c].astype(F32) * recv_b[l, s, r, :].astype(F32)).astype(BF)
 
         loop(tokens // 64, mix)
+        visit(l, "mix")
         gathers["o" + str(l)].arrive()
         save(gated, gated_o, l)
         save(wout_f, wout_o, l)
@@ -606,18 +595,18 @@
         save(wup_f, wup_o, l)
         for h in range(2):
             spec[h * tokens : (h + 1) * tokens, :] = dot(hidden_mid[l], wup_f[l, :, h * half : (h + 1) * half])
-        visit(l, "widen")
-
-        def activate(j):
-            r = rows_of(j, 16)
-            for h in range(2):
-                t = pl.ds(pl.multiple_of(h * tokens + j * 16, 16), 16)
-                act, incline = gelu_both(spec[t, :])
+            visit(l, ("widen0", "widen")[h])
+
+        for h in range(2):
+
+            def activate(j):
+                r = rows_of(j, 16)
+                act, incline = gelu_both(spec[pl.ds(pl.multiple_of(h * tokens + j * 16, 16), 16), :])
                 active[l, r, h * half : (h + 1) * half] = act.astype(BF)
                 slope[l, r, h * half : (h + 1) * half] = incline.astype(BF)
 
-        loop(tokens // 16, activate)
-        visit(l, "activate")
+            loop(tokens // 16, activate)
+            visit(l, ("act0", "activate")[h])
         save(active, active_o, l)
         save(slope, slope_o, l)
         gathers["d" + str(l)].arrive()
@@ -636,11 +625,7 @@
     for name in ("seg", "cot"):
         moving[name].finish()
 
-    def taps_given():
-        for k in range(1, n):
-            await_bytes(taps_s, tap_sems.at[0, k])
-
-    when(place.s == place.q, taps_given)
+    when(own_taps, lambda: await_bytes(taps_s, tap_sems.at[0]))
     for copy in saves:
         copy.wait()
 
@@ -669,14 +654,14 @@
         bf(*blocks), bf(*blocks), bf(*blocks), bf(*blocks),
         bf(tokens, 7 * channels), f32(2 * tokens, ff // 2), bf(2 * tokens, 7 * channels), f32(layers, 4, 2, tokens, channels),
     ] + [bf(*s) for s in wshapes] + [
-        bf(10, tokens, channels), bf(tokens, width), bf(tokens, width), bf(tokens, width), f32(tokens, width), bf(tokens, width), bf(tokens, width),
-        f32(8, 4 * tokens), f32(8, 4 * tokens), f32(8, 4 * tokens), bf(layers, taps, channels), bf(layers, taps, channels),
+        bf(10, tokens, channels), bf(tokens, width), bf(tokens, width), f32(tokens, width), bf(tokens, width),
+        pltpu.VMEM(segments.shape, segments.dtype), bf(layers, taps, channels), bf(layers, taps, channels),
         bf(2 * tokens, tokens), bf(tokens, 2 * tokens), bf(4, 2 * tokens, taps),
         pltpu.SemaphoreType.DMA((4 * layers, 9)),
         pltpu.SemaphoreType.DMA((2 * layers, 2)),
         pltpu.SemaphoreType.DMA((15 * layers + 3,)),
-        pltpu.SemaphoreType.DMA((3, 4)),
-        pltpu.SemaphoreType.DMA((2, n)),
+        pltpu.SemaphoreType.DMA((3, 2)),
+        pltpu.SemaphoreType.DMA((2,)),
         pltpu.SemaphoreType.DMA((4,)),
     ]
     return pl.pallas_call(
@@ -883,24 +868,34 @@
     return total
 
 
-BACKWARD_ORDER = {"d1": "yx", "u1": "direct", "i1": "yx", "d0": "yx", "u0": "yx", "i0": "yx"}
+BACKWARD_ORDER = {"d0": "yx", "d1": "yx", "e0": "xy", "e1": "xy", "i0": "direct", "i1": "direct", "o0": "direct", "o1": "direct", "u0": "yx", "u1": "yx", "v0": "xy", "v1": "xy"}
 BACKWARD_PLAN = {
-    (1, "sent"): ("d1.s1",),
-    (1, "out"): ("o1.s1",),
-    (1, "returned"): ("u1.s1",),
-    (1, "project"): ("kg1.over_mp",),
-    (0, "narrow"): ("d1.s1b",),
-    (0, "down"): ("i1.s1",),
-    (0, "sent"): ("u0.s1",),
-    (0, "out"): ("o0.s1", "d1.s2", "i1.s1b", "d0.s1"),
-    (0, "transform"): ("out.pass_on",),
-    (0, "returned"): ("u1.s2", "kg0.over_mp"),
-    (0, "in"): ("i1.s2", "u0.s1b"),
-    (0, "end"): ("d1.s3", "i0.s1", "d0.s1b"),
+    (1, "middle"): ("e1.s1",),
+    (1, "open"): ("d1.s1",),
+    (1, "sent"): ("v1.s1",),
+    (1, "transform"): ("o1.s1",),
+    (1, "gatep"): ("u1.s1",),
+    (1, "in"): ("d1.s1b",),
+    (1, "end"): ("v1.s1b",),
+    (0, "narrow"): ("i1.s1",),
+    (0, "down0"): ("d1.s2",),
+    (0, "down"): ("e1.s1b",),
+    (0, "up0"): ("u1.s1b",),
+    (0, "sent"): ("v1.s2", "e0.s1", "d0.s1"),
+    (0, "out"): ("e1.s2",),
+    (0, "transform"): ("i1.s2",),
+    (0, "came"): ("o0.s1",),
+    (0, "half"): ("u0.s1", "d0.s1b"),
+    (0, "returned"): ("v0.s1",),
+    (0, "gatep"): ("o1.s2", "u1.s2"),
+    (0, "in"): ("d1.s3", "d0.s2", "v1.s3"),
+    (0, "project"): ("e0.s1b",),
+    (0, "end"): ("v0.s1b", "u0.s1b"),
     (0, "tail"): (
-        "u0.s2", "u1.s3", "grad.pass_on", "kg0.over_y", "i1.s3", "d1.s4", "d0.s2", "o1.s2", "i0.s1b", "o0.s2", "u0.s3", "d0.s3",
-        "i0.s2", "kg0.take", "norm.over_mp", "o0.s3", "o1.s3", "u0.s4", "u1.s4", "i0.s3", "d0.s4", "i1.s4", "o0.s4", "kg1.over_y",
-        "o1.s4", "i0.s4", "norm.take", "kg1.take",
+        "kg1.over_mp", "i1.s3", "v0.s2", "kg0.over_mp", "kg1.over_group", "e0.s2", "u0.s2", "i0.s1", "d0.s3",
+        "v0.s3", "d1.s4", "i0.s2", "u1.s3", "kg1.take", "o1.s3", "o0.s2", "v1.s4", "v0.s4", "d0.s4", "e0.s3",
+        "e1.s3", "i1.s4", "kg0.over_group", "norm.over_mp", "o1.s4", "u0.s3", "u1.s4", "i0.s3", "o0.s3", "e0.s4",
+        "kg0.take", "e1.s4", "u0.s4", "norm.take", "i0.s4", "o0.s4",
     ),
 }
 
@@ -908,56 +903,49 @@
 class KernelGrad:
     def __init__(self, place, layer, refs, sems):
         self.p, self.l, self.sems = place, layer, sems
-        self.own, self.from_mp, self.mid, self.from_y, self.total, self.result = [r.at[layer] for r in refs]
+        self.own, self.from_mp, self.mid, self.from_group, self.total, self.result = [r.at[layer] for r in refs]
         self.owner = place.s == place.q
 
     def sem(self, k):
         return self.sems.at[self.l, k]
 
     def start(self):
-        p = self.p
-        k = lax.rem(p.q - p.s + p.n, p.n)
-        when(
-            jnp.logical_not(self.owner),
-            lambda: send(self.own, self.from_mp.at[lax.max(k - 1, 0)], self.sem(0), self.sem(1 + k), p.device(p.i, p.s)),
-        )
+        when(jnp.logical_not(self.owner), lambda: send(self.own, self.from_mp, self.sem(0), self.sem(1), self.p.opposite()))
 
     def over_mp(self):
         p = self.p
 
         def add():
-            total = self.own[...].astype(F32)
-            for k in range(1, p.n):
-                await_bytes(self.from_mp.at[k - 1], self.sem(1 + k))
-                total += self.from_mp[k - 1].astype(F32)
-            self.mid[...] = total.astype(BF)
-            send(self.mid, self.from_y, self.sem(5), self.sem(6), p.mate_y()[1])
+            await_bytes(self.from_mp, self.sem(1))
+            self.mid[...] = (self.own[...].astype(F32) + self.from_mp[...].astype(F32)).astype(BF)
+            for k, mate in enumerate((p.mate_x(), p.mate_y(), p.mate_xy())):
+                send(self.mid, self.from_group.at[k], self.sem(2 + k), self.sem(5 + k), mate[1])
 
         when(self.owner, add)
 
-    def over_y(self):
+    def over_group(self):
         p = self.p
 
         def add():
-            await_bytes(self.from_y, self.sem(6))
-            both = (self.mid[...].astype(F32) + self.from_y[...].astype(F32)).astype(BF)
+            for k in range(3):
+                await_bytes(self.from_group.at[k], self.sem(5 + k))
+            near = self.mid[...].astype(F32) + self.from_group[0].astype(F32)
+            far = self.from_group[1].astype(F32) + self.from_group[2].astype(F32)
+            both = (near + far).astype(BF)
             self.total[...] = both
             self.result[...] = both
-            for k in range(1, p.n):
-                send(self.total, self.result, self.sem(6 + k), self.sem(9 + k), p.partner(k)[1])
+            send(self.total, self.result, self.sem(8), self.sem(9), p.sibling())
 
         when(self.owner, add)
 
     def take(self):
-        p = self.p
-        k = lax.rem(p.s - p.q + p.n, p.n)
-        when(jnp.logical_not(self.owner), lambda: await_bytes(self.result, self.sem(9 + k)))
+        when(jnp.logical_not(self.owner), lambda: await_bytes(self.result, self.sem(9)))
 
     def finish(self):
         def given():
-            await_bytes(self.mid, self.sem(5))
-            for k in range(1, self.p.n):
-                await_bytes(self.total, self.sem(6 + k))
+            for k in range(3):
+                await_bytes(self.mid, self.sem(2 + k))
+            await_bytes(self.total, self.sem(8))
 
         when(self.owner, given)
         when(jnp.logical_not(self.owner), lambda: await_bytes(self.own, self.sem(0)))
@@ -994,7 +982,7 @@
     gains, subs, scales, masks_h, table_h, table_t_h, tap_t_h,
     out_in, cot, streams, hiddens, gacts, gslopes, conv_ins, conv_outs, gateds, middles, hidden_mids, actives, slopes,
     wins_h, win_h, wout_h, wup_h, wdn_h,
-    out_o, grad_o, res_o, sub_o, norm_o, out_p, grad_p,
+    out_o, grad_o, res_o, sub_o, norm_o,
     grad, middle_grad, stream, hidden, gact, gslope, conv_in, conv_out, gated, middle, hidden_mid, active, slope, wins, win, wout, wup, wdn,
     grads, r0, r1, r2, res,
     up_grad, out_grad, branch, joined, big_a, big_b, spread,
@@ -1036,25 +1024,22 @@
                 load(name, l - 1)
 
     top = layers - 1
-    for name in (
-        "branch", "down", "slope", "up", "active", "hidden_mid", "middle", "out", "gact", "gslope", "conv_out", "gated", "masks",
-        "conv_in", "table", "wins", "table_t", "tap_t", "in", "hidden", "stream",
-    ):
+    for name in ("branch", "down", "slope"):
         load(name, top)
     greet_all(place)
     bufs = (grads, r0, r1, r2, res)
-    bounds = (PIECE_DOWN, PIECE_UP, PIECE_OUT, PIECE_IN, PIECE_ROWS)
+    bounds = (PIECE_DOWN, PIECE_UP // 2, PIECE_UP, (PIECE_UP + PIECE_OUT) // 2, PIECE_OUT, PIECE_IN, PIECE_ROWS)
     groups = {}
     for l in range(layers):
-        for k, letter in enumerate("duoi"):
+        for k, letter in enumerate("deuvoi"):
             name = letter + str(l)
             order = BACKWARD_ORDER.get(name, "direct")
             groups[name] = Reduce(place, bufs, red_sems, len(groups), l, bounds[k], bounds[k + 1] - bounds[k], order)
     kernel_grads = [KernelGrad(place, l, (kg_s, kg_z, kg_t, kg_y, kg_u, kg_own), kg_sems) for l in range(layers)]
     norm_grads = NormGrad(place, (norm_s, norm_r, norm_t, norm_u, norm_v), norm_sems)
-    out_move = Move(place, out_in, out_o, out_p, move_sems.at[0])
-    grad_move = Move(place, branch, grad_o, grad_p, move_sems.at[1])
-    moving = {"out": out_move, "grad": grad_move, "norm": norm_grads, **groups}
+    out_move = Move(place, out_in, out_o, move_sems.at[0])
+    grad_move = Move(place, branch, grad_o, move_sems.at[1])
+    moving = {"norm": norm_grads, **groups}
     moving.update({"kg" + str(l): kernel_grads[l] for l in range(layers)})
 
     def visit(l, point):
@@ -1062,10 +1047,10 @@
             what, action = step.split(".")
             getattr(moving[what], action)()
 
-    def exchange_start(slot, src, dst, l):
+    def exchange_start(slot, src, dst, rows):
         for k in range(1, n):
             s, peer = place.partner(k)
-            send(src.at[s], dst.at[me], a2a_sems.at[slot, 0], a2a_sems.at[slot, 1], peer)
+            send(src.at[s, rows], dst.at[me, rows], a2a_sems.at[slot, 0], a2a_sems.at[slot, 1], peer)
 
     def exchange_wait(slot, src, dst, l):
         await_bytes(src.at[pl.ds(0, n - 1)], a2a_sems.at[slot, 0])
@@ -1076,6 +1061,8 @@
         return l * mine + spare * (1 - mine)
 
     out_move.start()
+    for name in ("up", "active", "hidden_mid", "middle", "out", "gact", "gslope", "conv_out"):
+        load(name, top)
     ready("branch", l=top)
 
     def widen_grad(j):
@@ -1096,6 +1083,9 @@
 
             loop(tokens // 32, activate)
         next_load("down", "slope", l=l)
+        if l == top:
+            for name in ("gated", "masks", "conv_in", "table", "wins", "table_t", "tap_t", "in", "hidden", "stream"):
+                load(name, top)
         visit(l, "activate")
         ready("up", "hidden_mid", "active", l=l)
         big_a[0:tokens, 0:width] = dot_nt(up_grad[...], wup[...])
@@ -1130,16 +1120,23 @@
 
             loop(GROUP // 2, block)
 
-        loop(n, grad_down)
-        groups["d" + str(l)].s0()
+        loop(n // 2, grad_down)
+        visit(l, "down0")
+        loop(n // 2, lambda q: grad_down(q + n // 2))
+        for letter in "de":
+            groups[letter + str(l)].s0()
         visit(l, "down")
-        loop(GROUP // 2, grad_up)
-        groups["u" + str(l)].s0()
+        loop(GROUP // 4, grad_up)
+        visit(l, "up0")
+        loop(GROUP // 4, lambda c: grad_up(c + GROUP // 4))
+        for letter in "uv":
+            groups[letter + str(l)].s0()
         next_load("hidden_mid", l=l)
         visit(l, "up")
         ready("middle", l=l)
         sums_mid = norm_back(big_a.at[:, 0:width], middle, grad, gains[l, 1:2, :], middle_grad, out_grad)
         next_load("middle", l=l)
+        visit(l, "middle")
 
         ready("out", l=l)
         big_b[0:tokens, 0:width] = dot_nt(out_grad[...], wout[...])
@@ -1157,9 +1154,10 @@
                     up * conv_out[s, r, :].astype(F32) * gslope[r, c].astype(F32)
                 ).astype(BF)
 
-        loop(tokens // 32, unmix)
+        for j in range(2):
+            loop(tokens // 64, lambda k: unmix(k + j * (tokens // 64)))
+            exchange_start(2 * l, send_c, recv_c, pl.ds(j * (tokens // 2), tokens // 2))
         next_load("gact", "gslope", "conv_out", l=l)
-        exchange_start(2 * l, send_c, recv_c, l)
         recv_c[me] = send_c[me]
         visit(l, "sent")
         ready("gated", l=l)
@@ -1175,6 +1173,7 @@
         next_load("conv_in", l=l)
         visit(l, "transform")
         exchange_wait(2 * l, send_c, recv_c, l)
+        visit(l, "arrived")
         spread_blocks(recv_c, masks, spread)
         big_b[:, 0 : 7 * channels] = dot(table[...], spread[...])
         visit(l, "came")
@@ -1185,15 +1184,15 @@
         if l == top:
             ready("table_t", "tap_t", l=l)
 
-        def untransform(j):
-            r = rows_of(j, 256)
+        for j in range(2):
+            r = slice(j * (quarter // 2), (j + 1) * (quarter // 2))
             parts = dot(table_t[r, 0:quarter], active[:, 0 : 7 * channels])
             parts += dot(table_t[r, quarter : 2 * quarter], active[:, half : half + 7 * channels])
             for s in range(n):
                 send_d[s, r, :] = join_blocks(parts, r, masks, s).astype(BF)
-
-        loop(quarter // 256, untransform)
-        exchange_start(2 * l + 1, send_d, recv_d, l)
+            exchange_start(2 * l + 1, send_d, recv_d, pl.ds(j * (quarter // 2), quarter // 2))
+            if j == 0:
+                visit(l, "half")
         recv_d[me] = send_d[me]
         next_load("active", l=l)
 
@@ -1208,6 +1207,7 @@
         visit(l, "returned")
         ready("in", "hidden", "stream", l=l)
         big_a[0:tokens, 0:width] = dot_nt(joined[:, width : 2 * width], win[1])
+        visit(l, "gatep")
         grad_in(1)
         visit(l, "in")
         exchange_wait(2 * l + 1, send_d, recv_d, l)
@@ -1221,6 +1221,7 @@
         if l == 0:
             grad_in(0)
             groups["i" + str(l)].s0()
+        visit(l, "in0")
         big_a[0:tokens, 0:width] = big_a[0:tokens, 0:width] + dot_nt(joined[:, 0:width], win[0])
         next_load("in", l=l)
         visit(l, "project")
@@ -1276,7 +1277,7 @@
 
     outs = [
         sds(tokens, width, dtype=BF), sds(tokens, width, dtype=BF), sds(layers, GROUP, PIECE_ROWS, width, dtype=BF),
-        sds(layers, taps, channels), sds(layers, 8, width), sds(tokens, width, dtype=BF), sds(tokens, width, dtype=BF),
+        sds(layers, taps, channels), sds(layers, 8, width),
     ]
     f32 = lambda *s: pltpu.VMEM(s, F32)
     bf = lambda *s: pltpu.VMEM(s, BF)
@@ -1293,16 +1294,16 @@
         bf(tokens, ff), bf(*wide), bf(*wide), bf(tokens, 2 * width),
         f32(2 * tokens, 7 * channels), f32(2 * tokens, ff // 2), bf(tokens, 7 * channels),
         bf(*blocks), bf(*blocks), bf(*blocks), bf(*blocks),
-        bf(*small), bf(layers, n - 1, taps, channels), bf(*small), bf(*small), bf(*small), bf(*small), f32(*small),
+        bf(*small), bf(*small), bf(*small), bf(layers, 3, taps, channels), bf(*small), bf(*small), f32(*small),
         bf(10, tokens, channels), bf(2 * tokens, tokens), bf(tokens, 2 * tokens), bf(4, taps, 2 * tokens),
         f32(layers, 8, width), f32(layers, GROUP - 1, 8, width), f32(layers, 8, width), f32(layers, n - 1, 8, width), f32(layers, 8, width),
         pltpu.SemaphoreType.DMA((layers, 21)),
         pltpu.SemaphoreType.DMA((2 * layers, 2)),
-        pltpu.SemaphoreType.DMA((4 * layers, 12)),
-        pltpu.SemaphoreType.DMA((layers, 9 + n)),
+        pltpu.SemaphoreType.DMA((6 * layers, 12)),
+        pltpu.SemaphoreType.DMA((layers, 10)),
         pltpu.SemaphoreType.DMA((layers, 4)),
         pltpu.SemaphoreType.DMA((3,)),
-        pltpu.SemaphoreType.DMA((2, 4)),
+        pltpu.SemaphoreType.DMA((2, 2)),
     ]
     return pl.pallas_call(
         functools.partial(backward_kernel, n, layers),
@@ -1376,7 +1377,7 @@
         n, stream_in, cotangent, segments, norm_gain, norm_bias, subs, factors, const(table), const(table.T), const(tap_table),
         w_in.transpose(0, 2, 1, 3), w_out, w_up, w_down,
     )
-    out, grad, res, sub, norms, *_ = backward(
+    out, grad, res, sub, norms = backward(
         n, norm_gain, subs, factors, masks, const(table), const(table.T), const(tap_table.transpose(0, 2, 1)),
         out, cot, (*kept, win, wout, wup, wdn),
     )

time: 244 us -> 224 us (0.918)
  Pallas kernels: 235 us -> 216 us
    pallas_call x1, Pallas kernels: 123 us -> 112 us  [backward(): pl.pallas_call(functools.partial(backward_kernel, n, layers), out_shape=o...]
    pallas_call x1, Pallas kernels: 106 us -> 98.8 us  [forward(): pl.pallas_call(functools.partial(forward_kernel, n, layers), out_shape=ou...]
where the time goes in v5:
time: 224 us
  Pallas kernels  216 us (96%)
  local copies, waits for them, and re-layouts  7.03 us (3%)
    pallas_call x1, Pallas kernels, backward(): pl.pallas_call(functools.partial(backward_kernel, n, layers), out_shape=o...  112 us
    pallas_call x1, Pallas kernels, forward(): pl.pallas_call(functools.partial(forward_kernel, n, layers), out_shape=ou...  98.8 us
    pallas_call x1, Pallas kernels, finish(): pl.pallas_call(finish_kernel, grid=(steps,), out_shape=[sds(tokens, width...  5.66 us
    unnamed x5, local copies, waits for them, and re-layouts  5.59 us

profile of v5, /device:TPU:0, one launch (start us, length us, event | category | flops | bytes accessed | tf_op | source)
XLA Modules:
  0.0 223.7 jit_solution(14040796600037862690)
XLA Ops:
  0.6 1.9 copy.29
  2.5 98.8 %forward.1 = (bf16[512,512]{1,0:T(8,128)(2,1)}, f32[2,512,512]{2,1,0:T(8,128)}, bf16[2,512,512]{2,1,0:T(8,128)(2,1)}, bf16[2,512,512]{2,1,0:T(8,128)(2,1)}, bf16...) custom-call(f32[512,512]{1,0:T(8,128)} %stream_in.1, ...), custom_call_target="tpu_custom_call" | custom-call | tf_op jit(solution)/shard_map/forward/pallas_call | solution.py:667
  101.4 111.5 %backward.1 = (bf16[512,512]{1,0:T(8,128)(2,1)}, bf16[512,512]{1,0:T(8,128)(2,1)}, bf16[2,8,176,512]{3,2,1,0:T(8,128)(2,1)}, f32[2,192,128]{2,1,0:T(8,128)}, f32[2,8,512]{2,1,0:T(8,128)}) custom-call(f32[2,2,512]{2,1,0:T(2,128)} %gains.3, f32[2,192,128]{2,1,0:T(8,128)} %bitcast.9, f32[2,192,128]{2,1,0:T(8,128)} %constant.10.clone.scales, ...), custom_call_target="tpu_custom_call" | custom-call | tf_op jit(solution)/shard_map/backward/pallas_call | solution.py:1308
  212.9 1.4 fusion
  214.3 0.0 copy-start
  214.3 5.7 %finish.1 = (f32[512,512]{1,0:T(8,128)}, f32[512,512]{1,0:T(8,128)}, f32[2,512,512]{2,1,0:T(8,128)}, f32[2,512,512]{2,1,0:T(8,128)}, f32[2,128,512]{2,1,0:T(8,128)}, /*index=5*/f32[2,2,512,128]{3,2,1,0:T(8,128)}) custom-call(bf16[512,512]{1,0:T(8,128)(2,1)} %get-tuple-element.58.out_i, bf16[512,512]{1,0:T(8,128)(2,1)} %get-tuple-element.59.grad_i, ...), custom_call_target="tpu_custom_call" | custom-call | tf_op jit(solution)/shard_map/finish/pallas_call | solution.py:1349
  220.0 3.0 %copy.27 = f32[2,512,2,128]{3,2,1,0:T(2,128)} copy(f32[2,512,2,128]{3,1,2,0:T(8,128)} %bitcast.7) | data formatting | bytes 2097152
  223.0 0.0 copy-done
  223.0 0.7 copy.31
Async XLA Ops:
  214.3 8.7 %copy-start = (f32[2,192,128]{2,1,0:T(8,128)S(1)}, f32[2,192,128]{2,1,0:T(8,128)}, u32[]{:S(2)}) copy-start(f32[2,192,128]{2,1,0:T(8,128)} %get-tuple-element.66) | copy-start | bytes 589828
